TPU v7x, 512 devices: a whole 4x8x8 slice. The times are simulated.
512 devices in a mesh: lat: 64 (over z, x, core), fld: 8 (over y).
Axes of the slice: x: 4, y: 8, z: 8, core: 2. Of those that a mesh axis runs over, the one named last changes fastest.
Arguments:
- grid: float32 [2, 640, 32, 2688], P(None, 'lat', 'fld'), may hold values from -6 to 6
- row_points: int32 [640], P('lat'), may hold values from 20 to 2576, as said below
- assignment: int32 [640], replicated, may hold values from 0 to 639, each once
- legendre: float32 [640, 640, 640], P('lat', 'fld'), may hold values from -0.25 to 0.25
- gauss_weights: float32 [640], P('fld'), may hold values from 0.25 to 2
- to_modes: float32 [32, 32], replicated, may hold values from -1 to 1
- from_modes: float32 [32, 32], replicated, may hold values from -1 to 1
- mode_depths: float32 [32], replicated, may hold values from 0.5 to 8
Outputs:
- grid_next: float32 [2, 640, 32, 2688], P(None, 'lat', 'fld')
Inputs may be any that keep to these rules, and one draw needn't show every extreme that they name: `row_points`: multiples of 4; row j, counted from the pole, has between 20 + 4 j - 12 and 20 + 4 j + 12 points, the row beside the equator exactly 2576; both hemispheres alike. `assignment`: every wavenumber from 0 to 639 stands in exactly one slot.
All inputs are finite; a program needn't handle non-finite values.
Results may differ from a plain program's by a relative error of at most 0.0003.
Values sent between devices are 32-bit elements; how exact they have to be, the bound alone decides.
No kernel may reach another device: no remote copies, remote signals or barrier semaphores. Data moves between devices by JAX's collectives and lax.ppermute only.
A program may use at most 128 MiB of HBM per device.

v0:
```python
import math

import jax
import jax.numpy as jnp
from jax import lax
from jax.sharding import PartitionSpec as P

PRECISE = lax.Precision.HIGHEST


def row_tables(point_count, wavenumbers, blocks):
    inner_index = jnp.arange(128, dtype=jnp.int32)
    outer_index = jnp.arange(blocks, dtype=jnp.int32) * 128
    phase_step = 2.0 * math.pi / point_count.astype(jnp.float32)
    inner_phase = (
        inner_index[None, :, None] * wavenumbers[None, None, :] % point_count[:, None, None]
    ).astype(jnp.float32) * phase_step[:, None, None]
    outer_phase = (
        outer_index[None, :, None] * wavenumbers[None, None, :] % point_count[:, None, None]
    ).astype(jnp.float32) * phase_step[:, None, None]
    return (jnp.cos(inner_phase), jnp.sin(inner_phase), jnp.cos(outer_phase), jnp.sin(outer_phase))


def body(grid, row_points, assignment, legendre, gauss_weights, to_modes, from_modes, mode_depths):
    hemispheres, row_pairs, fields, lon_points = grid.shape
    blocks = lon_points // 128
    slot_total = assignment.shape[0]
    slot_dev = legendre.shape[0]
    level_total = to_modes.shape[0]
    degree_dev = slot_total // lax.axis_size("fld")
    waves_own = lax.dynamic_slice_in_dim(assignment, lax.axis_index("lat") * slot_dev, slot_dev)
    cos_in, sin_in, cos_out, sin_out = row_tables(row_points, assignment, blocks)
    column = jnp.arange(lon_points, dtype=jnp.int32)
    inside = column[None, :] < row_points[:, None]
    resolved = 2 * assignment[None, :] < row_points[:, None]
    masked = jnp.where(inside[None, :, None, :], grid, 0.0).reshape(
        hemispheres, row_pairs, fields, blocks, 128
    )
    part_re = jnp.einsum("hrfab,rbm->hrfam", masked, cos_in, precision=PRECISE)
    part_im = -jnp.einsum("hrfab,rbm->hrfam", masked, sin_in, precision=PRECISE)
    real_part = jnp.sum(part_re * cos_out[None, :, None] + part_im * sin_out[None, :, None], axis=3)
    imag_part = jnp.sum(part_im * cos_out[None, :, None] - part_re * sin_out[None, :, None], axis=3)
    scaling = jnp.where(resolved, 1.0 / row_points.astype(jnp.float32)[:, None], 0.0)
    fourier = jnp.stack([real_part, imag_part], axis=3) * scaling[None, :, None, None, :]
    fourier = fourier.reshape(hemispheres, row_pairs, fields * 2, slot_total)
    owned_data = lax.all_to_all(
        lax.all_to_all(fourier, "lat", split_axis=3, concat_axis=1, tiled=True),
        "fld",
        split_axis=1,
        concat_axis=2,
        tiled=True,
    )
    weighted = owned_data * gauss_weights[None, :, None, None]
    legendre_slice = legendre
    degrees_now = jnp.arange(degree_dev * lax.axis_size("fld"), dtype=jnp.int32)
    parity_sign = jnp.where(degrees_now % 2 == 0, 1.0, -1.0)
    northern = jnp.einsum("sjk,jes->kse", legendre_slice, weighted[0], precision=PRECISE)
    southern = jnp.einsum("sjk,jes->kse", legendre_slice, weighted[1], precision=PRECISE)
    contrib = northern + parity_sign[:, None, None] * southern
    within = waves_own[None, :] + degrees_now[:, None] < slot_total
    spectrum_mine = lax.psum_scatter(
        contrib * within[:, :, None], "fld", scatter_dimension=0, tiled=True
    )
    row_count = spectrum_mine.shape[0]
    wave_degree = (
        waves_own[None, :]
        + lax.axis_index("fld") * degree_dev
        + jnp.arange(row_count, dtype=jnp.int32)[:, None]
    )
    factor = 1.0 + mode_depths[None, None, :] * (wave_degree * (wave_degree + 1)).astype(
        jnp.float32
    )[:, :, None] / (slot_total * (slot_total + 1))
    by_field = spectrum_mine.reshape(row_count, slot_dev, level_total, 2)
    in_modes = (
        jnp.einsum("gf,ksfr->ksgr", to_modes, by_field, precision=PRECISE) / factor[..., None]
    )
    updated = jnp.einsum("gf,ksfr->ksgr", from_modes, in_modes, precision=PRECISE)
    updated_mine = updated.reshape(row_count, slot_dev, level_total * 2)
    shard_piece = lax.all_gather(updated_mine, "fld", axis=0, tiled=True)
    row_count = shard_piece.shape[0]
    legendre_slice = legendre
    degrees_now = jnp.arange(row_count, dtype=jnp.int32)
    parity_sign = jnp.where(degrees_now % 2 == 0, 1.0, -1.0)
    north_add = jnp.einsum("sjk,kse->jes", legendre_slice, shard_piece, precision=PRECISE)
    south_add = jnp.einsum(
        "sjk,kse->jes", legendre_slice, shard_piece * parity_sign[:, None, None], precision=PRECISE
    )
    synthesis = jnp.stack([north_add, south_add])
    regrouped = lax.all_to_all(synthesis, "fld", split_axis=2, concat_axis=1, tiled=True)
    weighting = jnp.where(resolved, jnp.where(assignment[None, :] == 0, 1.0, 2.0), 0.0)
    coeffs = lax.all_to_all(regrouped, "lat", split_axis=1, concat_axis=3, tiled=True)
    item_count = coeffs.shape[0]
    by_part = coeffs.reshape(item_count, row_pairs, fields, 2, slot_total)
    real_in = by_part[:, :, :, 0] * weighting[None, :, None, :]
    imag_in = by_part[:, :, :, 1] * weighting[None, :, None, :]
    turned_re = (
        real_in[:, :, :, None, :] * cos_out[None, :, None]
        - imag_in[:, :, :, None, :] * sin_out[None, :, None]
    )
    turned_im = (
        real_in[:, :, :, None, :] * sin_out[None, :, None]
        + imag_in[:, :, :, None, :] * cos_out[None, :, None]
    )
    values = jnp.einsum("hrfam,rbm->hrfab", turned_re, cos_in, precision=PRECISE) - jnp.einsum(
        "hrfam,rbm->hrfab", turned_im, sin_in, precision=PRECISE
    )
    values = values.reshape(item_count, row_pairs, fields, lon_points)
    return jnp.where(inside[None, :, None, :], values, 0.0)


def solution(mesh):
    placed = (
        P(None, "lat", "fld", None),
        P("lat"),
        P(),
        P("lat", "fld", None),
        P("fld"),
        P(),
        P(),
        P(),
    )
    return jax.shard_map(
        body, mesh=mesh, in_specs=placed, out_specs=P(None, "lat", "fld", None), check_vma=False
    )
```

profile of v0, /device:TPU:1, one launch (start us, length us, event | category | flops | bytes accessed | tf_op | source)
XLA Modules:
  0.0 547.9 jit_solution(15727892996500297445)
XLA Ops:
  6.5 0.8 convert_divide_fusion
  7.4 0.7 broadcast_compare_fusion
  8.0 0.7 compare_select_fusion.3
  8.7 0.8 iota_compare_fusion
  9.5 1.4 iota_multiply_fusion
  10.9 0.7 broadcast_multiply_fusion.2
  11.6 0.7 compare_select_fusion.2
  12.3 1.4 broadcast_select_fusion
  13.7 1.3 reshape.250
  15.1 8.1 %fusion.68 = (f32[10,21,640]{2,1,0:T(8,128)S(1)}, f32[10,21,640]{2,1,0:T(8,128)S(1)}) fusion(f32[10]{0:T(128)S(1)} %get-tuple-element.16, s32[10]{0:T(128)S(1)} %compare_select_fusion.3, s32[21,640]{1,0:T(8,128)S(1)} %broadcast_multiply_fusion.1, pred[10]{0:T(512)(128)(4,1)S(1)} %broadcast_compare_fusion), kind=kLoop, calls=%fused_computation.73 | loop fusion | flops 1209600 | bytes 1129050 | tf_op jit(solution)/shard_map/cos | solution.py:21
  23.2 56.8 %fusion.22 = f32[10,640,2,4,21]{1,4,3,2,0:T(8,128)S(1)} fusion(f32[10]{0:T(128)S(1)} %get-tuple-element.16, s32[10]{0:T(128)S(1)} %compare_select_fusion.3, s32[128,640]{1,0:T(8,128)} %iota_multiply_fusion, f32[2,10,4,21,128]{4,3,2,1,0:T(8,128)} %reshape.250, pred[10]{0:T(512)(128)(4,1)S(1)} %broadcast_compare_fusion), kind=kOutput, calls=%fused_computation.27 | convolution fusion | flops 1658880000 | bytes 5488730 | tf_op jit(solution)/shard_map/hrfab,rbm->hrfam/dot_general | solution.py:40
  80.1 49.4 %fusion.1 = (f32[2,10,4,640]{3,2,0,1:T(4,128)S(1)}, f32[2,10,4,640]{3,2,0,1:T(4,128)S(1)}) fusion(f32[10,640,2,4,21]{1,4,3,2,0:T(8,128)S(1)} %fusion.22, f32[10,21,640]{2,1,0:T(8,128)S(1)} %get-tuple-element.12, f32[10,21,640]{2,1,0:T(8,128)S(1)} %get-tuple-element.11, f32[2,10,4,21,128]{4,3,2,1,0:T(8,128)S(1)} %copy-done.2, f32[10]{0:T(128)S(1)} %get-tuple-element.16, ...), kind=kOutput, calls=%fused_computation.7 | convolution fusion | flops 1668454400 | bytes 6973530 | tf_op jit(solution)/shard_map/hrfab,rbm->hrfam/dot_general | solution.py:39
  129.9 0.7 compare_select_fusion
  130.7 4.8 copy.82
  135.6 6.3 %reshape.262 = f32[64,1,1600]{2,1,0:T(1,128)S(1)} reshape(f32[640,2,8,10]{3,2,1,0:T(8,128)} %bitcast.117) | data formatting | bytes 819200
  141.8 30.4 %all_to_all.69 = f32[64,1,1600]{2,1,0:T(1,128)S(1)} all-to-all(f32[64,1,1600]{2,1,0:T(1,128)S(1)} %reshape.262), channel_id=1, replica_groups=mesh['lat'=64,'fld'=8] {'lat'}, dimensions={0} | all-to-all | bytes 819200 | tf_op jit(solution)/shard_map/all_to_all | solution.py:47
  172.2 0.5 broadcast.292
  172.7 1.6 reduce
  174.4 7.2 %reshape.263 = f32[640,2,8,10]{3,2,1,0:T(8,128)} reshape(f32[64,1600]{1,0:T(8,128)S(1)} %reduce) | data formatting | bytes 819200
  181.6 9.0 %copy.107 = f32[2,64,10,8,10]{4,3,0,2,1:T(8,128)} copy(f32[2,64,10,8,10]{2,3,0,4,1:T(8,128)} %bitcast.118) | data formatting | bytes 819200 | tf_op jit(solution)/shard_map/all_to_all | solution.py:47
  190.6 6.7 %reshape.264 = f32[8,1,12800]{2,1,0:T(1,128)} reshape(f32[640,2,8,10]{3,2,1,0:T(8,128)} %bitcast.119) | data formatting | bytes 819200
  197.3 6.8 %all-to-all-start.1 = ((f32[8,1,12800]{2,1,0:T(1,128)}), f32[8,1,12800]{2,1,0:T(1,128)S(1)}, u32[]{:S(2)}, u32[]{:S(2)}) async-start(f32[8,1,12800]{2,1,0:T(1,128)} %reshape.264), calls=%async_computation.1 | async-start | bytes 819200 | tf_op jit(solution)/shard_map/all_to_all | solution.py:46
  204.7 14.9 %all-to-all-done.1 = f32[8,1,12800]{2,1,0:T(1,128)S(1)} async-done(((f32[8,1,12800]{2,1,0:T(1,128)}), f32[8,1,12800]{2,1,0:T(1,128)S(1)}, u32[]{:S(2)}, u32[]{:S(2)}) %all-to-all-start.1) | async-done | bytes 409632 | tf_op jit(solution)/shard_map/all_to_all | solution.py:46
  219.6 1.6 reduce.1
  221.2 8.0 %reshape.265 = f32[640,2,8,10]{3,2,1,0:T(8,128)} reshape(f32[8,12800]{1,0:T(8,128)S(1)} %reduce.1) | data formatting | bytes 819200
  229.2 3.5 copy.87
  232.8 1.6 fusion.71
  234.4 2.9 bitcast_multiply_fusion.4
  237.2 2.8 copy.119
  240.4 29.7 %reduce-scatter.4.cloned.1.call-done = f32[80,640]{1,0:T(8,128)} async-done(((f32[640,640]{1,0:T(8,128)}), f32[80,640]{1,0:T(8,128)}) %reduce-scatter.4.cloned.1.call-update) | async-done | bytes 204816
  270.1 1.1 copy.120
  272.3 1.1 copy.90
  273.5 70.0 %all-gather.2.cloned.1.call-done = f32[640,10,64]{2,1,0:T(8,128)} async-done(((f32[80,10,64]{2,1,0:T(8,128)}), f32[640,10,64]{2,1,0:T(8,128)}) %all-gather.2.cloned.1.call-update) | async-done | bytes 1638416 | tf_op jit(solution)/shard_map/all_gather | solution.py:79
  343.4 5.1 copy.91
  348.5 3.8 convolution_bitcast_fusion.1
  352.3 2.3 fusion.58
  355.3 23.1 %all_to_all.70 = f32[2,80,64,10]{1,0,3,2:T(2,128)S(1)} all-to-all(f32[2,80,64,10]{1,0,3,2:T(2,128)S(1)} %copy.93), channel_id=1, replica_groups=mesh['lat'=64,'fld'=8] {'fld'}, dimensions={2} | all-to-all | bytes 819200 | tf_op jit(solution)/shard_map/all_to_all | solution.py:89
  378.4 4.5 copy.121
  383.0 6.1 %reshape.266 = f32[64,1,1600]{2,1,0:T(1,128)S(1)} reshape(f32[640,2,8,10]{3,2,1,0:T(8,128)} %bitcast.121) | data formatting | bytes 819200
  389.0 28.2 %all_to_all.71 = f32[64,1,1600]{2,1,0:T(1,128)S(1)} all-to-all(f32[64,1,1600]{2,1,0:T(1,128)S(1)} %reshape.266), channel_id=1, replica_groups=mesh['lat'=64,'fld'=8] {'lat'}, dimensions={0} | all-to-all | bytes 819200 | tf_op jit(solution)/shard_map/all_to_all | solution.py:91
  417.2 1.6 reduce.2
  418.9 7.2 %reshape.267 = f32[640,2,8,10]{3,2,1,0:T(8,128)} reshape(f32[64,1600]{1,0:T(8,128)S(1)} %reduce.2) | data formatting | bytes 819200
  426.1 7.9 %copy.97 = f32[2,10,8,64,10]{4,3,2,1,0:T(8,128)} copy(f32[2,10,8,64,10]{4,2,0,1,3:T(8,128)} %bitcast.122) | data formatting | bytes 819200 | tf_op jit(solution)/shard_map/all_to_all | solution.py:91
  434.0 5.1 reshape.253
  439.6 49.5 %fusion.4 = f32[10,128,2,4,21]{1,4,3,2,0:T(8,128)S(1)} fusion(f32[2,10,4,640]{3,2,0,1:T(4,128)S(1)} %get-tuple-element.17, f32[2,10,4,640]{3,2,0,1:T(4,128)S(1)} %get-tuple-element.18, f32[10,21,640]{2,1,0:T(8,128)} %copy-done.3, f32[10,21,640]{2,1,0:T(8,128)S(1)} %get-tuple-element.11, f32[10]{0:T(128)S(1)} %copy-done.15, s32[10]{0:T(128)S(1)} %copy-done.19, ...), kind=kOutput, calls=%fused_computation.12 | convolution fusion | flops 1662105600 | bytes 2672730 | tf_op jit(solution)/shard_map/hrfam,rbm->hrfab/dot_general | solution.py:104
  489.1 48.3 %fusion.53 = f32[2,10,4,21,128]{4,3,2,0,1:T(8,128)} fusion(f32[10,128,2,4,21]{1,4,3,2,0:T(8,128)S(1)} %fusion.4, f32[2,10,4,640]{3,2,0,1:T(4,128)S(1)} %get-tuple-element.17, f32[2,10,4,640]{3,2,0,1:T(4,128)S(1)} %get-tuple-element.18, f32[10,21,640]{2,1,0:T(8,128)S(1)} %copy-done.4, f32[10,21,640]{2,1,0:T(8,128)S(1)} %get-tuple-element.11, ...), kind=kOutput, calls=%fused_computation.58 | convolution fusion | flops 1662320640 | bytes 3532890 | tf_op jit(solution)/shard_map/hrfam,rbm->hrfab/dot_general | solution.py:104
  537.5 1.5 reshape.259
  539.0 1.9 copy_select_fusion
  (64 shorter events, 3.7 us)
Async XLA Ops:
  6.5 226.2 %copy-start = (f32[10,80,640]{2,1,0:T(8,128)S(1)}, f32[10,80,640]{2,1,0:T(8,128)}, u32[]{:S(2)}) copy-start(f32[10,80,640]{2,1,0:T(8,128)} %param.11) | copy-start | bytes 6144004
  6.5 8.5 %copy-start.9 = (s32[640]{0:T(1024)S(1)}, s32[640]{0:T(1024)}, u32[]{:S(2)}) copy-start(s32[640]{0:T(1024)} %param.10) | copy-start | bytes 7684
  7.4 72.7 %copy-start.14 = (f32[10]{0:T(128)}, f32[10]{0:T(128)S(1)}, u32[]{:S(2)}) copy-start(f32[10]{0:T(128)S(1)} %get-tuple-element.16) | copy-start | bytes 124
  8.0 72.0 %copy-start.16 = (pred[10]{0:T(512)(128)(4,1)}, pred[10]{0:T(512)(128)(4,1)S(1)}, u32[]{:S(2)}) copy-start(pred[10]{0:T(512)(128)(4,1)S(1)} %broadcast_compare_fusion) | copy-start | bytes 34
  8.7 71.4 %copy-start.18 = (s32[10]{0:T(128)}, s32[10]{0:T(128)S(1)}, u32[]{:S(2)}) copy-start(s32[10]{0:T(128)S(1)} %compare_select_fusion.3) | copy-start | bytes 124
  9.4 2.8 copy-start.5
  23.2 56.9 %copy-start.3 = (f32[10,21,640]{2,1,0:T(8,128)}, f32[10,21,640]{2,1,0:T(8,128)S(1)}, u32[]{:S(2)}) copy-start(f32[10,21,640]{2,1,0:T(8,128)S(1)} %get-tuple-element.12) | copy-start | bytes 1612804
  23.2 56.9 %copy-start.2 = (f32[2,10,4,21,128]{4,3,2,1,0:T(8,128)S(1)}, f32[2,10,4,21,128]{4,3,2,1,0:T(8,128)}, u32[]{:S(2)}) copy-start(f32[2,10,4,21,128]{4,3,2,1,0:T(8,128)} %reshape.250) | copy-start | bytes 2580484
  23.2 56.9 %copy-start.6 = (s32[128,640]{1,0:T(8,128)S(1)}, s32[128,640]{1,0:T(8,128)}, u32[]{:S(2)}) copy-start(s32[128,640]{1,0:T(8,128)} %iota_multiply_fusion) | copy-start | bytes 983044
  80.1 49.8 %copy-start.11 = (s32[10]{0:T(128)S(1)}, s32[10]{0:T(128)}, u32[]{:S(2)}) copy-start(s32[10]{0:T(128)} %param.9) | copy-start | bytes 124
  197.3 22.3 %all-to-all-start.1 = ((f32[8,1,12800]{2,1,0:T(1,128)}), f32[8,1,12800]{2,1,0:T(1,128)S(1)}, u32[]{:S(2)}, u32[]{:S(2)}) async-start(f32[8,1,12800]{2,1,0:T(1,128)} %reshape.264), calls=%async_computation.1 | async-start | bytes 819200 | tf_op jit(solution)/shard_map/all_to_all | solution.py:46
  204.1 66.0 %reduce-scatter.4.cloned.1.call-start = ((), (), s32[]{:S(2)}) async-start(), calls=%async_computation.6 | async-start | bytes 1843200
  229.2 3.5 copy-start.12
  237.2 3.1 copy-start.13
  237.2 33.9 %copy-start.20 = (f32[32,32]{1,0:T(8,128)S(1)}, f32[32,32]{1,0:T(8,128)}, u32[]{:S(2)}) copy-start(f32[32,32]{1,0:T(8,128)} %param.13) | copy-start | bytes 12292
  237.2 34.4 %copy-start.10 = (f32[32,32]{1,0:T(8,128)S(1)}, f32[32,32]{1,0:T(8,128)}, u32[]{:S(2)}) copy-start(f32[32,32]{1,0:T(8,128)} %param.14) | copy-start | bytes 12292
  240.0 103.4 %all-gather.2.cloned.1.call-start = ((), (), s32[]{:S(2)}) async-start(), calls=%async_computation.5 | async-start | bytes 5898240 | tf_op jit(solution)/shard_map/all_gather | solution.py:79
  348.5 3.8 copy-start.1
  433.9 5.1 copy-start.8
  434.0 5.6 %copy-start.7 = (s32[128,640]{1,0:T(8,128)S(1)}, s32[128,640]{1,0:T(8,128)}, u32[]{:S(2)}) copy-start(s32[128,640]{1,0:T(8,128)} %iota_multiply_fusion) | copy-start | bytes 983044
  434.0 5.6 %copy-start.15 = (f32[10]{0:T(128)S(1)}, f32[10]{0:T(128)}, u32[]{:S(2)}) copy-start(f32[10]{0:T(128)} %copy-done.14) | copy-start | bytes 124
  434.0 5.6 %copy-start.17 = (pred[10]{0:T(512)(128)(4,1)S(1)}, pred[10]{0:T(512)(128)(4,1)}, u32[]{:S(2)}) copy-start(pred[10]{0:T(512)(128)(4,1)} %copy-done.16) | copy-start | bytes 34
  434.0 5.6 %copy-start.19 = (s32[10]{0:T(128)S(1)}, s32[10]{0:T(128)}, u32[]{:S(2)}) copy-start(s32[10]{0:T(128)} %copy-done.18) | copy-start | bytes 124
  439.5 49.6 %copy-start.4 = (f32[10,21,640]{2,1,0:T(8,128)S(1)}, f32[10,21,640]{2,1,0:T(8,128)}, u32[]{:S(2)}) copy-start(f32[10,21,640]{2,1,0:T(8,128)} %copy-done.3) | copy-start | bytes 1612804
Sparse Core Ops, SparseCore 0:
  240.2 29.8 reduce-scatter.3
  273.6 69.8 all-gather.1
where the time goes:
time: 556 us; the launch traced here: 548 us
  matrix products  216 us (39%)
  waiting for transfers between devices  115 us (21%)
  local copies, waits for them, and re-layouts  90.9 us (16%)
  blocking collectives  81.7 us (15%)
  other arithmetic  23.7 us (4%)
  between operations  14 us (3%)
  starting transfers between devices  7.47 us (1%)
    all_gather x1, waiting for transfers between devices, body(): shard_piece = lax.all_gather(updated_mine, 'fld', axis=0, tiled=True)  70 us
    dot_general x1, matrix products, body(): part_im = -jnp.einsum('hrfab,rbm->hrfam', masked, sin_in, precision=PRECISE)  56.8 us
    dot_general x1, matrix products, body(): jnp.einsum('hrfam,rbm->hrfab', turned_im, sin_in, precision=PRECISE)  49.5 us
    dot_general x1, matrix products, body(): part_re = jnp.einsum('hrfab,rbm->hrfam', masked, cos_in, precision=PRECISE)  49.4 us
    dot_general x1, matrix products, body(): jnp.einsum('hrfam,rbm->hrfab', turned_re, cos_in, precision=PRECISE)  48.3 us
    unnamed x50, local copies, waits for them, and re-layouts  45.4 us
    all_to_all x1, blocking collectives, body(): lax.all_to_all(fourier, 'lat', split_axis=3, concat_axis=1, tiled=True)  30.4 us
    unnamed x3, waiting for transfers between devices  29.7 us
  transfers between devices with their start and end apart: 3, of which 3 were waited for; matrix products, arithmetic and copies ran while one was open for 0% of the time, Pallas kernels for 0%

commit v1 on v0

v1 whole, which is shorter than its diff:
```python
import math

import numpy as np
import jax
import jax.numpy as jnp
from jax import lax
from jax.experimental import pallas as pl
from jax.experimental.pallas import tpu as pltpu
from jax.sharding import PartitionSpec as P

F32 = jnp.float32
BF16 = jnp.bfloat16

HEMI = 2
ROWS = 10
FIELDS = 4
LEVELS = 32
LON = 2688
BLOCKS = LON // 128
WAVES = 640
LAT = 64
FLD = 8
PART = 2 * HEMI * FIELDS
MSG = ROWS * PART
LANES = 384
QUARTER = WAVES // 4
LEG = 896
VMEM = 48 << 20


def halves(x):
    top = x.astype(BF16)
    return top, (x - top.astype(F32)).astype(BF16)


def dot_split(a, b, dims):
    (ah, al), (bh, bl) = a, b
    d = (dims, ((), ()))
    out = lax.dot_general(ah, bl, d, preferred_element_type=F32)
    out = out + lax.dot_general(al, bh, d, preferred_element_type=F32)
    return out + lax.dot_general(ah, bh, d, preferred_element_type=F32)


AB = ((1,), (0,))
ABT = ((1,), (1,))


def turn(waves, points, index):
    product = waves * index
    quarter = points * 0.25
    count = jnp.floor(product * (4.0 / points) + 0.5)
    angle = (product - count * quarter) * (2.0 * math.pi / points)
    z = angle * angle
    s = angle * (
        1.0 + z * (-1 / 6 + z * (1 / 120 + z * (-1 / 5040 + z * (1 / 362880))))
    )
    c = 1.0 + z * (-0.5 + z * (1 / 24 + z * (-1 / 720 + z * (1 / 40320 - z / 3628800))))
    quad = count.astype(jnp.int32) & 3
    odd = (quad & 1) == 1
    cos_v = jnp.where(odd, s, c)
    sin_v = jnp.where(odd, c, s)
    cos_v = jnp.where((quad == 1) | (quad == 2), -cos_v, cos_v)
    sin_v = jnp.where(quad >= 2, -sin_v, sin_v)
    return cos_v, sin_v


def iota(shape, dim):
    return lax.broadcasted_iota(jnp.int32, shape, dim).astype(F32)


def tables(waves, points, cs_ref):
    c0, s0 = turn(waves, points, iota((16, WAVES), 0))
    c1, s1 = turn(waves, points, iota((8, WAVES), 0) * 16.0)
    for b in range(8):
        cb, sb = c1[b : b + 1], s1[b : b + 1]
        cs_ref[16 * b : 16 * b + 16, :WAVES] = c0 * cb - s0 * sb
        cs_ref[16 * b : 16 * b + 16, WAVES:] = s0 * cb + c0 * sb
    return turn(waves, points, iota((24, WAVES), 0) * 128.0)


def forward_kernel(points_ref, waves_ref, grid_ref, out_ref, cs_ref, fourier_ref):
    r = pl.program_id(0)
    count = points_ref[r]
    points = jnp.full((1, WAVES), count, jnp.int32).astype(F32)
    waves = waves_ref[...]
    co, so = tables(waves, points, cs_ref)
    wh, wl = halves(cs_ref[...])
    x = jnp.concatenate([grid_ref[0, 0], grid_ref[1, 0]], axis=0)
    column = lax.broadcasted_iota(jnp.int32, x.shape, 1)
    x = jnp.where(column < count, x, 0.0)
    x = jnp.concatenate([x[:, 128 * a : 128 * a + 128] for a in range(BLOCKS)], axis=0)
    xh, xl = halves(x)
    d = (AB, ((), ()))
    part = lax.dot_general(
        jnp.concatenate([xh, xl], axis=1),
        jnp.concatenate([wh, wh], axis=0),
        d,
        preferred_element_type=F32,
    ) + lax.dot_general(xh, wl, d, preferred_element_type=F32)
    re = jnp.zeros((8, WAVES), F32)
    im = jnp.zeros((8, WAVES), F32)
    for a in range(BLOCKS):
        pc = part[8 * a : 8 * a + 8, :WAVES]
        ps = part[8 * a : 8 * a + 8, WAVES:]
        ca, sa = co[a : a + 1], so[a : a + 1]
        re = re + (pc * ca - ps * sa)
        im = im - (ps * ca + pc * sa)
    scale = jnp.where(2.0 * waves < points, 1.0 / points, 0.0)
    row = pl.multiple_of(r * PART, PART)
    fourier_ref[pl.ds(row, 8), :] = re * scale
    fourier_ref[pl.ds(row + 8, 8), :] = im * scale

    @pl.when(r == ROWS - 1)
    def _():
        y = fourier_ref[...]
        shared = []
        for q in range(2):
            piece = y[:, 512 + 64 * q : 576 + 64 * q]
            shared += [jnp.concatenate([piece, piece], axis=1)] * 2
        full = jnp.concatenate(
            [
                y[:, :512],
                jnp.concatenate(shared, axis=1),
                jnp.zeros((LANES - 2 * MSG, 512), F32),
            ],
            axis=0,
        )
        out_ref[...] = full.T


def forward(row_points, waves, grid):
    return pl.pallas_call(
        forward_kernel,
        grid=(ROWS,),
        in_specs=[
            pl.BlockSpec(memory_space=pltpu.SMEM),
            pl.BlockSpec((1, WAVES), lambda r: (0, 0)),
            pl.BlockSpec((HEMI, 1, FIELDS, LON), lambda r: (0, r, 0, 0)),
        ],
        out_specs=pl.BlockSpec((LAT * FLD, LANES), lambda r: (0, 0)),
        out_shape=jax.ShapeDtypeStruct((LAT * FLD, LANES), F32),
        scratch_shapes=[
            pltpu.VMEM((128, 2 * WAVES), F32),
            pltpu.VMEM((MSG, WAVES), F32),
        ],
        compiler_params=pltpu.CompilerParams(vmem_limit_bytes=VMEM),
        cost_estimate=pl.CostEstimate(
            flops=3_000_000_000, bytes_accessed=2_000_000, transcendentals=0
        ),
        name="forward_fourier",
    )(row_points, waves, grid)


def inverse_kernel(points_ref, waves_ref, coeff_ref, out_ref, cs_ref, fourier_ref):
    r = pl.program_id(0)

    @pl.when(r == 0)
    def _():
        t = coeff_ref[...].T
        fourier_ref[:, :512] = t[:MSG]
        lane = lax.broadcasted_iota(jnp.int32, (MSG, 128), 1)
        sums = []
        for q in range(2):
            s = t[MSG : 2 * MSG, 256 * q : 256 * q + 128]
            s = s + t[MSG : 2 * MSG, 256 * q + 128 : 256 * q + 256]
            sums.append(s + pltpu.roll(s, 64, 1))
        fourier_ref[:, 512:] = jnp.where(lane < 64, sums[0], sums[1])

    count = points_ref[r]
    points = jnp.full((1, WAVES), count, jnp.int32).astype(F32)
    waves = waves_ref[...]
    co, so = tables(waves, points, cs_ref)
    wh, wl = halves(cs_ref[...])
    weight = jnp.where(2.0 * waves < points, jnp.where(waves == 0.0, 1.0, 2.0), 0.0)
    row = pl.multiple_of(r * PART, PART)
    re = fourier_ref[pl.ds(row, 8), :] * weight
    im = fourier_ref[pl.ds(row + 8, 8), :] * weight
    cosine, sine = [], []
    for a in range(BLOCKS):
        ca, sa = co[a : a + 1], so[a : a + 1]
        cosine.append(re * ca - im * sa)
        sine.append(-(re * sa + im * ca))
    turned = jnp.concatenate(
        [jnp.concatenate(cosine, axis=0), jnp.concatenate(sine, axis=0)], axis=1
    )
    th, tl = halves(turned)
    d = (ABT, ((), ()))
    both = lax.dot_general(
        th, jnp.concatenate([wh, wl], axis=0), d, preferred_element_type=F32
    )
    values = both[:, :128] + both[:, 128:]
    values = values + lax.dot_general(tl, wh, d, preferred_element_type=F32)
    wide = jnp.concatenate(
        [values[8 * a : 8 * a + 8] for a in range(BLOCKS)], axis=1
    )
    column = lax.broadcasted_iota(jnp.int32, wide.shape, 1)
    wide = jnp.where(column < count, wide, 0.0)
    out_ref[0, 0] = wide[:FIELDS]
    out_ref[1, 0] = wide[FIELDS:]


def inverse(row_points, waves, coeffs):
    return pl.pallas_call(
        inverse_kernel,
        grid=(ROWS,),
        in_specs=[
            pl.BlockSpec(memory_space=pltpu.SMEM),
            pl.BlockSpec((1, WAVES), lambda r: (0, 0)),
            pl.BlockSpec((LAT * FLD, LANES), lambda r: (0, 0)),
        ],
        out_specs=pl.BlockSpec((HEMI, 1, FIELDS, LON), lambda r: (0, r, 0, 0)),
        out_shape=jax.ShapeDtypeStruct((HEMI, ROWS, FIELDS, LON), F32),
        scratch_shapes=[
            pltpu.VMEM((128, 2 * WAVES), F32),
            pltpu.VMEM((MSG, WAVES), F32),
        ],
        compiler_params=pltpu.CompilerParams(vmem_limit_bytes=VMEM),
        name="inverse_fourier",
    )(row_points, waves, coeffs)


def pack_kernel(me_ref, legendre_ref, weight_ref, *refs):
    out_refs, tile_ref = refs[:FLD], refs[FLD]
    me = me_ref[0]
    lane = lax.broadcasted_iota(jnp.int32, (FLD * ROWS, LEG - WAVES), 1)
    weight = weight_ref[...]
    for t in range(FLD):
        g = lax.rem(me + t, FLD)
        shared = FLD + g // 4
        shift = lax.rem(WAVES - QUARTER * lax.rem(g, 4), WAVES)
        quarter = pltpu.roll(legendre_ref[shared], shift, 1)[:, : LEG - WAVES]
        extra = jnp.where(lane == QUARTER, weight, 0.0)
        quarter = jnp.where(lane < QUARTER, quarter, extra)
        own = legendre_ref[g]
        for i in range(LEG // 128):
            cut = slice(128 * i, 128 * i + 128)
            tile_ref[t, i] = own[:, cut] if i < 5 else quarter[:, 128 * i - WAVES :][:, :128]
        for i in range(LEG // 128):
            for r in range(ROWS):
                rows = pl.ds(r, FLD, stride=ROWS)
                out_refs[t][FLD * r : FLD * r + FLD, 128 * i : 128 * i + 128] = tile_ref[
                    t, i, rows, :
                ]


def pack(me, legendre, gauss_weights):
    vmem = pl.BlockSpec(memory_space=pltpu.VMEM)
    return pl.pallas_call(
        pack_kernel,
        in_specs=[pl.BlockSpec(memory_space=pltpu.SMEM), vmem, vmem],
        out_specs=[vmem] * FLD,
        out_shape=[jax.ShapeDtypeStruct((FLD * ROWS, LEG), F32)] * FLD,
        scratch_shapes=[pltpu.VMEM((FLD, LEG // 128, FLD * ROWS, 128), F32)],
        compiler_params=pltpu.CompilerParams(vmem_limit_bytes=VMEM),
        name="pack_legendre",
    )(me, legendre, gauss_weights.reshape(FLD * ROWS, 1))


def legendre_kernel(
    me_ref, assignment_ref, coeff_ref, to_ref, from_ref, depth_ref, *refs
):
    blocks, (out_ref, leg_ref, a_ref, x_ref, y_ref) = refs[:FLD], refs[FLD:]
    lat, fld = me_ref[1], me_ref[0]
    for t in range(FLD):
        source = lax.rem(fld + FLD - t, FLD)
        for r in range(ROWS):
            place = pl.multiple_of(r * LAT + FLD * source, FLD)
            leg_ref[pl.ds(place, FLD), :] = blocks[t][FLD * r : FLD * r + FLD, :]
    weight = leg_ref[:, LEG - 128 :].T[QUARTER - 128 : QUARTER - 127, :]
    lh, ll = halves(leg_ref[...])

    t = coeff_ref[...].T
    for kind, dest in ((0, a_ref), (1, x_ref)):
        for u in range(ROWS // 2):
            row = kind * MSG + 2 * u * PART
            even, odd = t[row : row + PART], t[row + PART : row + 2 * PART]
            for g in range(FLD):
                cut = slice(LAT * g, LAT * g + LAT)
                dest[PART * g : PART * g + PART, 128 * u : 128 * u + 128] = (
                    jnp.concatenate([even[:, cut], odd[:, cut]], axis=1)
                )
    own = halves(a_ref[...] * weight)
    shared = halves(x_ref[...] * weight)
    spectrum = jnp.concatenate(
        [
            dot_split(own, (lh[:, :WAVES], ll[:, :WAVES]), AB),
            dot_split(shared, (lh[:, WAVES:], ll[:, WAVES:]), AB),
        ],
        axis=1,
    )

    modes = dot_split(halves(to_ref[...]), halves(spectrum), AB)
    lane = lax.broadcasted_iota(jnp.int32, (1, LEG), 1)
    is_own = lane < WAVES
    degree = jnp.where(is_own, lane, lane - WAVES + QUARTER * lax.rem(fld, 4))
    wave_own = assignment_ref[lat * ROWS + fld]
    wave_shared = assignment_ref[lat * ROWS + FLD + fld // 4]
    total = degree + jnp.where(is_own, wave_own, wave_shared)
    within = (total < WAVES) & (lane < WAVES + QUARTER)
    total = jnp.where(within, total, 0)
    sign = jnp.where((degree & 1) == 0, 1.0, -1.0)
    ratio = (total * (total + 1)).astype(F32) * (1.0 / (WAVES * (WAVES + 1)))
    half = 2 * LEVELS
    modes = modes[:half] + sign * modes[half:]
    modes = jnp.where(within, modes, 0.0) / (1.0 + depth_ref[...] * ratio)
    updated = dot_split(halves(from_ref[...]), halves(modes), AB)
    row_id = lax.broadcasted_iota(jnp.int32, updated.shape, 0)
    updated = jnp.where((row_id & FIELDS) == 0, updated, updated * sign)

    for kind, cols in ((0, slice(0, WAVES)), (1, slice(WAVES, LEG))):
        back = dot_split(halves(updated[:, cols]), (lh[:, cols], ll[:, cols]), ABT)
        for u in range(ROWS // 2):
            row = kind * MSG + 2 * u * PART
            for g in range(0, FLD, 2):
                one = back[PART * g : PART * g + PART, 128 * u : 128 * u + 128]
                two = back[PART * g + PART : PART * g + 2 * PART, 128 * u : 128 * u + 128]
                for odd in range(2):
                    cut = slice(64 * odd, 64 * odd + 64)
                    y_ref[
                        row + PART * odd : row + PART * odd + PART, LAT * g : LAT * g + 128
                    ] = jnp.concatenate([one[:, cut], two[:, cut]], axis=1)
    y_ref[2 * MSG :, :] = jnp.zeros((LANES - 2 * MSG, LAT * FLD), F32)
    out_ref[...] = y_ref[...].T


def legendre_round(me, assignment, coeffs, to_big, from_big, depth_big, blocks):
    smem = pl.BlockSpec(memory_space=pltpu.SMEM)
    vmem = pl.BlockSpec(memory_space=pltpu.VMEM)
    return pl.pallas_call(
        legendre_kernel,
        in_specs=[smem, smem] + [vmem] * (4 + FLD),
        out_specs=vmem,
        out_shape=jax.ShapeDtypeStruct((LAT * FLD, LANES), F32),
        scratch_shapes=[
            pltpu.VMEM((WAVES, LEG), F32),
            pltpu.VMEM((PART * FLD, WAVES), F32),
            pltpu.VMEM((PART * FLD, WAVES), F32),
            pltpu.VMEM((LANES, LAT * FLD), F32),
        ],
        compiler_params=pltpu.CompilerParams(vmem_limit_bytes=VMEM),
        name="legendre_round",
    )(me, assignment, coeffs, to_big, from_big, depth_big, *blocks)


def mode_matrices(to_modes, from_modes, mode_depths):
    part = np.arange(PART * FLD)
    field = part // PART * FIELDS + part % FIELDS
    imag = part % PART // (HEMI * FIELDS)
    hemi = part % (HEMI * FIELDS) // FIELDS
    mode = np.arange(2 * LEVELS)
    same = (mode // LEVELS)[:, None] == imag[None, :]
    level = mode % LEVELS
    wide = to_modes[level][:, field]
    to_big = jnp.concatenate(
        [jnp.where(same & (hemi == h)[None, :], wide, 0.0) for h in range(HEMI)], axis=0
    )
    from_big = jnp.where(same.T, from_modes[field][:, level], 0.0)
    return to_big, from_big, mode_depths[level][:, None]


def body(grid, row_points, assignment, legendre, gauss_weights, to_modes, from_modes, mode_depths):
    waves = assignment.reshape(LAT, ROWS).T.reshape(1, WAVES).astype(F32)
    me = jnp.stack([lax.axis_index("fld"), lax.axis_index("lat")]).astype(jnp.int32)
    packed = pack(me, legendre, gauss_weights)
    blocks = [packed[0]] + [
        lax.ppermute(packed[t], "fld", [(i, (i + t) % FLD) for i in range(FLD)])
        for t in range(1, FLD)
    ]
    fourier = forward(row_points, waves, grid)
    coeffs = lax.all_to_all(fourier, ("fld", "lat"), 0, 0, tiled=True)
    big = mode_matrices(to_modes, from_modes, mode_depths)
    synthesis = legendre_round(me, assignment, coeffs, *big, blocks)
    back = lax.all_to_all(synthesis, ("fld", "lat"), 0, 0, tiled=True)
    return inverse(row_points, waves, back)


def solution(mesh):
    placed = (
        P(None, "lat", "fld", None),
        P("lat"),
        P(),
        P("lat", "fld", None),
        P("fld"),
        P(),
        P(),
        P(),
    )
    return jax.shard_map(
        body, mesh=mesh, in_specs=placed, out_specs=P(None, "lat", "fld", None), check_vma=False
    )
```

time: 556 us -> 165 us (0.30); the launches traced: 548 us -> 164 us
  matrix products: 216 us -> 0 us
  waiting for transfers between devices: 115 us -> 32.6 us
  local copies, waits for them, and re-layouts: 90.9 us -> 9.67 us
  starting transfers between devices: 7.47 us -> 52.6 us
  blocking collectives: 81.7 us -> 45 us
  Pallas kernels: 0 us -> 23.2 us
  other arithmetic: 23.7 us -> 0.82 us
  between operations: 14 us -> 0.28 us
    dot_general x10 -> x0, matrix products: 216 us -> none  [the longest x1 56.8 us: body(): part_im = -jnp.einsum('hrfab,rbm->hrfam', masked, sin_in, precision=PRECISE)]
    all_gather x1 -> x0, waiting for transfers between devices: 70 us -> none  [body(): shard_piece = lax.all_gather(updated_mine, 'fld', axis=0, tiled=True)]
    unnamed x50 -> x30, local copies, waits for them, and re-layouts: 45.4 us -> 3.13 us
    all_to_all x3 -> x1, blocking collectives: 81.7 us -> 45 us  [body(): back = lax.all_to_all(synthesis, ('fld', 'lat'), 0, 0, tiled=True)]
    ppermute x0 -> x7, waiting for transfers between devices: none -> 32.6 us  [body(): lax.ppermute(packed[t], 'fld', [(i, (i + t) % FLD) for i in range(FLD)])]
    unnamed x3 -> x0, waiting for transfers between devices: 29.7 us -> none
    ppermute x0 -> x7, starting transfers between devices: none -> 28.6 us  [body(): lax.ppermute(packed[t], 'fld', [(i, (i + t) % FLD) for i in range(FLD)])]
    pallas_call x0 -> x4, Pallas kernels: none -> 23.2 us  [the longest x1 9.57 us: inverse(): pl.pallas_call(inverse_kernel, grid=(ROWS,), in_specs=[pl.BlockSpec(memor...]
  transfers between devices with their start and end apart: 3 -> 8, of which waited for: 3 -> 5; matrix products, arithmetic and copies ran while one was open for 0% -> 3% of each run, Pallas kernels for 0% -> 1%
where the time goes in v1:
time: 165 us; the launch traced here: 164 us
  starting transfers between devices  52.6 us (32%)
  blocking collectives  45 us (27%)
  waiting for transfers between devices  32.6 us (20%)
  Pallas kernels  23.2 us (14%)
  local copies, waits for them, and re-layouts  9.67 us (6%)
    all_to_all x1, blocking collectives, body(): back = lax.all_to_all(synthesis, ('fld', 'lat'), 0, 0, tiled=True)  45 us
    ppermute x7, waiting for transfers between devices, body(): lax.ppermute(packed[t], 'fld', [(i, (i + t) % FLD) for i in range(FLD)])  32.6 us
    ppermute x7, starting transfers between devices, body(): lax.ppermute(packed[t], 'fld', [(i, (i + t) % FLD) for i in range(FLD)])  28.6 us
    all_to_all x1, starting transfers between devices, body(): coeffs = lax.all_to_all(fourier, ('fld', 'lat'), 0, 0, tiled=True)  24 us
    pallas_call x1, Pallas kernels, inverse(): pl.pallas_call(inverse_kernel, grid=(ROWS,), in_specs=[pl.BlockSpec(memor...  9.57 us
    pallas_call x1, Pallas kernels, forward(): pl.pallas_call(forward_kernel, grid=(ROWS,), in_specs=[pl.BlockSpec(memor...  7.37 us
    pallas_call x1, Pallas kernels, legendre_round(): pl.pallas_call(legendre_kernel, in_specs=[smem, smem] + [vmem] * (4 + FLD...  4.12 us
  transfers between devices with their start and end apart: 8, of which 5 were waited for; matrix products, arithmetic and copies ran while one was open for 3% of the time, Pallas kernels for 1%

profile of v1, /device:TPU:1, one launch (start us, length us, event | category | flops | bytes accessed | tf_op | source)
XLA Modules:
  0.0 164.2 jit_solution(16635710027009550030)
XLA Ops:
  0.0 0.7 convert_element_type.9
  0.7 0.1 convert_element_type.10
  0.8 0.1 copy.34
  0.9 0.1 convert_element_type.12.waves_ref
  1.0 0.7 copy-done.3
  1.7 1.2 copy-done.5
  2.8 7.4 %forward_fourier.1 = f32[512,384]{1,0:T(8,128)S(1)} custom-call(s32[10]{0:T(128)S(1)} %copy-done.3, f32[1,640]{1,0:T(1,128)S(1)} %convert_element_type.12.waves_ref, f32[2,10,4,2688]{3,2,1,0:T(4,128)S(1)} %copy-done.5), custom_call_target="tpu_custom_call" | custom-call | flops 3000000000 | bytes 2000000 | tf_op jit(solution)/shard_map/forward_fourier/pallas_call | solution.py:132
  10.2 0.0 copy-start.13
  10.2 0.0 copy-start.1
  10.2 1.7 %copy.35 = f32[512,1,384]{2,1,0:T(1,128)} copy(f32[512,1,384]{2,0,1:T(8,128)S(1)} %bitcast.22) | data formatting | bytes 1572864 | tf_op jit(solution)/shard_map/all_to_all | solution.py:370
  11.9 24.0 %all-to-all-start = ((f32[512,1,384]{2,1,0:T(1,128)}), f32[512,1,384]{2,1,0:T(1,128)}, u32[]{:S(2)}, u32[]{:S(2)}) async-start(f32[512,1,384]{2,1,0:T(1,128)} %copy.35), calls=%async_computation | async-start | bytes 1572864 | tf_op jit(solution)/shard_map/all_to_all | solution.py:370
  35.9 0.1 copy.41.weight_ref
  36.0 0.1 pad_add_fusion.me_ref
  36.1 2.2 %pack_legendre.1 = (f32[80,896]{1,0:T(8,128)S(1)}, f32[80,896]{1,0:T(8,128)}, f32[80,896]{1,0:T(8,128)}, f32[80,896]{1,0:T(8,128)}, f32[80,896]{1,0:T(8,128)}, /...) custom-call(s32[2]{0:T(128)S(1)} %pad_add_fusion.me_ref, f32[10,80,640]{2,1,0:T(8,128)S(1)} %copy-done.1, ...), custom_call_target="tpu_custom_call" | custom-call | tf_op jit(solution)/shard_map/pack_legendre/pallas_call | solution.py:248
  38.3 3.3 %collective-permute-start = (f32[80,896]{1,0:T(8,128)}, f32[80,896]{1,0:T(8,128)S(1)}, u32[]{:S(2)}, u32[]{:S(2)}) collective-permute-start(f32[80,896]{1,0:T(8,128)} %get-tuple-element.14), channel_id=1, source_target_pairs={{0,1},{1,2},{2,3},{3,4},{4,5},{5,6},{6,7},{7,0},{8,9},{9,10},{10,1... | collective-permute-start | bytes 860168 | tf_op jit(solution)/shard_map/ppermute | solution.py:366
  41.6 4.0 %collective-permute-start.1 = (f32[80,896]{1,0:T(8,128)}, f32[80,896]{1,0:T(8,128)S(1)}, u32[]{:S(2)}, u32[]{:S(2)}) collective-permute-start(f32[80,896]{1,0:T(8,128)} %get-tuple-element.15), channel_id=1, source_target_pairs={{0,2},{1,3},{2,4},{3,5},{4,6},{5,7},{6,0},{7,1},{8,10},{9,11},{10,... | collective-permute-start | bytes 860168 | tf_op jit(solution)/shard_map/ppermute | solution.py:366
  45.6 4.5 %collective-permute-start.2 = (f32[80,896]{1,0:T(8,128)}, f32[80,896]{1,0:T(8,128)S(1)}, u32[]{:S(2)}, u32[]{:S(2)}) collective-permute-start(f32[80,896]{1,0:T(8,128)} %get-tuple-element.16), channel_id=1, source_target_pairs={{0,3},{1,4},{2,5},{3,6},{4,7},{5,0},{6,1},{7,2},{8,11},{9,12},{10,... | collective-permute-start | bytes 860168 | tf_op jit(solution)/shard_map/ppermute | solution.py:366
  50.1 3.7 %collective-permute-start.3 = (f32[80,896]{1,0:T(8,128)}, f32[80,896]{1,0:T(8,128)S(1)}, u32[]{:S(2)}, u32[]{:S(2)}) collective-permute-start(f32[80,896]{1,0:T(8,128)} %get-tuple-element.17), channel_id=1, source_target_pairs={{0,4},{1,5},{2,6},{3,7},{4,0},{5,1},{6,2},{7,3},{8,12},{9,13},{10,... | collective-permute-start | bytes 860168 | tf_op jit(solution)/shard_map/ppermute | solution.py:366
  53.9 4.6 %collective-permute-start.4 = (f32[80,896]{1,0:T(8,128)S(1)}, f32[80,896]{1,0:T(8,128)S(1)}, u32[]{:S(2)}, u32[]{:S(2)}) collective-permute-start(f32[80,896]{1,0:T(8,128)S(1)} %get-tuple-element.18), channel_id=1, source_target_pairs={{0,5},{1,6},{2,7},{3,0},{4,1},{5,2},{6,3},{7,4},{8,13},{9,14},{10,... | collective-permute-start | bytes 860168 | tf_op jit(solution)/shard_map/ppermute | solution.py:366
  58.5 0.8 gather_fusion.4
  59.3 0.1 copy.42.depth_ref
  59.4 0.0 copy-start.2
  59.4 0.6 gather_fusion
  60.0 0.1 copy.36
  60.1 0.6 gather_fusion.1
  60.8 0.1 copy.37
  60.8 0.0 copy-done
  60.9 0.6 gather_fusion.2
  61.5 0.1 copy.39
  61.6 0.6 gather_fusion.3
  62.2 0.1 copy.40
  62.3 0.0 collective-permute-done.refs_1_
  62.3 5.1 %collective-permute-start.5 = (f32[80,896]{1,0:T(8,128)S(1)}, f32[80,896]{1,0:T(8,128)S(1)}, u32[]{:S(2)}, u32[]{:S(2)}) collective-permute-start(f32[80,896]{1,0:T(8,128)S(1)} %get-tuple-element.19), channel_id=1, source_target_pairs={{0,6},{1,7},{2,0},{3,1},{4,2},{5,3},{6,4},{7,5},{8,14},{9,15},{10,... | collective-permute-start | bytes 860168 | tf_op jit(solution)/shard_map/ppermute | solution.py:366
  67.4 1.5 collective-permute-done.1.refs_2_
  68.9 3.4 %collective-permute-start.6 = (f32[80,896]{1,0:T(8,128)S(1)}, f32[80,896]{1,0:T(8,128)S(1)}, u32[]{:S(2)}, u32[]{:S(2)}) collective-permute-start(f32[80,896]{1,0:T(8,128)S(1)} %get-tuple-element.20), channel_id=1, source_target_pairs={{0,7},{1,0},{2,1},{3,2},{4,3},{5,4},{6,5},{7,6},{8,15},{9,8},{10,9... | collective-permute-start | bytes 860168 | tf_op jit(solution)/shard_map/ppermute | solution.py:366
  72.4 0.0 all-to-all-done
  72.4 1.2 copy.49
  73.6 16.2 %collective-permute-done.2.refs_3_ = f32[80,896]{1,0:T(8,128)S(1)} collective-permute-done((f32[80,896]{1,0:T(8,128)}, f32[80,896]{1,0:T(8,128)S(1)}, u32[]{:S(2)}, u32[]{:S(2)}) %collective-permute-start.2) | collective-permute-done | bytes 286752 | tf_op jit(solution)/shard_map/ppermute | solution.py:366
  89.8 9.6 %collective-permute-done.3.refs_4_ = f32[80,896]{1,0:T(8,128)S(1)} collective-permute-done((f32[80,896]{1,0:T(8,128)}, f32[80,896]{1,0:T(8,128)S(1)}, u32[]{:S(2)}, u32[]{:S(2)}) %collective-permute-start.3) | collective-permute-done | bytes 286752 | tf_op jit(solution)/shard_map/ppermute | solution.py:366
  99.4 0.0 collective-permute-done.4.refs_5_
  99.4 1.8 %collective-permute-done.5.refs_6_ = f32[80,896]{1,0:T(8,128)S(1)} collective-permute-done((f32[80,896]{1,0:T(8,128)S(1)}, f32[80,896]{1,0:T(8,128)S(1)}, u32[]{:S(2)}, u32[]{:S(2)}) %collective-permute-start.5) | collective-permute-done | bytes 286752 | tf_op jit(solution)/shard_map/ppermute | solution.py:366
  101.2 3.5 %collective-permute-done.6.refs_7_ = f32[80,896]{1,0:T(8,128)S(1)} collective-permute-done((f32[80,896]{1,0:T(8,128)S(1)}, f32[80,896]{1,0:T(8,128)S(1)}, u32[]{:S(2)}, u32[]{:S(2)}) %collective-permute-start.6) | collective-permute-done | bytes 286752 | tf_op jit(solution)/shard_map/ppermute | solution.py:366
  104.6 4.1 %legendre_round.1 = f32[512,384]{1,0:T(8,128)S(1)} custom-call(s32[2]{0:T(128)S(1)} %pad_add_fusion.me_ref, s32[640]{0:T(1024)S(1)} %copy-done.2, f32[512,384]{1,0:T(8,128)S(1)} %bitcast.19, f32[128,128]{1,0:T(8,128)S(1)} %pad_maximum_fusion.to_ref, f32[128,64]{1,0:T(8,128)S(1)} %select_bitcast_fusion.from_ref, f32[64,1]{1,0:T(8,128)S(1)} %copy.42.depth_ref, ...), custom_call_target="tpu_custom_call" | custom-call | tf_op jit(solution)/shard_map/legendre_round/pallas_call | solution.py:329
  108.8 0.0 copy-start.4
  108.8 0.8 copy.43
  109.6 45.0 %all_to_all.22 = f32[512,1,384]{2,1,0:T(1,128)S(1)} all-to-all(f32[512,1,384]{2,1,0:T(1,128)S(1)} %copy.43), channel_id=1, replica_groups=mesh['lat'=64,'fld'=8] {'fld','lat'}, dimensions={0} | all-to-all | bytes 1572864 | tf_op jit(solution)/shard_map/all_to_all | solution.py:373
  154.6 0.1 copy.48
  154.6 9.6 %inverse_fourier.1 = f32[2,10,4,2688]{3,2,1,0:T(4,128)} custom-call(s32[10]{0:T(128)S(1)} %copy-done.4, f32[1,640]{1,0:T(1,128)S(1)} %convert_element_type.12.waves_ref, f32[512,384]{1,0:T(8,128)S(1)} %bitcast.21), custom_call_target="tpu_custom_call" | custom-call | tf_op jit(solution)/shard_map/inverse_fourier/pallas_call | solution.py:203
  (26 shorter events, 0.1 us)
Async XLA Ops:
  0.0 60.8 %copy-start = (f32[32,32]{1,0:T(8,128)S(1)}, f32[32,32]{1,0:T(8,128)}, u32[]{:S(2)}) copy-start(f32[32,32]{1,0:T(8,128)} %param.24) | copy-start | bytes 12292
  1.0 0.7 copy-start.3
  1.7 1.2 copy-start.5
  10.2 25.7 %copy-start.13 = (f32[80]{0:T(128)S(1)}, f32[80]{0:T(128)}, u32[]{:S(2)}) copy-start(f32[80]{0:T(128)} %param.22) | copy-start | bytes 964
  10.2 25.9 %copy-start.1 = (f32[10,80,640]{2,1,0:T(8,128)S(1)}, f32[10,80,640]{2,1,0:T(8,128)}, u32[]{:S(2)}) copy-start(f32[10,80,640]{2,1,0:T(8,128)} %legendre_ref.1) | copy-start | bytes 6144004
  11.9 46.6 %copy-start.12 = (s32[64]{0:T(128)S(1)}, s32[64]{0:T(128)}, u32[]{:S(2)}) copy-start(s32[64]{0:T(128)} %constant.39) | copy-start | bytes 772
  11.9 46.6 %copy-start.6 = (f32[32]{0:T(128)S(1)}, f32[32]{0:T(128)}, u32[]{:S(2)}) copy-start(f32[32]{0:T(128)} %param.25) | copy-start | bytes 388
  11.9 47.5 %copy-start.7 = (f32[32,32]{1,0:T(8,128)S(1)}, f32[32,32]{1,0:T(8,128)}, u32[]{:S(2)}) copy-start(f32[32,32]{1,0:T(8,128)} %param.23) | copy-start | bytes 12292
  11.9 48.2 %copy-start.11 = (s32[128]{0:T(128)S(1)}, s32[128]{0:T(128)}, u32[]{:S(2)}) copy-start(s32[128]{0:T(128)} %constant.40) | copy-start | bytes 1540
  11.9 60.4 %all-to-all-start = ((f32[512,1,384]{2,1,0:T(1,128)}), f32[512,1,384]{2,1,0:T(1,128)}, u32[]{:S(2)}, u32[]{:S(2)}) async-start(f32[512,1,384]{2,1,0:T(1,128)} %copy.35), calls=%async_computation | async-start | bytes 1572864 | tf_op jit(solution)/shard_map/all_to_all | solution.py:370
  36.1 26.2 %copy-start.9 = (pred[128,64]{0,1:T(32,128)(4,1)S(1)}, pred[128,64]{0,1:T(32,128)(4,1)}, u32[]{:S(2)}) copy-start(pred[128,64]{0,1:T(32,128)(4,1)} %constant.45) | copy-start | bytes 24580
  36.1 26.2 %copy-start.10 = (pred[128,64]{0,1:T(32,128)(4,1)S(1)}, pred[128,64]{0,1:T(32,128)(4,1)}, u32[]{:S(2)}) copy-start(pred[128,64]{0,1:T(32,128)(4,1)} %constant.44) | copy-start | bytes 24580
  36.1 36.2 %copy-start.8 = (pred[64,128]{0,1:T(32,128)(4,1)S(1)}, pred[64,128]{0,1:T(32,128)(4,1)}, u32[]{:S(2)}) copy-start(pred[64,128]{0,1:T(32,128)(4,1)} %constant.46) | copy-start | bytes 24580
  38.3 24.0 %collective-permute-start = (f32[80,896]{1,0:T(8,128)}, f32[80,896]{1,0:T(8,128)S(1)}, u32[]{:S(2)}, u32[]{:S(2)}) collective-permute-start(f32[80,896]{1,0:T(8,128)} %get-tuple-element.14), channel_id=1, source_target_pairs={{0,1},{1,2},{2,3},{3,4},{4,5},{5,6},{6,7},{7,0},{8,9},{9,10},{10,1... | collective-permute-start | bytes 860168 | tf_op jit(solution)/shard_map/ppermute | solution.py:366
  41.6 27.3 %collective-permute-start.1 = (f32[80,896]{1,0:T(8,128)}, f32[80,896]{1,0:T(8,128)S(1)}, u32[]{:S(2)}, u32[]{:S(2)}) collective-permute-start(f32[80,896]{1,0:T(8,128)} %get-tuple-element.15), channel_id=1, source_target_pairs={{0,2},{1,3},{2,4},{3,5},{4,6},{5,7},{6,0},{7,1},{8,10},{9,11},{10,... | collective-permute-start | bytes 860168 | tf_op jit(solution)/shard_map/ppermute | solution.py:366
  45.6 44.2 %collective-permute-start.2 = (f32[80,896]{1,0:T(8,128)}, f32[80,896]{1,0:T(8,128)S(1)}, u32[]{:S(2)}, u32[]{:S(2)}) collective-permute-start(f32[80,896]{1,0:T(8,128)} %get-tuple-element.16), channel_id=1, source_target_pairs={{0,3},{1,4},{2,5},{3,6},{4,7},{5,0},{6,1},{7,2},{8,11},{9,12},{10,... | collective-permute-start | bytes 860168 | tf_op jit(solution)/shard_map/ppermute | solution.py:366
  50.1 49.2 %collective-permute-start.3 = (f32[80,896]{1,0:T(8,128)}, f32[80,896]{1,0:T(8,128)S(1)}, u32[]{:S(2)}, u32[]{:S(2)}) collective-permute-start(f32[80,896]{1,0:T(8,128)} %get-tuple-element.17), channel_id=1, source_target_pairs={{0,4},{1,5},{2,6},{3,7},{4,0},{5,1},{6,2},{7,3},{8,12},{9,13},{10,... | collective-permute-start | bytes 860168 | tf_op jit(solution)/shard_map/ppermute | solution.py:366
  53.9 45.5 %collective-permute-start.4 = (f32[80,896]{1,0:T(8,128)S(1)}, f32[80,896]{1,0:T(8,128)S(1)}, u32[]{:S(2)}, u32[]{:S(2)}) collective-permute-start(f32[80,896]{1,0:T(8,128)S(1)} %get-tuple-element.18), channel_id=1, source_target_pairs={{0,5},{1,6},{2,7},{3,0},{4,1},{5,2},{6,3},{7,4},{8,13},{9,14},{10,... | collective-permute-start | bytes 860168 | tf_op jit(solution)/shard_map/ppermute | solution.py:366
  59.4 45.2 %copy-start.2 = (s32[640]{0:T(1024)S(1)}, s32[640]{0:T(1024)}, u32[]{:S(2)}) copy-start(s32[640]{0:T(1024)} %assignment_ref.1) | copy-start | bytes 7684
  62.3 38.8 %collective-permute-start.5 = (f32[80,896]{1,0:T(8,128)S(1)}, f32[80,896]{1,0:T(8,128)S(1)}, u32[]{:S(2)}, u32[]{:S(2)}) collective-permute-start(f32[80,896]{1,0:T(8,128)S(1)} %get-tuple-element.19), channel_id=1, source_target_pairs={{0,6},{1,7},{2,0},{3,1},{4,2},{5,3},{6,4},{7,5},{8,14},{9,15},{10,... | collective-permute-start | bytes 860168 | tf_op jit(solution)/shard_map/ppermute | solution.py:366
  68.9 35.7 %collective-permute-start.6 = (f32[80,896]{1,0:T(8,128)S(1)}, f32[80,896]{1,0:T(8,128)S(1)}, u32[]{:S(2)}, u32[]{:S(2)}) collective-permute-start(f32[80,896]{1,0:T(8,128)S(1)} %get-tuple-element.20), channel_id=1, source_target_pairs={{0,7},{1,0},{2,1},{3,2},{4,3},{5,4},{6,5},{7,6},{8,15},{9,8},{10,9... | collective-permute-start | bytes 860168 | tf_op jit(solution)/shard_map/ppermute | solution.py:366
  108.8 45.9 %copy-start.4 = (s32[10]{0:T(128)S(1)}, s32[10]{0:T(128)}, u32[]{:S(2)}) copy-start(s32[10]{0:T(128)} %points_ref.3) | copy-start | bytes 124

commit v2 on v1

--- a/solution.py
+++ b/solution.py
@@ -1,6 +1,5 @@
 import math
 
-import numpy as np
 import jax
 import jax.numpy as jnp
 from jax import lax
@@ -25,7 +24,16 @@
 LANES = 384
 QUARTER = WAVES // 4
 LEG = 896
-VMEM = 48 << 20
+BLOCK = FLD * ROWS
+SLABS = 6
+REST = SLABS * BLOCK
+LMSG = REST + 24
+TAIL = QUARTER - 128
+WLANE = 64
+FIRST = 256
+VMEM = 20 << 20
+UNPACK_VMEM = 58 << 20
+UNPACK_COST = 10_000_000_000
 
 
 def halves(x):
@@ -220,53 +228,173 @@
 
 
 def pack_kernel(me_ref, legendre_ref, weight_ref, *refs):
-    out_refs, tile_ref = refs[:FLD], refs[FLD]
+    near_refs = {0: refs[0], 1: refs[1], 7: refs[2]}
+    up_ref, down_ref, tile_ref = refs[3:]
     me = me_ref[0]
-    lane = lax.broadcasted_iota(jnp.int32, (FLD * ROWS, LEG - WAVES), 1)
-    weight = weight_ref[...]
+    lane = lax.broadcasted_iota(jnp.int32, (BLOCK, 128), 1)
+    weight = jnp.concatenate(
+        [weight_ref[...], jnp.zeros((FLD, 128 - ROWS), F32)], axis=1
+    )
+    weight = pltpu.roll(weight, WLANE, 1)
     for t in range(FLD):
+
+        def store(row, value, t=t):
+            if t in (0, 1, 7):
+                ref, at = near_refs[t], row
+            elif t < 4:
+                ref, at = up_ref, (t - 2) * LMSG + row
+            elif t > 4:
+                ref, at = down_ref, (6 - t) * LMSG + row
+            elif row < FIRST:
+                ref, at = up_ref, 2 * LMSG + row
+            else:
+                ref, at = down_ref, 2 * LMSG + row - FIRST
+            ref[pl.ds(at, FLD), :] = value
+
         g = lax.rem(me + t, FLD)
         shared = FLD + g // 4
         shift = lax.rem(WAVES - QUARTER * lax.rem(g, 4), WAVES)
-        quarter = pltpu.roll(legendre_ref[shared], shift, 1)[:, : LEG - WAVES]
-        extra = jnp.where(lane == QUARTER, weight, 0.0)
-        quarter = jnp.where(lane < QUARTER, quarter, extra)
+        quarter = pltpu.roll(legendre_ref[shared], shift, 1)
         own = legendre_ref[g]
-        for i in range(LEG // 128):
-            cut = slice(128 * i, 128 * i + 128)
-            tile_ref[t, i] = own[:, cut] if i < 5 else quarter[:, 128 * i - WAVES :][:, :128]
-        for i in range(LEG // 128):
+        for i in range(5):
+            tile_ref[t, i] = own[:, 128 * i : 128 * i + 128]
+        tile_ref[t, 5] = quarter[:, :128]
+        tile_ref[t, 6] = jnp.where(lane < TAIL, quarter[:, 128:256], 0.0)
+        for i in range(SLABS):
             for r in range(ROWS):
                 rows = pl.ds(r, FLD, stride=ROWS)
-                out_refs[t][FLD * r : FLD * r + FLD, 128 * i : 128 * i + 128] = tile_ref[
-                    t, i, rows, :
-                ]
+                store(BLOCK * i + FLD * r, tile_ref[t, i, rows, :])
+        for i in range(3):
+            rest = weight if i == 2 else jnp.zeros((FLD, 128), F32)
+            for r in range(4 * i, min(4 * i + 4, ROWS)):
+                part = tile_ref[t, 6, pl.ds(r, FLD, stride=ROWS), :]
+                rest = rest + (pltpu.roll(part, TAIL * (r % 4), 1) if r % 4 else part)
+            store(REST + FLD * i, rest)
 
 
 def pack(me, legendre, gauss_weights):
     vmem = pl.BlockSpec(memory_space=pltpu.VMEM)
+    rows = (LMSG, LMSG, LMSG, 2 * LMSG + FIRST, 3 * LMSG - FIRST)
     return pl.pallas_call(
         pack_kernel,
         in_specs=[pl.BlockSpec(memory_space=pltpu.SMEM), vmem, vmem],
-        out_specs=[vmem] * FLD,
-        out_shape=[jax.ShapeDtypeStruct((FLD * ROWS, LEG), F32)] * FLD,
-        scratch_shapes=[pltpu.VMEM((FLD, LEG // 128, FLD * ROWS, 128), F32)],
+        out_specs=[vmem] * 5,
+        out_shape=[jax.ShapeDtypeStruct((n, 128), F32) for n in rows],
+        scratch_shapes=[pltpu.VMEM((FLD, LEG // 128, BLOCK, 128), F32)],
         compiler_params=pltpu.CompilerParams(vmem_limit_bytes=VMEM),
         name="pack_legendre",
-    )(me, legendre, gauss_weights.reshape(FLD * ROWS, 1))
-
-
-def legendre_kernel(
-    me_ref, assignment_ref, coeff_ref, to_ref, from_ref, depth_ref, *refs
-):
-    blocks, (out_ref, leg_ref, a_ref, x_ref, y_ref) = refs[:FLD], refs[FLD:]
-    lat, fld = me_ref[1], me_ref[0]
+    )(me, legendre, gauss_weights.reshape(FLD, ROWS))
+
+
+def shift(x, step):
+    return lax.ppermute(x, "fld", [(i, (i + step) % FLD) for i in range(FLD)])
+
+
+def ring(up1, down1, up2, down2):
+    up2, down2 = shift(up2, 2), shift(down2, -2)
+    up1, down1 = shift(up1, 1), shift(down1, -1)
+    up3, down3 = shift(up2[LMSG : 2 * LMSG], 1), shift(down2[LMSG : 2 * LMSG], -1)
+    up4, down4 = shift(up2[2 * LMSG :], 2), shift(down2[2 * LMSG :], -2)
+    return up1, up2, up3, up4, down1, down2, down3, down4
+
+
+def mode_matrices(to_modes, from_modes):
+    def ids(shape, dim):
+        return lax.broadcasted_iota(jnp.int32, shape, dim)
+
+    def product(a, b):
+        return lax.dot_general(
+            a, b, (AB, ((), ())), precision=lax.Precision.HIGHEST, preferred_element_type=F32
+        )
+
+    def field(part):
+        return part // PART * FIELDS + part % FIELDS
+
+    parts, modes = PART * FLD, 2 * LEVELS
+    spread = (ids((LEVELS, parts), 0) == field(ids((LEVELS, parts), 1))).astype(F32)
+    double = (ids((parts, LEVELS), 0) % LEVELS == ids((parts, LEVELS), 1)).astype(F32)
+    wide = product(double, product(to_modes, spread))
+    row, part = ids((parts, parts), 0), ids((parts, parts), 1) % PART
+    to_big = jnp.where(
+        (row // LEVELS % 2 == part // 8) & (row // modes == part % 8 // FIELDS), wide, 0.0
+    )
+    spread = (field(ids((parts, LEVELS), 0)) == ids((parts, LEVELS), 1)).astype(F32)
+    double = (ids((LEVELS, modes), 0) == ids((LEVELS, modes), 1) % LEVELS).astype(F32)
+    wide = product(product(spread, from_modes), double)
+    part, column = ids((parts, modes), 0) % PART, ids((parts, modes), 1)
+    return to_big, jnp.where(part // 8 == column // LEVELS, wide, 0.0)
+
+
+def unpack_kernel(me_ref, own_msg, *refs):
+    ups, downs, (leg_ref, weight_ref) = refs[:4], refs[4:8], refs[8:]
+    fld = me_ref[0]
+    lane = lax.broadcasted_iota(jnp.int32, (FLD, 128), 1)
     for t in range(FLD):
+
+        def load(row, t=t):
+            if t == 0:
+                return own_msg[row : row + FLD]
+            if t < 4:
+                return ups[t - 1][row : row + FLD]
+            if t > 4:
+                return downs[7 - t][row : row + FLD]
+            if row < FIRST:
+                return ups[3][row : row + FLD]
+            return downs[3][row - FIRST : row - FIRST + FLD]
+
         source = lax.rem(fld + FLD - t, FLD)
         for r in range(ROWS):
-            place = pl.multiple_of(r * LAT + FLD * source, FLD)
-            leg_ref[pl.ds(place, FLD), :] = blocks[t][FLD * r : FLD * r + FLD, :]
-    weight = leg_ref[:, LEG - 128 :].T[QUARTER - 128 : QUARTER - 127, :]
+            place = pl.ds(pl.multiple_of(r * LAT + FLD * source, FLD), FLD)
+            for i in range(SLABS):
+                leg_ref[place, 128 * i : 128 * i + 128] = load(BLOCK * i + FLD * r)
+            rest = load(REST + FLD * (r // 4))
+            if r % 4:
+                rest = pltpu.roll(rest, 128 - TAIL * (r % 4), 1)
+            leg_ref[place, 768:] = jnp.where(lane < TAIL, rest, 0.0)
+        weight_ref[pl.ds(pl.multiple_of(FLD * source, FLD), FLD), :] = load(REST + 2 * FLD)
+
+
+def unpack(me, own, moved):
+    vmem = pl.BlockSpec(memory_space=pltpu.VMEM)
+    taken = [
+        pl.BlockSpec((min(LMSG, x.shape[0]), 128), lambda i: (0, 0)) for x in moved
+    ]
+    return pl.pallas_call(
+        unpack_kernel,
+        grid=(1,),
+        in_specs=[pl.BlockSpec(memory_space=pltpu.SMEM), vmem] + taken,
+        out_specs=[vmem, vmem],
+        out_shape=[
+            jax.ShapeDtypeStruct((WAVES, LEG), F32),
+            jax.ShapeDtypeStruct((LAT, 128), F32),
+        ],
+        compiler_params=pltpu.CompilerParams(vmem_limit_bytes=UNPACK_VMEM),
+        cost_estimate=pl.CostEstimate(
+            flops=UNPACK_COST, bytes_accessed=5_000_000, transcendentals=0
+        ),
+        name="unpack_legendre",
+    )(me, own, *moved)
+
+
+def legendre_kernel(
+    me_ref,
+    assignment_ref,
+    coeff_ref,
+    to_ref,
+    from_ref,
+    depth_ref,
+    leg_ref,
+    weight_ref,
+    out_ref,
+    a_ref,
+    x_ref,
+    y_ref,
+):
+    lat, fld = me_ref[1], me_ref[0]
+    weight = weight_ref[...].T
+    weight = jnp.concatenate(
+        [weight[WLANE + r : WLANE + r + 1] for r in range(ROWS)], axis=1
+    )
     lh, ll = halves(leg_ref[...])
 
     t = coeff_ref[...].T
@@ -289,7 +417,8 @@
         axis=1,
     )
 
-    modes = dot_split(halves(to_ref[...]), halves(spectrum), AB)
+    to_big, from_big = mode_matrices(to_ref[...], from_ref[...])
+    modes = dot_split(halves(to_big), halves(spectrum), AB)
     lane = lax.broadcasted_iota(jnp.int32, (1, LEG), 1)
     is_own = lane < WAVES
     degree = jnp.where(is_own, lane, lane - WAVES + QUARTER * lax.rem(fld, 4))
@@ -301,9 +430,10 @@
     sign = jnp.where((degree & 1) == 0, 1.0, -1.0)
     ratio = (total * (total + 1)).astype(F32) * (1.0 / (WAVES * (WAVES + 1)))
     half = 2 * LEVELS
+    depth = jnp.concatenate([depth_ref[...], depth_ref[...]], axis=0)
     modes = modes[:half] + sign * modes[half:]
-    modes = jnp.where(within, modes, 0.0) / (1.0 + depth_ref[...] * ratio)
-    updated = dot_split(halves(from_ref[...]), halves(modes), AB)
+    modes = jnp.where(within, modes, 0.0) / (1.0 + depth * ratio)
+    updated = dot_split(halves(from_big), halves(modes), AB)
     row_id = lax.broadcasted_iota(jnp.int32, updated.shape, 0)
     updated = jnp.where((row_id & FIELDS) == 0, updated, updated * sign)
 
@@ -323,53 +453,36 @@
     out_ref[...] = y_ref[...].T
 
 
-def legendre_round(me, assignment, coeffs, to_big, from_big, depth_big, blocks):
+def legendre_round(*args):
     smem = pl.BlockSpec(memory_space=pltpu.SMEM)
     vmem = pl.BlockSpec(memory_space=pltpu.VMEM)
     return pl.pallas_call(
         legendre_kernel,
-        in_specs=[smem, smem] + [vmem] * (4 + FLD),
+        in_specs=[smem, smem] + [vmem] * 6,
         out_specs=vmem,
         out_shape=jax.ShapeDtypeStruct((LAT * FLD, LANES), F32),
         scratch_shapes=[
-            pltpu.VMEM((WAVES, LEG), F32),
             pltpu.VMEM((PART * FLD, WAVES), F32),
             pltpu.VMEM((PART * FLD, WAVES), F32),
             pltpu.VMEM((LANES, LAT * FLD), F32),
         ],
         compiler_params=pltpu.CompilerParams(vmem_limit_bytes=VMEM),
         name="legendre_round",
-    )(me, assignment, coeffs, to_big, from_big, depth_big, *blocks)
-
-
-def mode_matrices(to_modes, from_modes, mode_depths):
-    part = np.arange(PART * FLD)
-    field = part // PART * FIELDS + part % FIELDS
-    imag = part % PART // (HEMI * FIELDS)
-    hemi = part % (HEMI * FIELDS) // FIELDS
-    mode = np.arange(2 * LEVELS)
-    same = (mode // LEVELS)[:, None] == imag[None, :]
-    level = mode % LEVELS
-    wide = to_modes[level][:, field]
-    to_big = jnp.concatenate(
-        [jnp.where(same & (hemi == h)[None, :], wide, 0.0) for h in range(HEMI)], axis=0
-    )
-    from_big = jnp.where(same.T, from_modes[field][:, level], 0.0)
-    return to_big, from_big, mode_depths[level][:, None]
+    )(*args)
 
 
 def body(grid, row_points, assignment, legendre, gauss_weights, to_modes, from_modes, mode_depths):
     waves = assignment.reshape(LAT, ROWS).T.reshape(1, WAVES).astype(F32)
     me = jnp.stack([lax.axis_index("fld"), lax.axis_index("lat")]).astype(jnp.int32)
-    packed = pack(me, legendre, gauss_weights)
-    blocks = [packed[0]] + [
-        lax.ppermute(packed[t], "fld", [(i, (i + t) % FLD) for i in range(FLD)])
-        for t in range(1, FLD)
-    ]
+    own, *messages = pack(me, legendre, gauss_weights)
+    waves, own = lax.optimization_barrier((waves, own))
+    rows, weight = unpack(me, own, ring(*messages))
     fourier = forward(row_points, waves, grid)
     coeffs = lax.all_to_all(fourier, ("fld", "lat"), 0, 0, tiled=True)
-    big = mode_matrices(to_modes, from_modes, mode_depths)
-    synthesis = legendre_round(me, assignment, coeffs, *big, blocks)
+    depths = mode_depths.reshape(LEVELS, 1)
+    synthesis = legendre_round(
+        me, assignment, coeffs, to_modes, from_modes, depths, rows, weight
+    )
     back = lax.all_to_all(synthesis, ("fld", "lat"), 0, 0, tiled=True)
     return inverse(row_points, waves, back)
 

time: 165 us -> 147 us (0.89)
  waiting for transfers between devices: 32.6 us -> 10.9 us
  local copies, waits for them, and re-layouts: 9.67 us -> 13.5 us
  starting transfers between devices: 52.6 us -> 49.6 us
  Pallas kernels: 23.2 us -> 25.8 us
    ppermute x7 -> x8, waiting for transfers between devices: 32.6 us -> 10.9 us  [shift(): return lax.ppermute(x, 'fld', [(i, (i + step) % FLD) for i in range(FLD)])]
    unnamed x30 -> x38, local copies, waits for them, and re-layouts: 3.13 us -> 7.97 us
    gather x9 -> x0, local copies, waits for them, and re-layouts: 3.56 us -> none  [the longest x4 1.41 us: mode_matrices(): from_big = jnp.where(same.T, from_modes[field][:, level], 0.0)]
    pallas_call x1 -> x2, Pallas kernels: 4.12 us -> 7.24 us  [the longest x1 3.94 us: legendre_round(): pl.pallas_call(legendre_kernel, in_specs=[smem, smem] + [vmem] * 6, out_s...]
    all_to_all x1, starting transfers between devices: 24 us -> 21.5 us  [body(): coeffs = lax.all_to_all(fourier, ('fld', 'lat'), 0, 0, tiled=True)]
    slice x0 -> x4, local copies, waits for them, and re-layouts: none -> 1.91 us  [the longest x2 0.99 us: ring(): up3, down3 = (shift(up2[LMSG:2 * LMSG], 1), shift(down2[LMSG:2 * LMSG], -1))]
    ppermute x7 -> x8, starting transfers between devices: 28.6 us -> 28.1 us  [shift(): return lax.ppermute(x, 'fld', [(i, (i + step) % FLD) for i in range(FLD)])]
  transfers between devices with their start and end apart: 8 -> 9, of which waited for: 5 -> 3; matrix products, arithmetic and copies ran while one was open for 3% -> 3% of each run, Pallas kernels for 1% -> 7%
where the time goes in v2:
time: 147 us; the launch traced here: 146 us
  starting transfers between devices  49.6 us (34%)
  blocking collectives  45.5 us (31%)
  Pallas kernels  25.8 us (18%)
  local copies, waits for them, and re-layouts  13.5 us (9%)
  waiting for transfers between devices  10.9 us (7%)
    all_to_all x1, blocking collectives, body(): back = lax.all_to_all(synthesis, ('fld', 'lat'), 0, 0, tiled=True)  45.5 us
    ppermute x8, starting transfers between devices, shift(): return lax.ppermute(x, 'fld', [(i, (i + step) % FLD) for i in range(FLD)])  28.1 us
    all_to_all x1, starting transfers between devices, body(): coeffs = lax.all_to_all(fourier, ('fld', 'lat'), 0, 0, tiled=True)  21.5 us
    ppermute x8, waiting for transfers between devices, shift(): return lax.ppermute(x, 'fld', [(i, (i + step) % FLD) for i in range(FLD)])  10.9 us
    pallas_call x1, Pallas kernels, inverse(): pl.pallas_call(inverse_kernel, grid=(ROWS,), in_specs=[pl.BlockSpec(memor...  9.57 us
    unnamed x38, local copies, waits for them, and re-layouts  7.97 us
    pallas_call x1, Pallas kernels, forward(): pl.pallas_call(forward_kernel, grid=(ROWS,), in_specs=[pl.BlockSpec(memor...  7.37 us
    pallas_call x1, Pallas kernels, legendre_round(): pl.pallas_call(legendre_kernel, in_specs=[smem, smem] + [vmem] * 6, out_s...  3.94 us
  transfers between devices with their start and end apart: 9, of which 3 were waited for; matrix products, arithmetic and copies ran while one was open for 3% of the time, Pallas kernels for 7%

profile of v2, /device:TPU:1, one launch (start us, length us, event | category | flops | bytes accessed | tf_op | source)
XLA Modules:
  0.0 146.4 jit_solution(1890133773712504062)
XLA Ops:
  0.0 0.7 reshape.26.weight_ref
  0.7 0.1 pad_add_fusion.me_ref
  0.8 1.6 %copy-done.1 = f32[10,80,640]{2,1,0:T(8,128)S(1)} copy-done((f32[10,80,640]{2,1,0:T(8,128)S(1)}, f32[10,80,640]{2,1,0:T(8,128)}, u32[]{:S(2)}) %copy-start.1) | copy-done | bytes 2048024
  2.4 1.7 %pack_legendre.1 = (f32[504,128]{1,0:T(8,128)S(1)}, f32[504,128]{1,0:T(8,128)S(1)}, f32[504,128]{1,0:T(8,128)S(1)}, f32[1264,128]{1,0:T(8,128)S(1)}, f32[1256,128]{1,0:T(8,128)S(1)}) custom-call(s32[2]{0:T(128)S(1)} %pad_add_fusion.me_ref, f32[10,80,640]{2,1,0:T(8,128)S(1)} %copy-done.1, f32[8,10]{1,0:T(8,128)S(1)} %reshape.26.weight_ref), custom_call_target="tpu_custom_call" | custom-call | tf_op jit(solution)/shard_map/pack_legendre/pallas_call | solution.py:278
  4.1 0.7 copy-done.11
  4.7 5.0 %collective-permute-start.1 = (f32[1264,128]{1,0:T(8,128)S(1)}, f32[1264,128]{1,0:T(8,128)S(1)}, u32[]{:S(2)}, u32[]{:S(2)}) collective-permute-start(f32[1264,128]{1,0:T(8,128)S(1)} %get-tuple-element.18), channel_id=1, source_target_pairs={{0,2},{1,3},{2,4},{3,5},{4,6},{5,7},{6,0},{7,1},{8,10},{9,11},{10,... | collective-permute-start | bytes 1941512 | tf_op jit(solution)/shard_map/ppermute | solution.py:290
  9.8 3.6 %collective-permute-start.5 = (f32[1256,128]{1,0:T(8,128)S(1)}, f32[1256,128]{1,0:T(8,128)}, u32[]{:S(2)}, u32[]{:S(2)}) collective-permute-start(f32[1256,128]{1,0:T(8,128)S(1)} %get-tuple-element.20), channel_id=1, source_target_pairs={{0,6},{1,7},{2,0},{3,1},{4,2},{5,3},{6,4},{7,5},{8,14},{9,15},{10,... | collective-permute-start | bytes 1929224 | tf_op jit(solution)/shard_map/ppermute | solution.py:290
  13.4 0.7 convert_element_type.20
  14.1 0.1 convert_element_type.21
  14.2 0.1 copy.12
  14.3 0.1 convert_element_type.23.waves_ref
  14.3 0.7 copy-done.8
  15.0 1.2 copy-done.10
  16.2 7.4 %forward_fourier.1 = f32[512,384]{1,0:T(8,128)S(1)} custom-call(s32[10]{0:T(128)S(1)} %copy-done.8, f32[1,640]{1,0:T(1,128)S(1)} %convert_element_type.23.waves_ref, f32[2,10,4,2688]{3,2,1,0:T(4,128)S(1)} %copy-done.10), custom_call_target="tpu_custom_call" | custom-call | flops 3000000000 | bytes 2000000 | tf_op jit(solution)/shard_map/forward_fourier/pallas_call | solution.py:140
  23.6 0.0 copy-start.13
  23.6 1.7 %copy.13 = f32[512,1,384]{2,1,0:T(1,128)} copy(f32[512,1,384]{2,0,1:T(8,128)S(1)} %bitcast.15) | data formatting | bytes 1572864 | tf_op jit(solution)/shard_map/all_to_all | solution.py:481
  25.3 21.5 %all-to-all-start = ((f32[512,1,384]{2,1,0:T(1,128)}), f32[512,1,384]{2,1,0:T(1,128)S(1)}, u32[]{:S(2)}, u32[]{:S(2)}) async-start(f32[512,1,384]{2,1,0:T(1,128)} %copy.13), calls=%async_computation | async-start | bytes 1572864 | tf_op jit(solution)/shard_map/all_to_all | solution.py:481
  46.8 3.3 %collective-permute-start = (f32[504,128]{1,0:T(8,128)S(1)}, f32[504,128]{1,0:T(8,128)S(1)}, u32[]{:S(2)}, u32[]{:S(2)}) collective-permute-start(f32[504,128]{1,0:T(8,128)S(1)} %get-tuple-element.17), channel_id=1, source_target_pairs={{0,1},{1,2},{2,3},{3,4},{4,5},{5,6},{6,7},{7,0},{8,9},{9,10},{10,1... | collective-permute-start | bytes 774152 | tf_op jit(solution)/shard_map/ppermute | solution.py:290
  50.1 3.5 %collective-permute-start.4 = (f32[504,128]{1,0:T(8,128)S(1)}, f32[504,128]{1,0:T(8,128)}, u32[]{:S(2)}, u32[]{:S(2)}) collective-permute-start(f32[504,128]{1,0:T(8,128)S(1)} %get-tuple-element.19), channel_id=1, source_target_pairs={{0,7},{1,0},{2,1},{3,2},{4,3},{5,4},{6,5},{7,6},{8,15},{9,8},{10,9... | collective-permute-start | bytes 774152 | tf_op jit(solution)/shard_map/ppermute | solution.py:290
  53.5 0.0 collective-permute-done.5.refs_5_
  53.5 1.0 slice.18
  54.5 3.4 %collective-permute-start.6 = (f32[504,128]{1,0:T(8,128)S(1)}, f32[504,128]{1,0:T(8,128)}, u32[]{:S(2)}, u32[]{:S(2)}) collective-permute-start(f32[504,128]{1,0:T(8,128)S(1)} %slice.18), channel_id=1, source_target_pairs={{0,7},{1,0},{2,1},{3,2},{4,3},{5,4},{6,5},{7,6},{8,15},{9,8},{10,9... | collective-permute-start | bytes 774152 | tf_op jit(solution)/shard_map/ppermute | solution.py:290
  57.9 0.0 collective-permute-done.1.refs_1_
  57.9 1.9 %collective-permute-start.2 = (f32[504,128]{1,0:T(8,128)S(1)}, f32[504,128]{1,0:T(8,128)S(1)}, u32[]{:S(2)}, u32[]{:S(2)}) collective-permute-start(f32[504,128]{1,0:T(8,128)S(1)} %slice.16), channel_id=1, source_target_pairs={{0,1},{1,2},{2,3},{3,4},{4,5},{5,6},{6,7},{7,0},{8,9},{9,10},{10,1... | collective-permute-start | bytes 774152 | tf_op jit(solution)/shard_map/ppermute | solution.py:290
  59.9 3.5 %collective-permute-start.3 = (f32[256,128]{1,0:T(8,128)S(1)}, f32[256,128]{1,0:T(8,128)S(1)}, u32[]{:S(2)}, u32[]{:S(2)}) collective-permute-start(f32[256,128]{1,0:T(8,128)S(1)} %slice.17), channel_id=1, source_target_pairs={{0,2},{1,3},{2,4},{3,5},{4,6},{5,7},{6,0},{7,1},{8,10},{9,11},{10,... | collective-permute-start | bytes 393224 | tf_op jit(solution)/shard_map/ppermute | solution.py:290
  63.4 0.9 slice.19
  64.3 4.8 %collective-permute-done.refs_0_ = f32[504,128]{1,0:T(8,128)S(1)} collective-permute-done((f32[504,128]{1,0:T(8,128)S(1)}, f32[504,128]{1,0:T(8,128)S(1)}, u32[]{:S(2)}, u32[]{:S(2)}) %collective-permute-start) | collective-permute-done | bytes 258080 | tf_op jit(solution)/shard_map/ppermute | solution.py:290
  69.1 3.9 %collective-permute-start.7 = (f32[248,128]{1,0:T(8,128)S(1)}, f32[248,128]{1,0:T(8,128)S(1)}, u32[]{:S(2)}, u32[]{:S(2)}) collective-permute-start(f32[248,128]{1,0:T(8,128)S(1)} %slice.19), channel_id=1, source_target_pairs={{0,6},{1,7},{2,0},{3,1},{4,2},{5,3},{6,4},{7,5},{8,14},{9,15},{10,... | collective-permute-start | bytes 380936 | tf_op jit(solution)/shard_map/ppermute | solution.py:290
  73.1 0.1 copy.14.depth_ref
  73.2 0.0 copy-start.7
  73.2 0.0 collective-permute-done.4.refs_4_
  73.2 4.7 %collective-permute-done.7.refs_7_ = f32[248,128]{1,0:T(8,128)S(1)} collective-permute-done((f32[248,128]{1,0:T(8,128)S(1)}, f32[248,128]{1,0:T(8,128)S(1)}, u32[]{:S(2)}, u32[]{:S(2)}) %collective-permute-start.7) | collective-permute-done | bytes 127008 | tf_op jit(solution)/shard_map/ppermute | solution.py:290
  77.9 1.4 collective-permute-done.3.refs_3_
  79.3 0.0 collective-permute-done.6.refs_6_
  79.3 0.0 collective-permute-done.2.refs_2_
  79.3 0.6 copy-done.16
  80.0 0.7 copy-done.15
  80.7 3.3 %unpack_legendre.1 = (f32[640,896]{1,0:T(8,128)}, f32[64,128]{1,0:T(8,128)}) custom-call(s32[2]{0:T(128)} %copy-done.6, f32[504,128]{1,0:T(8,128)} %copy-done.11, f32[504,128]{1,0:T(8,128)} %copy-done.14, f32[1264,128]{1,0:T(8,128)} %copy-done.12, f32[504,128]{1,0:T(8,128)} %copy-done.15, f32[256,128]{1,0:T(8,128)} %copy-done.16, ...), custom_call_target="tpu_custom_call" | custom-call | flops 10000000000 | bytes 5000000 | tf_op jit(solution)/shard_map/unpack_legendre/pallas_call | solution.py:362
  84.0 0.0 all-to-all-done
  84.0 0.1 copy.21
  84.1 1.6 %copy-done = f32[640,896]{1,0:T(8,128)S(1)} copy-done((f32[640,896]{1,0:T(8,128)S(1)}, f32[640,896]{1,0:T(8,128)}, u32[]{:S(2)}) %copy-start) | copy-done | bytes 2293784
  85.7 0.8 copy-done.2
  86.5 3.9 %legendre_round.1 = f32[512,384]{1,0:T(8,128)S(1)} custom-call(s32[2]{0:T(128)S(1)} %copy-done.7, s32[640]{0:T(1024)S(1)} %copy-done.5, f32[512,384]{1,0:T(8,128)S(1)} %bitcast.12, f32[32,32]{1,0:T(8,128)S(1)} %copy-done.3, f32[32,32]{1,0:T(8,128)S(1)} %copy-done.4, f32[32,1]{1,0:T(8,128)S(1)} %copy.14.depth_ref, f32[640,896]{1,0:T(8,128)S(1)} %copy-done, ...), custom_call_target="tpu_custom_call" | custom-call | tf_op jit(solution)/shard_map/legendre_round/pallas_call | solution.py:459
  90.4 0.0 copy-start.9
  90.5 0.8 copy.15
  91.3 45.5 %all_to_all.22 = f32[512,1,384]{2,1,0:T(1,128)S(1)} all-to-all(f32[512,1,384]{2,1,0:T(1,128)S(1)} %copy.15), channel_id=1, replica_groups=mesh['lat'=64,'fld'=8] {'fld','lat'}, dimensions={0} | all-to-all | bytes 1572864 | tf_op jit(solution)/shard_map/all_to_all | solution.py:486
  136.7 0.1 copy.20
  136.8 9.6 %inverse_fourier.1 = f32[2,10,4,2688]{3,2,1,0:T(4,128)} custom-call(s32[10]{0:T(128)S(1)} %copy-done.9, f32[1,640]{1,0:T(1,128)S(1)} %convert_element_type.23.waves_ref, f32[512,384]{1,0:T(8,128)S(1)} %bitcast.14), custom_call_target="tpu_custom_call" | custom-call | tf_op jit(solution)/shard_map/inverse_fourier/pallas_call | solution.py:211
  (27 shorter events, 0.1 us)
Async XLA Ops:
  0.8 1.6 %copy-start.1 = (f32[10,80,640]{2,1,0:T(8,128)S(1)}, f32[10,80,640]{2,1,0:T(8,128)}, u32[]{:S(2)}) copy-start(f32[10,80,640]{2,1,0:T(8,128)} %legendre_ref.1) | copy-start | bytes 6144004
  2.4 21.2 %copy-start.6 = (s32[2]{0:T(128)}, s32[2]{0:T(128)S(1)}, u32[]{:S(2)}) copy-start(s32[2]{0:T(128)S(1)} %pad_add_fusion.me_ref) | copy-start | bytes 28
  4.0 0.7 copy-start.11
  4.7 53.1 %collective-permute-start.1 = (f32[1264,128]{1,0:T(8,128)S(1)}, f32[1264,128]{1,0:T(8,128)S(1)}, u32[]{:S(2)}, u32[]{:S(2)}) collective-permute-start(f32[1264,128]{1,0:T(8,128)S(1)} %get-tuple-element.18), channel_id=1, source_target_pairs={{0,2},{1,3},{2,4},{3,5},{4,6},{5,7},{6,0},{7,1},{8,10},{9,11},{10,... | collective-permute-start | bytes 1941512 | tf_op jit(solution)/shard_map/ppermute | solution.py:290
  9.8 43.8 %collective-permute-start.5 = (f32[1256,128]{1,0:T(8,128)S(1)}, f32[1256,128]{1,0:T(8,128)}, u32[]{:S(2)}, u32[]{:S(2)}) collective-permute-start(f32[1256,128]{1,0:T(8,128)S(1)} %get-tuple-element.20), channel_id=1, source_target_pairs={{0,6},{1,7},{2,0},{3,1},{4,2},{5,3},{6,4},{7,5},{8,14},{9,15},{10,... | collective-permute-start | bytes 1929224 | tf_op jit(solution)/shard_map/ppermute | solution.py:290
  14.3 0.7 copy-start.8
  15.0 1.2 copy-start.10
  23.6 49.5 %copy-start.13 = (f32[32]{0:T(128)S(1)}, f32[32]{0:T(128)}, u32[]{:S(2)}) copy-start(f32[32]{0:T(128)} %param.15) | copy-start | bytes 388
  25.3 58.7 %all-to-all-start = ((f32[512,1,384]{2,1,0:T(1,128)}), f32[512,1,384]{2,1,0:T(1,128)S(1)}, u32[]{:S(2)}, u32[]{:S(2)}) async-start(f32[512,1,384]{2,1,0:T(1,128)} %copy.13), calls=%async_computation | async-start | bytes 1572864 | tf_op jit(solution)/shard_map/all_to_all | solution.py:481
  46.8 22.4 %collective-permute-start = (f32[504,128]{1,0:T(8,128)S(1)}, f32[504,128]{1,0:T(8,128)S(1)}, u32[]{:S(2)}, u32[]{:S(2)}) collective-permute-start(f32[504,128]{1,0:T(8,128)S(1)} %get-tuple-element.17), channel_id=1, source_target_pairs={{0,1},{1,2},{2,3},{3,4},{4,5},{5,6},{6,7},{7,0},{8,9},{9,10},{10,1... | collective-permute-start | bytes 774152 | tf_op jit(solution)/shard_map/ppermute | solution.py:290
  50.1 23.1 %collective-permute-start.4 = (f32[504,128]{1,0:T(8,128)S(1)}, f32[504,128]{1,0:T(8,128)}, u32[]{:S(2)}, u32[]{:S(2)}) collective-permute-start(f32[504,128]{1,0:T(8,128)S(1)} %get-tuple-element.19), channel_id=1, source_target_pairs={{0,7},{1,0},{2,1},{3,2},{4,3},{5,4},{6,5},{7,6},{8,15},{9,8},{10,9... | collective-permute-start | bytes 774152 | tf_op jit(solution)/shard_map/ppermute | solution.py:290
  54.5 24.8 %collective-permute-start.6 = (f32[504,128]{1,0:T(8,128)S(1)}, f32[504,128]{1,0:T(8,128)}, u32[]{:S(2)}, u32[]{:S(2)}) collective-permute-start(f32[504,128]{1,0:T(8,128)S(1)} %slice.18), channel_id=1, source_target_pairs={{0,7},{1,0},{2,1},{3,2},{4,3},{5,4},{6,5},{7,6},{8,15},{9,8},{10,9... | collective-permute-start | bytes 774152 | tf_op jit(solution)/shard_map/ppermute | solution.py:290
  57.9 21.4 %copy-start.12 = (f32[1264,128]{1,0:T(8,128)}, f32[1264,128]{1,0:T(8,128)S(1)}, u32[]{:S(2)}) copy-start(f32[1264,128]{1,0:T(8,128)S(1)} %collective-permute-done.1.refs_1_) | copy-start | bytes 1941508
  57.9 21.4 %collective-permute-start.2 = (f32[504,128]{1,0:T(8,128)S(1)}, f32[504,128]{1,0:T(8,128)S(1)}, u32[]{:S(2)}, u32[]{:S(2)}) collective-permute-start(f32[504,128]{1,0:T(8,128)S(1)} %slice.16), channel_id=1, source_target_pairs={{0,1},{1,2},{2,3},{3,4},{4,5},{5,6},{6,7},{7,0},{8,9},{9,10},{10,1... | collective-permute-start | bytes 774152 | tf_op jit(solution)/shard_map/ppermute | solution.py:290
  59.9 19.4 %collective-permute-start.3 = (f32[256,128]{1,0:T(8,128)S(1)}, f32[256,128]{1,0:T(8,128)S(1)}, u32[]{:S(2)}, u32[]{:S(2)}) collective-permute-start(f32[256,128]{1,0:T(8,128)S(1)} %slice.17), channel_id=1, source_target_pairs={{0,2},{1,3},{2,4},{3,5},{4,6},{5,7},{6,0},{7,1},{8,10},{9,11},{10,... | collective-permute-start | bytes 393224 | tf_op jit(solution)/shard_map/ppermute | solution.py:290
  69.1 4.0 %copy-start.14 = (f32[504,128]{1,0:T(8,128)}, f32[504,128]{1,0:T(8,128)S(1)}, u32[]{:S(2)}) copy-start(f32[504,128]{1,0:T(8,128)S(1)} %collective-permute-done.refs_0_) | copy-start | bytes 774148
  69.1 8.8 %collective-permute-start.7 = (f32[248,128]{1,0:T(8,128)S(1)}, f32[248,128]{1,0:T(8,128)S(1)}, u32[]{:S(2)}, u32[]{:S(2)}) collective-permute-start(f32[248,128]{1,0:T(8,128)S(1)} %slice.19), channel_id=1, source_target_pairs={{0,6},{1,7},{2,0},{3,1},{4,2},{5,3},{6,4},{7,5},{8,14},{9,15},{10,... | collective-permute-start | bytes 380936 | tf_op jit(solution)/shard_map/ppermute | solution.py:290
  73.2 10.9 %copy-start.3 = (f32[32,32]{1,0:T(8,128)S(1)}, f32[32,32]{1,0:T(8,128)}, u32[]{:S(2)}) copy-start(f32[32,32]{1,0:T(8,128)} %to_ref.1) | copy-start | bytes 12292
  73.2 10.9 %copy-start.4 = (f32[32,32]{1,0:T(8,128)S(1)}, f32[32,32]{1,0:T(8,128)}, u32[]{:S(2)}) copy-start(f32[32,32]{1,0:T(8,128)} %from_ref.1) | copy-start | bytes 12292
  73.2 10.9 %copy-start.5 = (s32[640]{0:T(1024)S(1)}, s32[640]{0:T(1024)}, u32[]{:S(2)}) copy-start(s32[640]{0:T(1024)} %assignment_ref.1) | copy-start | bytes 7684
  73.2 10.9 %copy-start.7 = (s32[2]{0:T(128)S(1)}, s32[2]{0:T(128)}, u32[]{:S(2)}) copy-start(s32[2]{0:T(128)} %copy-done.6) | copy-start | bytes 28
  77.9 1.5 %copy-start.17 = (f32[248,128]{1,0:T(8,128)}, f32[248,128]{1,0:T(8,128)S(1)}, u32[]{:S(2)}) copy-start(f32[248,128]{1,0:T(8,128)S(1)} %collective-permute-done.7.refs_7_) | copy-start | bytes 380932
  79.3 0.7 copy-start.16
  80.0 0.7 copy-start.15
  84.1 1.6 %copy-start = (f32[640,896]{1,0:T(8,128)S(1)}, f32[640,896]{1,0:T(8,128)}, u32[]{:S(2)}) copy-start(f32[640,896]{1,0:T(8,128)} %get-tuple-element.21.leg_ref) | copy-start | bytes 6881284
  85.7 0.8 copy-start.2
  90.4 46.3 %copy-start.9 = (s32[10]{0:T(128)S(1)}, s32[10]{0:T(128)}, u32[]{:S(2)}) copy-start(s32[10]{0:T(128)} %points_ref.3) | copy-start | bytes 124

commit v3 on v2

--- a/solution.py
+++ b/solution.py
@@ -21,7 +21,8 @@
 FLD = 8
 PART = 2 * HEMI * FIELDS
 MSG = ROWS * PART
-LANES = 384
+HALF_MSG = MSG // 2
+LANES = 256
 QUARTER = WAVES // 4
 LEG = 896
 BLOCK = FLD * ROWS
@@ -32,8 +33,8 @@
 WLANE = 64
 FIRST = 256
 VMEM = 20 << 20
-UNPACK_VMEM = 58 << 20
-UNPACK_COST = 10_000_000_000
+UNPACK_VMEM = 50 << 20
+UNPACK_COST = 9_000_000_000
 
 
 def halves(x):
@@ -121,18 +122,19 @@
     @pl.when(r == ROWS - 1)
     def _():
         y = fourier_ref[...]
+        top = lax.broadcasted_iota(jnp.int32, (8, 128), 0) < FIELDS
+        low = lax.broadcasted_iota(jnp.int32, (8, 128), 1) < 64
         shared = []
-        for q in range(2):
-            piece = y[:, 512 + 64 * q : 576 + 64 * q]
-            shared += [jnp.concatenate([piece, piece], axis=1)] * 2
-        full = jnp.concatenate(
-            [
-                y[:, :512],
-                jnp.concatenate(shared, axis=1),
-                jnp.zeros((LANES - 2 * MSG, 512), F32),
-            ],
-            axis=0,
-        )
+        for row in range(0, MSG, PART):
+            re, im = y[row : row + 8, 512:], y[row + 8 : row + PART, 512:]
+            re_other, im_other = pltpu.roll(re, FIELDS, 0), pltpu.roll(im, FIELDS, 0)
+            total = jnp.where(top, re + re_other, im + im_other)
+            change = jnp.where(top, re - re_other, im_other - im)
+            first = jnp.where(low, total, pltpu.roll(change, 64, 1))
+            second = jnp.where(low, pltpu.roll(total, 64, 1), change)
+            shared.append(jnp.concatenate([first, first, second, second], axis=1))
+        pad = jnp.zeros((LANES - MSG - HALF_MSG, 512), F32)
+        full = jnp.concatenate([y[:, :512], *shared, pad], axis=0)
         out_ref[...] = full.T
 
 
@@ -166,13 +168,21 @@
     def _():
         t = coeff_ref[...].T
         fourier_ref[:, :512] = t[:MSG]
-        lane = lax.broadcasted_iota(jnp.int32, (MSG, 128), 1)
-        sums = []
-        for q in range(2):
-            s = t[MSG : 2 * MSG, 256 * q : 256 * q + 128]
-            s = s + t[MSG : 2 * MSG, 256 * q + 128 : 256 * q + 256]
-            sums.append(s + pltpu.roll(s, 64, 1))
-        fourier_ref[:, 512:] = jnp.where(lane < 64, sums[0], sums[1])
+        top = lax.broadcasted_iota(jnp.int32, (8, 128), 0) < FIELDS
+        low = lax.broadcasted_iota(jnp.int32, (8, 128), 1) < 64
+        for i in range(ROWS):
+            rows = slice(MSG + 8 * i, MSG + 8 * i + 8)
+            one = t[rows, :128] + t[rows, 128:256]
+            two = t[rows, 256:384] + t[rows, 384:]
+            one_other, two_other = pltpu.roll(one, 64, 1), pltpu.roll(two, 64, 1)
+            north = jnp.where(low, one + one_other, two + two_other)
+            south = jnp.where(low, one - one_other, two_other - two)
+            fourier_ref[PART * i : PART * i + 8, 512:] = jnp.where(
+                top, north, pltpu.roll(south, FIELDS, 0)
+            )
+            fourier_ref[PART * i + 8 : PART * i + PART, 512:] = jnp.where(
+                top, pltpu.roll(north, FIELDS, 0), south
+            )
 
     count = points_ref[r]
     points = jnp.full((1, WAVES), count, jnp.int32).astype(F32)
@@ -227,15 +237,38 @@
     )(row_points, waves, coeffs)
 
 
+def quarter_degree(place):
+    quarter = sum((place >= QUARTER * i).astype(jnp.int32) for i in range(1, 4))
+    inside = place - QUARTER * quarter
+    return 2 * (QUARTER * (quarter >> 1) + inside) + (quarter & 1)
+
+
+def permuted(x, one_hot):
+    out = None
+    parts = []
+    for _ in range(3):
+        parts.append(x.astype(BF16))
+        x = x - parts[-1].astype(F32)
+    for part in reversed(parts):
+        moved = lax.dot_general(part, one_hot, (AB, ((), ())), preferred_element_type=F32)
+        out = moved if out is None else out + moved
+    return out
+
+
 def pack_kernel(me_ref, legendre_ref, weight_ref, *refs):
     near_refs = {0: refs[0], 1: refs[1], 7: refs[2]}
-    up_ref, down_ref, tile_ref = refs[3:]
+    up_ref, down_ref, tile_ref, order_ref = refs[3:]
     me = me_ref[0]
     lane = lax.broadcasted_iota(jnp.int32, (BLOCK, 128), 1)
     weight = jnp.concatenate(
         [weight_ref[...], jnp.zeros((FLD, 128 - ROWS), F32)], axis=1
     )
     weight = pltpu.roll(weight, WLANE, 1)
+    place = lax.broadcasted_iota(jnp.int32, (WAVES, WAVES), 1)
+    degree = lax.broadcasted_iota(jnp.int32, (WAVES, WAVES), 0)
+    one_hot = (degree == quarter_degree(place)).astype(BF16)
+    for q in range(2):
+        order_ref[q] = permuted(legendre_ref[FLD + q], one_hot)
     for t in range(FLD):
 
         def store(row, value, t=t):
@@ -252,9 +285,8 @@
             ref[pl.ds(at, FLD), :] = value
 
         g = lax.rem(me + t, FLD)
-        shared = FLD + g // 4
         shift = lax.rem(WAVES - QUARTER * lax.rem(g, 4), WAVES)
-        quarter = pltpu.roll(legendre_ref[shared], shift, 1)
+        quarter = pltpu.roll(order_ref[g // 4], shift, 1)
         own = legendre_ref[g]
         for i in range(5):
             tile_ref[t, i] = own[:, 128 * i : 128 * i + 128]
@@ -280,7 +312,10 @@
         in_specs=[pl.BlockSpec(memory_space=pltpu.SMEM), vmem, vmem],
         out_specs=[vmem] * 5,
         out_shape=[jax.ShapeDtypeStruct((n, 128), F32) for n in rows],
-        scratch_shapes=[pltpu.VMEM((FLD, LEG // 128, BLOCK, 128), F32)],
+        scratch_shapes=[
+            pltpu.VMEM((FLD, LEG // 128, BLOCK, 128), F32),
+            pltpu.VMEM((2, BLOCK, WAVES), F32),
+        ],
         compiler_params=pltpu.CompilerParams(vmem_limit_bytes=VMEM),
         name="pack_legendre",
     )(me, legendre, gauss_weights.reshape(FLD, ROWS))
@@ -322,7 +357,21 @@
     double = (ids((LEVELS, modes), 0) == ids((LEVELS, modes), 1) % LEVELS).astype(F32)
     wide = product(product(spread, from_modes), double)
     part, column = ids((parts, modes), 0) % PART, ids((parts, modes), 1)
-    return to_big, jnp.where(part // 8 == column // LEVELS, wide, 0.0)
+    from_big = jnp.where(part // 8 == column // LEVELS, wide, 0.0)
+
+    def half_field(part):
+        return part // 8 * FIELDS + part % FIELDS
+
+    spread = (ids((LEVELS, modes), 0) == half_field(ids((LEVELS, modes), 1))).astype(F32)
+    double = (ids((modes, LEVELS), 0) % LEVELS == ids((modes, LEVELS), 1)).astype(F32)
+    wide = product(double, product(to_modes, spread))
+    row, column = ids((modes, modes), 0), ids((modes, modes), 1)
+    to_half = jnp.where(row // LEVELS == column % 8 // FIELDS, wide, 0.0)
+    spread = (half_field(ids((modes, LEVELS), 0)) == ids((modes, LEVELS), 1)).astype(F32)
+    double = (ids((LEVELS, modes), 0) == ids((LEVELS, modes), 1) % LEVELS).astype(F32)
+    wide = product(product(spread, from_modes), double)
+    from_half = jnp.where(row % 8 // FIELDS == column // LEVELS, wide, 0.0)
+    return to_big, from_big, to_half, from_half
 
 
 def unpack_kernel(me_ref, own_msg, *refs):
@@ -398,58 +447,60 @@
     lh, ll = halves(leg_ref[...])
 
     t = coeff_ref[...].T
-    for kind, dest in ((0, a_ref), (1, x_ref)):
+    for start, part, dest in ((0, PART, a_ref), (MSG, 8, x_ref)):
         for u in range(ROWS // 2):
-            row = kind * MSG + 2 * u * PART
-            even, odd = t[row : row + PART], t[row + PART : row + 2 * PART]
+            row = start + 2 * u * part
+            even, odd = t[row : row + part], t[row + part : row + 2 * part]
             for g in range(FLD):
                 cut = slice(LAT * g, LAT * g + LAT)
-                dest[PART * g : PART * g + PART, 128 * u : 128 * u + 128] = (
+                dest[part * g : part * g + part, 128 * u : 128 * u + 128] = (
                     jnp.concatenate([even[:, cut], odd[:, cut]], axis=1)
                 )
     own = halves(a_ref[...] * weight)
     shared = halves(x_ref[...] * weight)
-    spectrum = jnp.concatenate(
-        [
-            dot_split(own, (lh[:, :WAVES], ll[:, :WAVES]), AB),
-            dot_split(shared, (lh[:, WAVES:], ll[:, WAVES:]), AB),
-        ],
-        axis=1,
-    )
-
-    to_big, from_big = mode_matrices(to_ref[...], from_ref[...])
+    to_big, from_big, to_half, from_half = mode_matrices(to_ref[...], from_ref[...])
+    spectrum = dot_split(own, (lh[:, :WAVES], ll[:, :WAVES]), AB)
     modes = dot_split(halves(to_big), halves(spectrum), AB)
+    spectrum = dot_split(shared, (lh[:, WAVES:], ll[:, WAVES:]), AB)
+    modes_shared = dot_split(halves(to_half), halves(spectrum), AB)
+
     lane = lax.broadcasted_iota(jnp.int32, (1, LEG), 1)
     is_own = lane < WAVES
-    degree = jnp.where(is_own, lane, lane - WAVES + QUARTER * lax.rem(fld, 4))
+    quarter = lax.rem(fld, 4)
+    place = QUARTER * (quarter // 2) + lane - WAVES
+    degree = jnp.where(is_own, lane, 2 * place + lax.rem(quarter, 2))
     wave_own = assignment_ref[lat * ROWS + fld]
     wave_shared = assignment_ref[lat * ROWS + FLD + fld // 4]
     total = degree + jnp.where(is_own, wave_own, wave_shared)
     within = (total < WAVES) & (lane < WAVES + QUARTER)
     total = jnp.where(within, total, 0)
-    sign = jnp.where((degree & 1) == 0, 1.0, -1.0)
+    sign = jnp.where((degree & 1) == 0, 1.0, -1.0)[:, :WAVES]
     ratio = (total * (total + 1)).astype(F32) * (1.0 / (WAVES * (WAVES + 1)))
     half = 2 * LEVELS
     depth = jnp.concatenate([depth_ref[...], depth_ref[...]], axis=0)
-    modes = modes[:half] + sign * modes[half:]
+    modes = jnp.concatenate(
+        [modes[:half] + sign * modes[half:], modes_shared], axis=1
+    )
     modes = jnp.where(within, modes, 0.0) / (1.0 + depth * ratio)
-    updated = dot_split(halves(from_big), halves(modes), AB)
+    updated = dot_split(halves(from_big), halves(modes[:, :WAVES]), AB)
     row_id = lax.broadcasted_iota(jnp.int32, updated.shape, 0)
     updated = jnp.where((row_id & FIELDS) == 0, updated, updated * sign)
-
-    for kind, cols in ((0, slice(0, WAVES)), (1, slice(WAVES, LEG))):
-        back = dot_split(halves(updated[:, cols]), (lh[:, cols], ll[:, cols]), ABT)
+    updated_shared = dot_split(halves(from_half), halves(modes[:, WAVES:]), AB)
+
+    back = dot_split(halves(updated), (lh[:, :WAVES], ll[:, :WAVES]), ABT)
+    back_shared = dot_split(halves(updated_shared), (lh[:, WAVES:], ll[:, WAVES:]), ABT)
+    for start, part, values in ((0, PART, back), (MSG, 8, back_shared)):
         for u in range(ROWS // 2):
-            row = kind * MSG + 2 * u * PART
+            row = start + 2 * u * part
             for g in range(0, FLD, 2):
-                one = back[PART * g : PART * g + PART, 128 * u : 128 * u + 128]
-                two = back[PART * g + PART : PART * g + 2 * PART, 128 * u : 128 * u + 128]
+                both = values[part * g : part * g + 2 * part, 128 * u : 128 * u + 128]
+                one, two = both[:part], both[part:]
                 for odd in range(2):
                     cut = slice(64 * odd, 64 * odd + 64)
                     y_ref[
-                        row + PART * odd : row + PART * odd + PART, LAT * g : LAT * g + 128
+                        row + part * odd : row + part * odd + part, LAT * g : LAT * g + 128
                     ] = jnp.concatenate([one[:, cut], two[:, cut]], axis=1)
-    y_ref[2 * MSG :, :] = jnp.zeros((LANES - 2 * MSG, LAT * FLD), F32)
+    y_ref[MSG + HALF_MSG :, :] = jnp.zeros((LANES - MSG - HALF_MSG, LAT * FLD), F32)
     out_ref[...] = y_ref[...].T
 
 
@@ -463,7 +514,7 @@
         out_shape=jax.ShapeDtypeStruct((LAT * FLD, LANES), F32),
         scratch_shapes=[
             pltpu.VMEM((PART * FLD, WAVES), F32),
-            pltpu.VMEM((PART * FLD, WAVES), F32),
+            pltpu.VMEM((8 * FLD, WAVES), F32),
             pltpu.VMEM((LANES, LAT * FLD), F32),
         ],
         compiler_params=pltpu.CompilerParams(vmem_limit_bytes=VMEM),

time: 147 us -> 157 us (1.068)
  waiting for transfers between devices: 10.9 us -> 35.3 us
  blocking collectives: 45.5 us -> 36.2 us
  local copies, waits for them, and re-layouts: 13.5 us -> 7.75 us
    ppermute x8, waiting for transfers between devices: 10.9 us -> 32 us  [shift(): return lax.ppermute(x, 'fld', [(i, (i + step) % FLD) for i in range(FLD)])]
    all_to_all x1, blocking collectives: 45.5 us -> 36.2 us  [body(): back = lax.all_to_all(synthesis, ('fld', 'lat'), 0, 0, tiled=True)]
    unnamed x38 -> x22, local copies, waits for them, and re-layouts: 7.97 us -> 4.01 us
    all_to_all x1, waiting for transfers between devices: 0.01 us -> 3.31 us  [body(): coeffs = lax.all_to_all(fourier, ('fld', 'lat'), 0, 0, tiled=True)]
  transfers between devices with their start and end apart: 9 -> 9, of which waited for: 3 -> 3; matrix products, arithmetic and copies ran while one was open for 3% -> 2% of each run, Pallas kernels for 7% -> 6%
where the time goes in v3:
time: 157 us; the launch traced here: 156 us
  starting transfers between devices  49.5 us (32%)
  blocking collectives  36.2 us (23%)
  waiting for transfers between devices  35.3 us (22%)
  Pallas kernels  26.4 us (17%)
  local copies, waits for them, and re-layouts  7.75 us (5%)
    all_to_all x1, blocking collectives, body(): back = lax.all_to_all(synthesis, ('fld', 'lat'), 0, 0, tiled=True)  36.2 us
    ppermute x8, waiting for transfers between devices, shift(): return lax.ppermute(x, 'fld', [(i, (i + step) % FLD) for i in range(FLD)])  32 us
    ppermute x8, starting transfers between devices, shift(): return lax.ppermute(x, 'fld', [(i, (i + step) % FLD) for i in range(FLD)])  28 us
    all_to_all x1, starting transfers between devices, body(): coeffs = lax.all_to_all(fourier, ('fld', 'lat'), 0, 0, tiled=True)  21.6 us
    pallas_call x1, Pallas kernels, inverse(): pl.pallas_call(inverse_kernel, grid=(ROWS,), in_specs=[pl.BlockSpec(memor...  9.49 us
    pallas_call x1, Pallas kernels, forward(): pl.pallas_call(forward_kernel, grid=(ROWS,), in_specs=[pl.BlockSpec(memor...  7.37 us
    unnamed x22, local copies, waits for them, and re-layouts  4.01 us
    pallas_call x1, Pallas kernels, legendre_round(): pl.pallas_call(legendre_kernel, in_specs=[smem, smem] + [vmem] * 6, out_s...  3.84 us
  transfers between devices with their start and end apart: 9, of which 3 were waited for; matrix products, arithmetic and copies ran while one was open for 2% of the time, Pallas kernels for 6%

profile of v3, /device:TPU:1, one launch (start us, length us, event | category | flops | bytes accessed | tf_op | source)
XLA Modules:
  0.0 156.2 jit_solution(10543452948314490676)
XLA Ops:
  0.0 0.0 copy-start.5
  0.0 0.7 reshape.26.weight_ref
  0.7 0.1 pad_add_fusion.me_ref
  0.8 1.6 %copy-done.1 = f32[10,80,640]{2,1,0:T(8,128)S(1)} copy-done((f32[10,80,640]{2,1,0:T(8,128)S(1)}, f32[10,80,640]{2,1,0:T(8,128)}, u32[]{:S(2)}) %copy-start.1) | copy-done | bytes 2048024
  2.4 3.0 %pack_legendre.1 = (f32[504,128]{1,0:T(8,128)S(1)}, f32[504,128]{1,0:T(8,128)}, f32[504,128]{1,0:T(8,128)}, f32[1264,128]{1,0:T(8,128)S(1)}, f32[1256,128]{1,0:T(8,128)S(1)}) custom-call(s32[2]{0:T(128)S(1)} %pad_add_fusion.me_ref, f32[10,80,640]{2,1,0:T(8,128)S(1)} %copy-done.1, f32[8,10]{1,0:T(8,128)S(1)} %reshape.26.weight_ref), custom_call_target="tpu_custom_call" | custom-call | tf_op jit(solution)/shard_map/pack_legendre/pallas_call | solution.py:310
  5.4 0.7 copy-done.7
  6.1 5.0 %collective-permute-start.1 = (f32[1264,128]{1,0:T(8,128)S(1)}, f32[1264,128]{1,0:T(8,128)S(1)}, u32[]{:S(2)}, u32[]{:S(2)}) collective-permute-start(f32[1264,128]{1,0:T(8,128)S(1)} %get-tuple-element.18), channel_id=1, source_target_pairs={{0,2},{1,3},{2,4},{3,5},{4,6},{5,7},{6,0},{7,1},{8,10},{9,11},{10,... | collective-permute-start | bytes 1941512 | tf_op jit(solution)/shard_map/ppermute | solution.py:325
  11.1 3.6 %collective-permute-start.5 = (f32[1256,128]{1,0:T(8,128)S(1)}, f32[1256,128]{1,0:T(8,128)S(1)}, u32[]{:S(2)}, u32[]{:S(2)}) collective-permute-start(f32[1256,128]{1,0:T(8,128)S(1)} %get-tuple-element.20), channel_id=1, source_target_pairs={{0,6},{1,7},{2,0},{3,1},{4,2},{5,3},{6,4},{7,5},{8,14},{9,15},{10,... | collective-permute-start | bytes 1929224 | tf_op jit(solution)/shard_map/ppermute | solution.py:325
  14.7 2.8 %collective-permute-start = (f32[504,128]{1,0:T(8,128)}, f32[504,128]{1,0:T(8,128)}, u32[]{:S(2)}, u32[]{:S(2)}) collective-permute-start(f32[504,128]{1,0:T(8,128)} %get-tuple-element.17), channel_id=1, source_target_pairs={{0,1},{1,2},{2,3},{3,4},{4,5},{5,6},{6,7},{7,0},{8,9},{9,10},{10,1... | collective-permute-start | bytes 774152 | tf_op jit(solution)/shard_map/ppermute | solution.py:325
  17.5 3.7 %collective-permute-start.4 = (f32[504,128]{1,0:T(8,128)}, f32[504,128]{1,0:T(8,128)}, u32[]{:S(2)}, u32[]{:S(2)}) collective-permute-start(f32[504,128]{1,0:T(8,128)} %get-tuple-element.19), channel_id=1, source_target_pairs={{0,7},{1,0},{2,1},{3,2},{4,3},{5,4},{6,5},{7,6},{8,15},{9,8},{10,9... | collective-permute-start | bytes 774152 | tf_op jit(solution)/shard_map/ppermute | solution.py:325
  21.2 0.7 convert_element_type.20
  21.9 0.1 convert_element_type.21
  22.0 0.1 copy.12
  22.1 0.1 convert_element_type.23.waves_ref
  22.2 23.1 %collective-permute-done.5.refs_5_ = f32[1256,128]{1,0:T(8,128)S(1)} collective-permute-done((f32[1256,128]{1,0:T(8,128)S(1)}, f32[1256,128]{1,0:T(8,128)S(1)}, u32[]{:S(2)}, u32[]{:S(2)}) %collective-permute-start.5) | collective-permute-done | bytes 643104 | tf_op jit(solution)/shard_map/ppermute | solution.py:325
  45.3 1.9 %collective-permute-start.6 = (f32[504,128]{1,0:T(8,128)S(1)}, f32[504,128]{1,0:T(8,128)S(1)}, u32[]{:S(2)}, u32[]{:S(2)}) collective-permute-start(f32[504,128]{1,0:T(8,128)S(1)} %slice.18), channel_id=1, source_target_pairs={{0,7},{1,0},{2,1},{3,2},{4,3},{5,4},{6,5},{7,6},{8,15},{9,8},{10,9... | collective-permute-start | bytes 774152 | tf_op jit(solution)/shard_map/ppermute | solution.py:325
  47.2 0.0 collective-permute-done.1.refs_1_
  47.2 0.7 slice.16
  47.9 3.3 %collective-permute-start.2 = (f32[504,128]{1,0:T(8,128)}, f32[504,128]{1,0:T(8,128)S(1)}, u32[]{:S(2)}, u32[]{:S(2)}) collective-permute-start(f32[504,128]{1,0:T(8,128)} %slice.16), channel_id=1, source_target_pairs={{0,1},{1,2},{2,3},{3,4},{4,5},{5,6},{6,7},{7,0},{8,9},{9,10},{10,1... | collective-permute-start | bytes 774152 | tf_op jit(solution)/shard_map/ppermute | solution.py:325
  51.3 0.0 copy-done.5
  51.3 0.0 copy-done.6
  51.3 7.4 %forward_fourier.1 = f32[512,256]{1,0:T(8,128)S(1)} custom-call(s32[10]{0:T(128)S(1)} %copy-done.5, f32[1,640]{1,0:T(1,128)S(1)} %convert_element_type.23.waves_ref, f32[2,10,4,2688]{3,2,1,0:T(4,128)S(1)} %copy-done.6), custom_call_target="tpu_custom_call" | custom-call | flops 3000000000 | bytes 2000000 | tf_op jit(solution)/shard_map/forward_fourier/pallas_call | solution.py:142
  58.7 0.0 copy-start.9
  58.7 0.0 copy-start.8
  58.7 1.3 copy.13
  60.0 21.6 %all-to-all-start = ((f32[512,1,256]{2,1,0:T(1,128)}), f32[512,1,256]{2,1,0:T(1,128)S(1)}, u32[]{:S(2)}, u32[]{:S(2)}) async-start(f32[512,1,256]{2,1,0:T(1,128)} %copy.13), calls=%async_computation | async-start | bytes 1048576 | tf_op jit(solution)/shard_map/all_to_all | solution.py:532
  81.6 4.2 %collective-permute-start.3 = (f32[256,128]{1,0:T(8,128)S(1)}, f32[256,128]{1,0:T(8,128)S(1)}, u32[]{:S(2)}, u32[]{:S(2)}) collective-permute-start(f32[256,128]{1,0:T(8,128)S(1)} %slice.17), channel_id=1, source_target_pairs={{0,2},{1,3},{2,4},{3,5},{4,6},{5,7},{6,0},{7,1},{8,10},{9,11},{10,... | collective-permute-start | bytes 393224 | tf_op jit(solution)/shard_map/ppermute | solution.py:325
  85.9 0.0 collective-permute-done.refs_0_
  85.9 3.4 %collective-permute-start.7 = (f32[248,128]{1,0:T(8,128)S(1)}, f32[248,128]{1,0:T(8,128)S(1)}, u32[]{:S(2)}, u32[]{:S(2)}) collective-permute-start(f32[248,128]{1,0:T(8,128)S(1)} %slice.19), channel_id=1, source_target_pairs={{0,6},{1,7},{2,0},{3,1},{4,2},{5,3},{6,4},{7,5},{8,14},{9,15},{10,... | collective-permute-start | bytes 380936 | tf_op jit(solution)/shard_map/ppermute | solution.py:325
  89.3 0.0 copy-done.9
  89.3 0.1 copy.14.depth_ref
  89.4 0.0 collective-permute-done.4.refs_4_
  89.4 8.9 %collective-permute-done.7.refs_7_ = f32[248,128]{1,0:T(8,128)S(1)} collective-permute-done((f32[248,128]{1,0:T(8,128)S(1)}, f32[248,128]{1,0:T(8,128)S(1)}, u32[]{:S(2)}, u32[]{:S(2)}) %collective-permute-start.7) | collective-permute-done | bytes 127008 | tf_op jit(solution)/shard_map/ppermute | solution.py:325
  98.3 0.0 collective-permute-done.3.refs_3_
  98.3 0.0 collective-permute-done.6.refs_6_
  98.3 0.0 collective-permute-done.2.refs_2_
  98.3 0.0 copy-done.8
  98.3 2.7 %unpack_legendre.1 = (f32[640,896]{1,0:T(8,128)}, f32[64,128]{1,0:T(8,128)S(1)}) custom-call(s32[2]{0:T(128)S(1)} %pad_add_fusion.me_ref, f32[504,128]{1,0:T(8,128)S(1)} %copy-done.8, f32[504,128]{1,0:T(8,128)} %collective-permute-done.refs_0_, f32[1264,128]{1,0:T(8,128)S(1)} %collective-permute-done.1.refs_1_, ...), custom_call_target="tpu_custom_call" | custom-call | flops 8999999488 | bytes 5000000 | tf_op jit(solution)/shard_map/unpack_legendre/pallas_call | solution.py:411
  101.0 3.3 %all-to-all-done = f32[512,1,256]{2,1,0:T(1,128)S(1)} async-done(((f32[512,1,256]{2,1,0:T(1,128)}), f32[512,1,256]{2,1,0:T(1,128)S(1)}, u32[]{:S(2)}, u32[]{:S(2)}) %all-to-all-start) | async-done | bytes 524320 | tf_op jit(solution)/shard_map/all_to_all | solution.py:532
  104.4 0.0 copy-done.2
  104.4 0.0 copy-done.3
  104.4 0.0 copy-done.4
  104.4 0.0 copy-start
  104.4 1.6 %copy-done = f32[640,896]{1,0:T(8,128)S(1)} copy-done((f32[640,896]{1,0:T(8,128)S(1)}, f32[640,896]{1,0:T(8,128)}, u32[]{:S(2)}) %copy-start) | copy-done | bytes 2293784
  106.1 3.8 %legendre_round.1 = f32[512,256]{1,0:T(8,128)S(1)} custom-call(s32[2]{0:T(128)S(1)} %pad_add_fusion.me_ref, s32[640]{0:T(1024)S(1)} %copy-done.4, f32[512,256]{1,0:T(8,128)S(1)} %bitcast.13, f32[32,32]{1,0:T(8,128)S(1)} %copy-done.2, f32[32,32]{1,0:T(8,128)S(1)} %copy-done.3, f32[32,1]{1,0:T(8,128)S(1)} %copy.14.depth_ref, f32[640,896]{1,0:T(8,128)S(1)} %copy-done, ...), custom_call_target="tpu_custom_call" | custom-call | tf_op jit(solution)/shard_map/legendre_round/pallas_call | solution.py:510
  109.9 0.5 copy.15
  110.5 36.2 %all_to_all.22 = f32[512,1,256]{2,1,0:T(1,128)S(1)} all-to-all(f32[512,1,256]{2,1,0:T(1,128)S(1)} %copy.15), channel_id=1, replica_groups=mesh['lat'=64,'fld'=8] {'fld','lat'}, dimensions={0} | all-to-all | bytes 1048576 | tf_op jit(solution)/shard_map/all_to_all | solution.py:537
  146.7 9.5 %inverse_fourier.1 = f32[2,10,4,2688]{3,2,1,0:T(4,128)} custom-call(s32[10]{0:T(128)S(1)} %copy-done.5, f32[1,640]{1,0:T(1,128)S(1)} %convert_element_type.23.waves_ref, f32[512,256]{1,0:T(8,128)S(1)} %bitcast.12), custom_call_target="tpu_custom_call" | custom-call | tf_op jit(solution)/shard_map/inverse_fourier/pallas_call | solution.py:221
  (11 shorter events, 0.1 us)
Async XLA Ops:
  0.0 51.3 %copy-start.5 = (s32[10]{0:T(128)S(1)}, s32[10]{0:T(128)}, u32[]{:S(2)}) copy-start(s32[10]{0:T(128)} %points_ref.3) | copy-start | bytes 124
  0.8 1.6 %copy-start.1 = (f32[10,80,640]{2,1,0:T(8,128)S(1)}, f32[10,80,640]{2,1,0:T(8,128)}, u32[]{:S(2)}) copy-start(f32[10,80,640]{2,1,0:T(8,128)} %legendre_ref.1) | copy-start | bytes 6144004
  2.4 48.9 %copy-start.6 = (f32[2,10,4,2688]{3,2,1,0:T(4,128)S(1)}, f32[2,10,4,2688]{3,2,1,0:T(4,128)}, u32[]{:S(2)}) copy-start(f32[2,10,4,2688]{3,2,1,0:T(4,128)} %grid_ref.1) | copy-start | bytes 2580484
  5.4 0.7 copy-start.7
  6.1 41.1 %collective-permute-start.1 = (f32[1264,128]{1,0:T(8,128)S(1)}, f32[1264,128]{1,0:T(8,128)S(1)}, u32[]{:S(2)}, u32[]{:S(2)}) collective-permute-start(f32[1264,128]{1,0:T(8,128)S(1)} %get-tuple-element.18), channel_id=1, source_target_pairs={{0,2},{1,3},{2,4},{3,5},{4,6},{5,7},{6,0},{7,1},{8,10},{9,11},{10,... | collective-permute-start | bytes 1941512 | tf_op jit(solution)/shard_map/ppermute | solution.py:325
  11.1 34.2 %collective-permute-start.5 = (f32[1256,128]{1,0:T(8,128)S(1)}, f32[1256,128]{1,0:T(8,128)S(1)}, u32[]{:S(2)}, u32[]{:S(2)}) collective-permute-start(f32[1256,128]{1,0:T(8,128)S(1)} %get-tuple-element.20), channel_id=1, source_target_pairs={{0,6},{1,7},{2,0},{3,1},{4,2},{5,3},{6,4},{7,5},{8,14},{9,15},{10,... | collective-permute-start | bytes 1929224 | tf_op jit(solution)/shard_map/ppermute | solution.py:325
  14.7 71.2 %collective-permute-start = (f32[504,128]{1,0:T(8,128)}, f32[504,128]{1,0:T(8,128)}, u32[]{:S(2)}, u32[]{:S(2)}) collective-permute-start(f32[504,128]{1,0:T(8,128)} %get-tuple-element.17), channel_id=1, source_target_pairs={{0,1},{1,2},{2,3},{3,4},{4,5},{5,6},{6,7},{7,0},{8,9},{9,10},{10,1... | collective-permute-start | bytes 774152 | tf_op jit(solution)/shard_map/ppermute | solution.py:325
  17.5 71.9 %collective-permute-start.4 = (f32[504,128]{1,0:T(8,128)}, f32[504,128]{1,0:T(8,128)}, u32[]{:S(2)}, u32[]{:S(2)}) collective-permute-start(f32[504,128]{1,0:T(8,128)} %get-tuple-element.19), channel_id=1, source_target_pairs={{0,7},{1,0},{2,1},{3,2},{4,3},{5,4},{6,5},{7,6},{8,15},{9,8},{10,9... | collective-permute-start | bytes 774152 | tf_op jit(solution)/shard_map/ppermute | solution.py:325
  45.3 53.0 %collective-permute-start.6 = (f32[504,128]{1,0:T(8,128)S(1)}, f32[504,128]{1,0:T(8,128)S(1)}, u32[]{:S(2)}, u32[]{:S(2)}) collective-permute-start(f32[504,128]{1,0:T(8,128)S(1)} %slice.18), channel_id=1, source_target_pairs={{0,7},{1,0},{2,1},{3,2},{4,3},{5,4},{6,5},{7,6},{8,15},{9,8},{10,9... | collective-permute-start | bytes 774152 | tf_op jit(solution)/shard_map/ppermute | solution.py:325
  47.9 50.3 %collective-permute-start.2 = (f32[504,128]{1,0:T(8,128)}, f32[504,128]{1,0:T(8,128)S(1)}, u32[]{:S(2)}, u32[]{:S(2)}) collective-permute-start(f32[504,128]{1,0:T(8,128)} %slice.16), channel_id=1, source_target_pairs={{0,1},{1,2},{2,3},{3,4},{4,5},{5,6},{6,7},{7,0},{8,9},{9,10},{10,1... | collective-permute-start | bytes 774152 | tf_op jit(solution)/shard_map/ppermute | solution.py:325
  58.7 30.6 %copy-start.9 = (f32[32]{0:T(128)S(1)}, f32[32]{0:T(128)}, u32[]{:S(2)}) copy-start(f32[32]{0:T(128)} %param.15) | copy-start | bytes 388
  58.7 39.6 %copy-start.8 = (f32[504,128]{1,0:T(8,128)S(1)}, f32[504,128]{1,0:T(8,128)}, u32[]{:S(2)}) copy-start(f32[504,128]{1,0:T(8,128)} %copy-done.7) | copy-start | bytes 774148
  60.0 44.3 %all-to-all-start = ((f32[512,1,256]{2,1,0:T(1,128)}), f32[512,1,256]{2,1,0:T(1,128)S(1)}, u32[]{:S(2)}, u32[]{:S(2)}) async-start(f32[512,1,256]{2,1,0:T(1,128)} %copy.13), calls=%async_computation | async-start | bytes 1048576 | tf_op jit(solution)/shard_map/all_to_all | solution.py:532
  81.6 16.6 %collective-permute-start.3 = (f32[256,128]{1,0:T(8,128)S(1)}, f32[256,128]{1,0:T(8,128)S(1)}, u32[]{:S(2)}, u32[]{:S(2)}) collective-permute-start(f32[256,128]{1,0:T(8,128)S(1)} %slice.17), channel_id=1, source_target_pairs={{0,2},{1,3},{2,4},{3,5},{4,6},{5,7},{6,0},{7,1},{8,10},{9,11},{10,... | collective-permute-start | bytes 393224 | tf_op jit(solution)/shard_map/ppermute | solution.py:325
  85.9 12.4 %collective-permute-start.7 = (f32[248,128]{1,0:T(8,128)S(1)}, f32[248,128]{1,0:T(8,128)S(1)}, u32[]{:S(2)}, u32[]{:S(2)}) collective-permute-start(f32[248,128]{1,0:T(8,128)S(1)} %slice.19), channel_id=1, source_target_pairs={{0,6},{1,7},{2,0},{3,1},{4,2},{5,3},{6,4},{7,5},{8,14},{9,15},{10,... | collective-permute-start | bytes 380936 | tf_op jit(solution)/shard_map/ppermute | solution.py:325
  89.4 15.0 %copy-start.2 = (f32[32,32]{1,0:T(8,128)S(1)}, f32[32,32]{1,0:T(8,128)}, u32[]{:S(2)}) copy-start(f32[32,32]{1,0:T(8,128)} %to_ref.1) | copy-start | bytes 12292
  89.4 15.0 %copy-start.3 = (f32[32,32]{1,0:T(8,128)S(1)}, f32[32,32]{1,0:T(8,128)}, u32[]{:S(2)}) copy-start(f32[32,32]{1,0:T(8,128)} %from_ref.1) | copy-start | bytes 12292
  89.4 15.0 %copy-start.4 = (s32[640]{0:T(1024)S(1)}, s32[640]{0:T(1024)}, u32[]{:S(2)}) copy-start(s32[640]{0:T(1024)} %assignment_ref.1) | copy-start | bytes 7684
  104.4 1.6 %copy-start = (f32[640,896]{1,0:T(8,128)S(1)}, f32[640,896]{1,0:T(8,128)}, u32[]{:S(2)}) copy-start(f32[640,896]{1,0:T(8,128)} %get-tuple-element.21.leg_ref) | copy-start | bytes 6881284

commit v4 on v3

--- a/solution.py
+++ b/solution.py
@@ -33,8 +33,8 @@
 WLANE = 64
 FIRST = 256
 VMEM = 20 << 20
-UNPACK_VMEM = 50 << 20
-UNPACK_COST = 9_000_000_000
+ROUND_VMEM = 48 << 20
+TRAVEL_COST = 5_000_000_000
 
 
 def halves(x):
@@ -261,8 +261,9 @@
     me = me_ref[0]
     lane = lax.broadcasted_iota(jnp.int32, (BLOCK, 128), 1)
     weight = jnp.concatenate(
-        [weight_ref[...], jnp.zeros((FLD, 128 - ROWS), F32)], axis=1
-    )
+        [weight_ref[:, ROWS * d : ROWS * d + ROWS] for d in range(FLD)], axis=0
+    )
+    weight = jnp.concatenate([weight, jnp.zeros((FLD, 128 - ROWS), F32)], axis=1)
     weight = pltpu.roll(weight, WLANE, 1)
     place = lax.broadcasted_iota(jnp.int32, (WAVES, WAVES), 1)
     degree = lax.broadcasted_iota(jnp.int32, (WAVES, WAVES), 0)
@@ -318,7 +319,7 @@
         ],
         compiler_params=pltpu.CompilerParams(vmem_limit_bytes=VMEM),
         name="pack_legendre",
-    )(me, legendre, gauss_weights.reshape(FLD, ROWS))
+    )(me, legendre, gauss_weights.reshape(1, BLOCK))
 
 
 def shift(x, step):
@@ -374,9 +375,7 @@
     return to_big, from_big, to_half, from_half
 
 
-def unpack_kernel(me_ref, own_msg, *refs):
-    ups, downs, (leg_ref, weight_ref) = refs[:4], refs[4:8], refs[8:]
-    fld = me_ref[0]
+def unpack(fld, own_msg, ups, downs, leg_ref, weight_ref):
     lane = lax.broadcasted_iota(jnp.int32, (FLD, 128), 1)
     for t in range(FLD):
 
@@ -403,43 +402,31 @@
         weight_ref[pl.ds(pl.multiple_of(FLD * source, FLD), FLD), :] = load(REST + 2 * FLD)
 
 
-def unpack(me, own, moved):
-    vmem = pl.BlockSpec(memory_space=pltpu.VMEM)
-    taken = [
-        pl.BlockSpec((min(LMSG, x.shape[0]), 128), lambda i: (0, 0)) for x in moved
-    ]
+def arrival_kernel(*refs):
+    refs[-1][...] = jnp.zeros((8, 128), F32)
+
+
+def arrival(moved):
     return pl.pallas_call(
-        unpack_kernel,
-        grid=(1,),
-        in_specs=[pl.BlockSpec(memory_space=pltpu.SMEM), vmem] + taken,
-        out_specs=[vmem, vmem],
-        out_shape=[
-            jax.ShapeDtypeStruct((WAVES, LEG), F32),
-            jax.ShapeDtypeStruct((LAT, 128), F32),
-        ],
-        compiler_params=pltpu.CompilerParams(vmem_limit_bytes=UNPACK_VMEM),
+        arrival_kernel,
+        in_specs=[pl.BlockSpec(memory_space=pl.ANY)] * len(moved),
+        out_specs=pl.BlockSpec(memory_space=pltpu.VMEM),
+        out_shape=jax.ShapeDtypeStruct((8, 128), F32),
+        compiler_params=pltpu.CompilerParams(vmem_limit_bytes=1 << 20),
         cost_estimate=pl.CostEstimate(
-            flops=UNPACK_COST, bytes_accessed=5_000_000, transcendentals=0
+            flops=TRAVEL_COST, bytes_accessed=0, transcendentals=0
         ),
-        name="unpack_legendre",
-    )(me, own, *moved)
+        name="arrival",
+    )(*moved)
 
 
 def legendre_kernel(
-    me_ref,
-    assignment_ref,
-    coeff_ref,
-    to_ref,
-    from_ref,
-    depth_ref,
-    leg_ref,
-    weight_ref,
-    out_ref,
-    a_ref,
-    x_ref,
-    y_ref,
+    me_ref, assignment_ref, coeff_ref, to_ref, from_ref, depth_ref, zero_ref, *refs
 ):
+    own_msg, ups, downs = refs[0], refs[1:5], refs[5:9]
+    out_ref, leg_ref, weight_ref, a_ref, x_ref, y_ref = refs[9:]
     lat, fld = me_ref[1], me_ref[0]
+    unpack(fld, own_msg, ups, downs, leg_ref, weight_ref)
     weight = weight_ref[...].T
     weight = jnp.concatenate(
         [weight[WLANE + r : WLANE + r + 1] for r in range(ROWS)], axis=1
@@ -507,17 +494,23 @@
 def legendre_round(*args):
     smem = pl.BlockSpec(memory_space=pltpu.SMEM)
     vmem = pl.BlockSpec(memory_space=pltpu.VMEM)
+    taken = [
+        pl.BlockSpec((min(LMSG, x.shape[0]), 128), lambda i: (0, 0)) for x in args[8:]
+    ]
     return pl.pallas_call(
         legendre_kernel,
-        in_specs=[smem, smem] + [vmem] * 6,
+        grid=(1,),
+        in_specs=[smem, smem] + [vmem] * 6 + taken,
         out_specs=vmem,
         out_shape=jax.ShapeDtypeStruct((LAT * FLD, LANES), F32),
         scratch_shapes=[
+            pltpu.VMEM((WAVES, LEG), F32),
+            pltpu.VMEM((LAT, 128), F32),
             pltpu.VMEM((PART * FLD, WAVES), F32),
             pltpu.VMEM((8 * FLD, WAVES), F32),
             pltpu.VMEM((LANES, LAT * FLD), F32),
         ],
-        compiler_params=pltpu.CompilerParams(vmem_limit_bytes=VMEM),
+        compiler_params=pltpu.CompilerParams(vmem_limit_bytes=ROUND_VMEM),
         name="legendre_round",
     )(*args)
 
@@ -527,12 +520,13 @@
     me = jnp.stack([lax.axis_index("fld"), lax.axis_index("lat")]).astype(jnp.int32)
     own, *messages = pack(me, legendre, gauss_weights)
     waves, own = lax.optimization_barrier((waves, own))
-    rows, weight = unpack(me, own, ring(*messages))
+    moved = ring(*messages)
+    zero = arrival(moved)
     fourier = forward(row_points, waves, grid)
     coeffs = lax.all_to_all(fourier, ("fld", "lat"), 0, 0, tiled=True)
     depths = mode_depths.reshape(LEVELS, 1)
     synthesis = legendre_round(
-        me, assignment, coeffs, to_modes, from_modes, depths, rows, weight
+        me, assignment, coeffs, to_modes, from_modes, depths, zero, own, *moved
     )
     back = lax.all_to_all(synthesis, ("fld", "lat"), 0, 0, tiled=True)
     return inverse(row_points, waves, back)

time: 157 us -> 131 us (0.83)
  waiting for transfers between devices: 35.3 us -> 5.77 us
  blocking collectives: 36.2 us -> 42.1 us
  Pallas kernels: 26.4 us -> 24 us
  starting transfers between devices: 49.5 us -> 51.6 us
    ppermute x8, waiting for transfers between devices: 32 us -> 5.77 us  [shift(): return lax.ppermute(x, 'fld', [(i, (i + step) % FLD) for i in range(FLD)])]
    all_to_all x1, blocking collectives: 36.2 us -> 42.1 us  [body(): back = lax.all_to_all(synthesis, ('fld', 'lat'), 0, 0, tiled=True)]
    all_to_all x1, waiting for transfers between devices: 3.31 us -> 0.01 us  [body(): coeffs = lax.all_to_all(fourier, ('fld', 'lat'), 0, 0, tiled=True)]
    pallas_call x2, Pallas kernels: 6.59 us -> 3.97 us  [the longest x1 3.97 us: legendre_round(): pl.pallas_call(legendre_kernel, grid=(1,), in_specs=[smem, smem] + [vmem]...]
    all_to_all x1, starting transfers between devices: 21.6 us -> 23.6 us  [body(): coeffs = lax.all_to_all(fourier, ('fld', 'lat'), 0, 0, tiled=True)]
    unnamed x22 -> x18, local copies, waits for them, and re-layouts: 4.01 us -> 3.36 us
  transfers between devices with their start and end apart: 9 -> 9, of which waited for: 3 -> 1; matrix products, arithmetic and copies ran while one was open for 2% -> 2% of each run, Pallas kernels for 6% -> 6%
where the time goes in v4:
time: 131 us; the launch traced here: 130 us
  starting transfers between devices  51.6 us (39%)
  blocking collectives  42.1 us (32%)
  Pallas kernels  24 us (18%)
  local copies, waits for them, and re-layouts  6.37 us (5%)
  waiting for transfers between devices  5.77 us (4%)
    all_to_all x1, blocking collectives, body(): back = lax.all_to_all(synthesis, ('fld', 'lat'), 0, 0, tiled=True)  42.1 us
    ppermute x8, starting transfers between devices, shift(): return lax.ppermute(x, 'fld', [(i, (i + step) % FLD) for i in range(FLD)])  28 us
    all_to_all x1, starting transfers between devices, body(): coeffs = lax.all_to_all(fourier, ('fld', 'lat'), 0, 0, tiled=True)  23.6 us
    pallas_call x1, Pallas kernels, inverse(): pl.pallas_call(inverse_kernel, grid=(ROWS,), in_specs=[pl.BlockSpec(memor...  9.49 us
    pallas_call x1, Pallas kernels, forward(): pl.pallas_call(forward_kernel, grid=(ROWS,), in_specs=[pl.BlockSpec(memor...  7.38 us
    ppermute x8, waiting for transfers between devices, shift(): return lax.ppermute(x, 'fld', [(i, (i + step) % FLD) for i in range(FLD)])  5.77 us
    pallas_call x1, Pallas kernels, legendre_round(): pl.pallas_call(legendre_kernel, grid=(1,), in_specs=[smem, smem] + [vmem]...  3.97 us
    unnamed x18, local copies, waits for them, and re-layouts  3.36 us
  transfers between devices with their start and end apart: 9, of which 1 were waited for; matrix products, arithmetic and copies ran while one was open for 2% of the time, Pallas kernels for 6%

profile of v4, /device:TPU:1, one launch (start us, length us, event | category | flops | bytes accessed | tf_op | source)
XLA Modules:
  0.0 130.2 jit_solution(18257343383856254977)
XLA Ops:
  0.0 0.0 copy-start.3
  0.0 0.0 copy-start.5
  0.0 0.1 pad_add_fusion.me_ref
  0.1 0.0 copy-start
  0.1 1.6 %copy-done = f32[10,80,640]{2,1,0:T(8,128)S(1)} copy-done((f32[10,80,640]{2,1,0:T(8,128)S(1)}, f32[10,80,640]{2,1,0:T(8,128)}, u32[]{:S(2)}) %copy-start) | copy-done | bytes 2048024
  1.7 0.0 copy-start.4
  1.7 0.7 copy-done.4
  2.3 0.0 copy-start.6
  2.3 3.2 %pack_legendre.1 = (f32[504,128]{1,0:T(8,128)S(1)}, f32[504,128]{1,0:T(8,128)}, f32[504,128]{1,0:T(8,128)}, f32[1264,128]{1,0:T(8,128)S(1)}, f32[1256,128]{1,0:T(8,128)}) custom-call(s32[2]{0:T(128)S(1)} %pad_add_fusion.me_ref, f32[10,80,640]{2,1,0:T(8,128)S(1)} %copy-done, f32[1,80]{1,0:T(1,128)S(1)} %bitcast.17), custom_call_target="tpu_custom_call" | custom-call | tf_op jit(solution)/shard_map/pack_legendre/pallas_call | solution.py:311
  5.5 5.0 %collective-permute-start.1 = (f32[1264,128]{1,0:T(8,128)S(1)}, f32[1264,128]{1,0:T(8,128)S(1)}, u32[]{:S(2)}, u32[]{:S(2)}) collective-permute-start(f32[1264,128]{1,0:T(8,128)S(1)} %get-tuple-element.15), channel_id=1, source_target_pairs={{0,2},{1,3},{2,4},{3,5},{4,6},{5,7},{6,0},{7,1},{8,10},{9,11},{10,... | collective-permute-start | bytes 1941512 | tf_op jit(solution)/shard_map/ppermute | solution.py:326
  10.5 3.6 %collective-permute-start.5 = (f32[1256,128]{1,0:T(8,128)}, f32[1256,128]{1,0:T(8,128)S(1)}, u32[]{:S(2)}, u32[]{:S(2)}) collective-permute-start(f32[1256,128]{1,0:T(8,128)} %get-tuple-element.17), channel_id=1, source_target_pairs={{0,6},{1,7},{2,0},{3,1},{4,2},{5,3},{6,4},{7,5},{8,14},{9,15},{10,... | collective-permute-start | bytes 1929224 | tf_op jit(solution)/shard_map/ppermute | solution.py:326
  14.1 0.0 copy-done.3
  14.2 0.1 convert_element_type.21
  14.3 0.1 copy.12
  14.4 0.1 convert_element_type.23.waves_ref
  14.4 0.0 copy-done.5
  14.4 0.0 copy-done.6
  14.4 7.4 %forward_fourier.1 = f32[512,256]{1,0:T(8,128)S(1)} custom-call(s32[10]{0:T(128)S(1)} %copy-done.5, f32[1,640]{1,0:T(1,128)S(1)} %convert_element_type.23.waves_ref, f32[2,10,4,2688]{3,2,1,0:T(4,128)S(1)} %copy-done.6), custom_call_target="tpu_custom_call" | custom-call | flops 3000000000 | bytes 2000000 | tf_op jit(solution)/shard_map/forward_fourier/pallas_call | solution.py:142
  21.8 0.0 copy-start.7
  21.8 1.3 %copy.13 = f32[512,1,256]{2,1,0:T(1,128)} copy(f32[512,1,256]{2,0,1:T(8,128)S(1)} %bitcast.16) | data formatting | bytes 1048576 | tf_op jit(solution)/shard_map/all_to_all | solution.py:526
  23.2 23.6 %all-to-all-start = ((f32[512,1,256]{2,1,0:T(1,128)}), f32[512,1,256]{2,1,0:T(1,128)}, u32[]{:S(2)}, u32[]{:S(2)}) async-start(f32[512,1,256]{2,1,0:T(1,128)} %copy.13), calls=%async_computation | async-start | bytes 1048576 | tf_op jit(solution)/shard_map/all_to_all | solution.py:526
  46.7 3.3 %collective-permute-start = (f32[504,128]{1,0:T(8,128)}, f32[504,128]{1,0:T(8,128)S(1)}, u32[]{:S(2)}, u32[]{:S(2)}) collective-permute-start(f32[504,128]{1,0:T(8,128)} %get-tuple-element.14), channel_id=1, source_target_pairs={{0,1},{1,2},{2,3},{3,4},{4,5},{5,6},{6,7},{7,0},{8,9},{9,10},{10,1... | collective-permute-start | bytes 774152 | tf_op jit(solution)/shard_map/ppermute | solution.py:326
  50.1 3.5 %collective-permute-start.4 = (f32[504,128]{1,0:T(8,128)}, f32[504,128]{1,0:T(8,128)S(1)}, u32[]{:S(2)}, u32[]{:S(2)}) collective-permute-start(f32[504,128]{1,0:T(8,128)} %get-tuple-element.16), channel_id=1, source_target_pairs={{0,7},{1,0},{2,1},{3,2},{4,3},{5,4},{6,5},{7,6},{8,15},{9,8},{10,9... | collective-permute-start | bytes 774152 | tf_op jit(solution)/shard_map/ppermute | solution.py:326
  53.5 0.0 collective-permute-done.5.refs_5_.refs_6_
  53.5 0.7 slice.18
  54.2 3.3 %collective-permute-start.6 = (f32[504,128]{1,0:T(8,128)}, f32[504,128]{1,0:T(8,128)S(1)}, u32[]{:S(2)}, u32[]{:S(2)}) collective-permute-start(f32[504,128]{1,0:T(8,128)} %slice.18), channel_id=1, source_target_pairs={{0,7},{1,0},{2,1},{3,2},{4,3},{5,4},{6,5},{7,6},{8,15},{9,8},{10,9... | collective-permute-start | bytes 774152 | tf_op jit(solution)/shard_map/ppermute | solution.py:326
  57.6 0.0 collective-permute-done.1.refs_1_.refs_2_
  57.6 1.9 %collective-permute-start.2 = (f32[504,128]{1,0:T(8,128)S(1)}, f32[504,128]{1,0:T(8,128)S(1)}, u32[]{:S(2)}, u32[]{:S(2)}) collective-permute-start(f32[504,128]{1,0:T(8,128)S(1)} %slice.16), channel_id=1, source_target_pairs={{0,1},{1,2},{2,3},{3,4},{4,5},{5,6},{6,7},{7,0},{8,9},{9,10},{10,1... | collective-permute-start | bytes 774152 | tf_op jit(solution)/shard_map/ppermute | solution.py:326
  59.6 3.5 %collective-permute-start.3 = (f32[256,128]{1,0:T(8,128)S(1)}, f32[256,128]{1,0:T(8,128)S(1)}, u32[]{:S(2)}, u32[]{:S(2)}) collective-permute-start(f32[256,128]{1,0:T(8,128)S(1)} %slice.17), channel_id=1, source_target_pairs={{0,2},{1,3},{2,4},{3,5},{4,6},{5,7},{6,0},{7,1},{8,10},{9,11},{10,... | collective-permute-start | bytes 393224 | tf_op jit(solution)/shard_map/ppermute | solution.py:326
  63.1 0.0 collective-permute-done.refs_0_.refs_1_
  63.1 3.9 %collective-permute-start.7 = (f32[248,128]{1,0:T(8,128)S(1)}, f32[248,128]{1,0:T(8,128)S(1)}, u32[]{:S(2)}, u32[]{:S(2)}) collective-permute-start(f32[248,128]{1,0:T(8,128)S(1)} %slice.19), channel_id=1, source_target_pairs={{0,6},{1,7},{2,0},{3,1},{4,2},{5,3},{6,4},{7,5},{8,14},{9,15},{10,... | collective-permute-start | bytes 380936 | tf_op jit(solution)/shard_map/ppermute | solution.py:326
  67.0 0.0 copy-done.7
  67.0 0.1 copy.14.depth_ref
  67.1 0.0 copy-start.1
  67.1 0.0 copy-start.2
  67.1 0.0 collective-permute-done.4.refs_4_.refs_5_
  67.1 5.7 %collective-permute-done.7.refs_7_.refs_8_ = f32[248,128]{1,0:T(8,128)S(1)} collective-permute-done((f32[248,128]{1,0:T(8,128)S(1)}, f32[248,128]{1,0:T(8,128)S(1)}, u32[]{:S(2)}, u32[]{:S(2)}) %collective-permute-start.7) | collective-permute-done | bytes 127008 | tf_op jit(solution)/shard_map/ppermute | solution.py:326
  72.9 0.0 collective-permute-done.3.refs_3_.refs_4_
  72.9 0.0 collective-permute-done.6.refs_6_.refs_7_
  72.9 0.0 collective-permute-done.2.refs_2_.refs_3_
  72.9 0.0 all-to-all-done
  72.9 1.1 copy.21
  74.0 0.0 copy-done.1
  74.0 0.0 copy-done.2
  74.0 4.0 %legendre_round.1 = f32[512,256]{1,0:T(8,128)S(1)} custom-call(s32[2]{0:T(128)S(1)} %pad_add_fusion.me_ref, s32[640]{0:T(1024)S(1)} %copy-done.3, f32[512,256]{1,0:T(8,128)S(1)} %bitcast.13, f32[32,32]{1,0:T(8,128)S(1)} %copy-done.1, f32[32,32]{1,0:T(8,128)S(1)} %copy-done.2, f32[32,1]{1,0:T(8,128)S(1)} %copy.14.depth_ref, f32[8,128]{1,0:T(8,128)S(1)} %arrival.1.zero_ref, ...), custom_call_target="tpu_custom_call" | custom-call | tf_op jit(solution)/shard_map/legendre_round/pallas_call | solution.py:500
  78.0 0.5 copy.15
  78.5 42.1 %all_to_all.22 = f32[512,1,256]{2,1,0:T(1,128)S(1)} all-to-all(f32[512,1,256]{2,1,0:T(1,128)S(1)} %copy.15), channel_id=1, replica_groups=mesh['lat'=64,'fld'=8] {'fld','lat'}, dimensions={0} | all-to-all | bytes 1048576 | tf_op jit(solution)/shard_map/all_to_all | solution.py:531
  120.7 9.5 %inverse_fourier.1 = f32[2,10,4,2688]{3,2,1,0:T(4,128)} custom-call(s32[10]{0:T(128)S(1)} %copy-done.5, f32[1,640]{1,0:T(1,128)S(1)} %convert_element_type.23.waves_ref, f32[512,256]{1,0:T(8,128)S(1)} %bitcast.15), custom_call_target="tpu_custom_call" | custom-call | tf_op jit(solution)/shard_map/inverse_fourier/pallas_call | solution.py:221
  (6 shorter events, 0.1 us)
Async XLA Ops:
  0.0 14.1 %copy-start.3 = (s32[640]{0:T(1024)S(1)}, s32[640]{0:T(1024)}, u32[]{:S(2)}) copy-start(s32[640]{0:T(1024)} %assignment_ref.1) | copy-start | bytes 7684
  0.0 14.4 %copy-start.5 = (s32[10]{0:T(128)S(1)}, s32[10]{0:T(128)}, u32[]{:S(2)}) copy-start(s32[10]{0:T(128)} %points_ref.3) | copy-start | bytes 124
  0.1 1.6 %copy-start = (f32[10,80,640]{2,1,0:T(8,128)S(1)}, f32[10,80,640]{2,1,0:T(8,128)}, u32[]{:S(2)}) copy-start(f32[10,80,640]{2,1,0:T(8,128)} %legendre_ref.1) | copy-start | bytes 6144004
  1.7 0.7 copy-start.4
  2.3 12.1 %copy-start.6 = (f32[2,10,4,2688]{3,2,1,0:T(4,128)S(1)}, f32[2,10,4,2688]{3,2,1,0:T(4,128)}, u32[]{:S(2)}) copy-start(f32[2,10,4,2688]{3,2,1,0:T(4,128)} %grid_ref.1) | copy-start | bytes 2580484
  5.5 52.1 %collective-permute-start.1 = (f32[1264,128]{1,0:T(8,128)S(1)}, f32[1264,128]{1,0:T(8,128)S(1)}, u32[]{:S(2)}, u32[]{:S(2)}) collective-permute-start(f32[1264,128]{1,0:T(8,128)S(1)} %get-tuple-element.15), channel_id=1, source_target_pairs={{0,2},{1,3},{2,4},{3,5},{4,6},{5,7},{6,0},{7,1},{8,10},{9,11},{10,... | collective-permute-start | bytes 1941512 | tf_op jit(solution)/shard_map/ppermute | solution.py:326
  10.5 43.0 %collective-permute-start.5 = (f32[1256,128]{1,0:T(8,128)}, f32[1256,128]{1,0:T(8,128)S(1)}, u32[]{:S(2)}, u32[]{:S(2)}) collective-permute-start(f32[1256,128]{1,0:T(8,128)} %get-tuple-element.17), channel_id=1, source_target_pairs={{0,6},{1,7},{2,0},{3,1},{4,2},{5,3},{6,4},{7,5},{8,14},{9,15},{10,... | collective-permute-start | bytes 1929224 | tf_op jit(solution)/shard_map/ppermute | solution.py:326
  21.8 45.2 %copy-start.7 = (f32[32]{0:T(128)S(1)}, f32[32]{0:T(128)}, u32[]{:S(2)}) copy-start(f32[32]{0:T(128)} %param.15) | copy-start | bytes 388
  23.2 49.7 %all-to-all-start = ((f32[512,1,256]{2,1,0:T(1,128)}), f32[512,1,256]{2,1,0:T(1,128)}, u32[]{:S(2)}, u32[]{:S(2)}) async-start(f32[512,1,256]{2,1,0:T(1,128)} %copy.13), calls=%async_computation | async-start | bytes 1048576 | tf_op jit(solution)/shard_map/all_to_all | solution.py:526
  46.7 16.4 %collective-permute-start = (f32[504,128]{1,0:T(8,128)}, f32[504,128]{1,0:T(8,128)S(1)}, u32[]{:S(2)}, u32[]{:S(2)}) collective-permute-start(f32[504,128]{1,0:T(8,128)} %get-tuple-element.14), channel_id=1, source_target_pairs={{0,1},{1,2},{2,3},{3,4},{4,5},{5,6},{6,7},{7,0},{8,9},{9,10},{10,1... | collective-permute-start | bytes 774152 | tf_op jit(solution)/shard_map/ppermute | solution.py:326
  50.1 17.1 %collective-permute-start.4 = (f32[504,128]{1,0:T(8,128)}, f32[504,128]{1,0:T(8,128)S(1)}, u32[]{:S(2)}, u32[]{:S(2)}) collective-permute-start(f32[504,128]{1,0:T(8,128)} %get-tuple-element.16), channel_id=1, source_target_pairs={{0,7},{1,0},{2,1},{3,2},{4,3},{5,4},{6,5},{7,6},{8,15},{9,8},{10,9... | collective-permute-start | bytes 774152 | tf_op jit(solution)/shard_map/ppermute | solution.py:326
  54.2 18.6 %collective-permute-start.6 = (f32[504,128]{1,0:T(8,128)}, f32[504,128]{1,0:T(8,128)S(1)}, u32[]{:S(2)}, u32[]{:S(2)}) collective-permute-start(f32[504,128]{1,0:T(8,128)} %slice.18), channel_id=1, source_target_pairs={{0,7},{1,0},{2,1},{3,2},{4,3},{5,4},{6,5},{7,6},{8,15},{9,8},{10,9... | collective-permute-start | bytes 774152 | tf_op jit(solution)/shard_map/ppermute | solution.py:326
  57.6 15.2 %collective-permute-start.2 = (f32[504,128]{1,0:T(8,128)S(1)}, f32[504,128]{1,0:T(8,128)S(1)}, u32[]{:S(2)}, u32[]{:S(2)}) collective-permute-start(f32[504,128]{1,0:T(8,128)S(1)} %slice.16), channel_id=1, source_target_pairs={{0,1},{1,2},{2,3},{3,4},{4,5},{5,6},{6,7},{7,0},{8,9},{9,10},{10,1... | collective-permute-start | bytes 774152 | tf_op jit(solution)/shard_map/ppermute | solution.py:326
  59.6 13.3 %collective-permute-start.3 = (f32[256,128]{1,0:T(8,128)S(1)}, f32[256,128]{1,0:T(8,128)S(1)}, u32[]{:S(2)}, u32[]{:S(2)}) collective-permute-start(f32[256,128]{1,0:T(8,128)S(1)} %slice.17), channel_id=1, source_target_pairs={{0,2},{1,3},{2,4},{3,5},{4,6},{5,7},{6,0},{7,1},{8,10},{9,11},{10,... | collective-permute-start | bytes 393224 | tf_op jit(solution)/shard_map/ppermute | solution.py:326
  63.1 9.7 %collective-permute-start.7 = (f32[248,128]{1,0:T(8,128)S(1)}, f32[248,128]{1,0:T(8,128)S(1)}, u32[]{:S(2)}, u32[]{:S(2)}) collective-permute-start(f32[248,128]{1,0:T(8,128)S(1)} %slice.19), channel_id=1, source_target_pairs={{0,6},{1,7},{2,0},{3,1},{4,2},{5,3},{6,4},{7,5},{8,14},{9,15},{10,... | collective-permute-start | bytes 380936 | tf_op jit(solution)/shard_map/ppermute | solution.py:326
  67.1 6.9 %copy-start.1 = (f32[32,32]{1,0:T(8,128)S(1)}, f32[32,32]{1,0:T(8,128)}, u32[]{:S(2)}) copy-start(f32[32,32]{1,0:T(8,128)} %to_ref.1) | copy-start | bytes 12292
  67.1 6.9 %copy-start.2 = (f32[32,32]{1,0:T(8,128)S(1)}, f32[32,32]{1,0:T(8,128)}, u32[]{:S(2)}) copy-start(f32[32,32]{1,0:T(8,128)} %from_ref.1) | copy-start | bytes 12292

commit v5 on v4

--- a/solution.py
+++ b/solution.py
@@ -327,11 +327,13 @@
 
 
 def ring(up1, down1, up2, down2):
-    up2, down2 = shift(up2, 2), shift(down2, -2)
-    up1, down1 = shift(up1, 1), shift(down1, -1)
-    up3, down3 = shift(up2[LMSG : 2 * LMSG], 1), shift(down2[LMSG : 2 * LMSG], -1)
-    up4, down4 = shift(up2[2 * LMSG :], 2), shift(down2[2 * LMSG :], -2)
-    return up1, up2, up3, up4, down1, down2, down3, down4
+    far = shift(up2, 2), shift(down2, -2)
+    third = (
+        shift(jnp.concatenate([far[0][LMSG : 2 * LMSG], up1]), 1),
+        shift(jnp.concatenate([far[1][LMSG : 2 * LMSG], down1]), -1),
+    )
+    fourth = shift(far[0][2 * LMSG :], 2), shift(far[1][2 * LMSG :], -2)
+    return far, third, fourth
 
 
 def mode_matrices(to_modes, from_modes):
@@ -495,7 +497,8 @@
     smem = pl.BlockSpec(memory_space=pltpu.SMEM)
     vmem = pl.BlockSpec(memory_space=pltpu.VMEM)
     taken = [
-        pl.BlockSpec((min(LMSG, x.shape[0]), 128), lambda i: (0, 0)) for x in args[8:]
+        pl.BlockSpec((min(LMSG, x.shape[0]), 128), lambda i, place=place: (place, 0))
+        for x, place in zip(args[8:], (1, 0, 0, 0) * 2)
     ]
     return pl.pallas_call(
         legendre_kernel,
@@ -520,8 +523,9 @@
     me = jnp.stack([lax.axis_index("fld"), lax.axis_index("lat")]).astype(jnp.int32)
     own, *messages = pack(me, legendre, gauss_weights)
     waves, own = lax.optimization_barrier((waves, own))
-    moved = ring(*messages)
-    zero = arrival(moved)
+    far, third, fourth = ring(*messages)
+    zero = arrival([*far, *third, *fourth])
+    moved = [x for way in zip(third, far, third, fourth) for x in way]
     fourier = forward(row_points, waves, grid)
     coeffs = lax.all_to_all(fourier, ("fld", "lat"), 0, 0, tiled=True)
     depths = mode_depths.reshape(LEVELS, 1)

time: 131 us -> 129 us (0.985)
  starting transfers between devices: 51.6 us -> 45.1 us
  waiting for transfers between devices: 5.77 us -> 8.14 us
  local copies, waits for them, and re-layouts: 6.37 us -> 8.17 us
    all_to_all x1, waiting for transfers between devices: 0.01 us -> 6.34 us  [body(): coeffs = lax.all_to_all(fourier, ('fld', 'lat'), 0, 0, tiled=True)]
    ppermute x8 -> x6, starting transfers between devices: 28 us -> 22.7 us  [shift(): return lax.ppermute(x, 'fld', [(i, (i + step) % FLD) for i in range(FLD)])]
    ppermute x8 -> x6, waiting for transfers between devices: 5.77 us -> 1.8 us  [shift(): return lax.ppermute(x, 'fld', [(i, (i + step) % FLD) for i in range(FLD)])]
  transfers between devices with their start and end apart: 9 -> 7, of which waited for: 1 -> 3; matrix products, arithmetic and copies ran while one was open for 2% -> 4% of each run, Pallas kernels for 6% -> 6%
where the time goes in v5:
time: 129 us; the launch traced here: 128 us
  starting transfers between devices  45.1 us (35%)
  blocking collectives  41.9 us (32%)
  Pallas kernels  23.8 us (18%)
  local copies, waits for them, and re-layouts  8.17 us (6%)
  waiting for transfers between devices  8.14 us (6%)
    all_to_all x1, blocking collectives, body(): back = lax.all_to_all(synthesis, ('fld', 'lat'), 0, 0, tiled=True)  41.9 us
    ppermute x6, starting transfers between devices, shift(): return lax.ppermute(x, 'fld', [(i, (i + step) % FLD) for i in range(FLD)])  22.7 us
    all_to_all x1, starting transfers between devices, body(): coeffs = lax.all_to_all(fourier, ('fld', 'lat'), 0, 0, tiled=True)  22.4 us
    pallas_call x1, Pallas kernels, inverse(): pl.pallas_call(inverse_kernel, grid=(ROWS,), in_specs=[pl.BlockSpec(memor...  9.49 us
    pallas_call x1, Pallas kernels, forward(): pl.pallas_call(forward_kernel, grid=(ROWS,), in_specs=[pl.BlockSpec(memor...  7.34 us
    all_to_all x1, waiting for transfers between devices, body(): coeffs = lax.all_to_all(fourier, ('fld', 'lat'), 0, 0, tiled=True)  6.34 us
    unnamed x18, local copies, waits for them, and re-layouts  4.54 us
    pallas_call x1, Pallas kernels, legendre_round(): pl.pallas_call(legendre_kernel, grid=(1,), in_specs=[smem, smem] + [vmem]...  3.98 us
  transfers between devices with their start and end apart: 7, of which 3 were waited for; matrix products, arithmetic and copies ran while one was open for 4% of the time, Pallas kernels for 6%

profile of v5, /device:TPU:1, one launch (start us, length us, event | category | flops | bytes accessed | tf_op | source)
XLA Modules:
  0.0 128.3 jit_solution(17048089043781919347)
XLA Ops:
  0.0 0.0 copy-start.3
  0.0 0.0 copy-start.5
  0.0 0.1 pad_add_fusion.me_ref
  0.1 0.0 copy-start
  0.1 1.6 %copy-done = f32[10,80,640]{2,1,0:T(8,128)S(1)} copy-done((f32[10,80,640]{2,1,0:T(8,128)S(1)}, f32[10,80,640]{2,1,0:T(8,128)}, u32[]{:S(2)}) %copy-start) | copy-done | bytes 2048024
  1.7 0.0 copy-start.4
  1.7 0.7 copy-done.4
  2.3 3.0 %pack_legendre.1 = (f32[504,128]{1,0:T(8,128)S(1)}, f32[504,128]{1,0:T(8,128)S(1)}, f32[504,128]{1,0:T(8,128)S(1)}, f32[1264,128]{1,0:T(8,128)S(1)}, f32[1256,128]{1,0:T(8,128)}) custom-call(s32[2]{0:T(128)S(1)} %pad_add_fusion.me_ref, f32[10,80,640]{2,1,0:T(8,128)S(1)} %copy-done, f32[1,80]{1,0:T(1,128)S(1)} %bitcast.17), custom_call_target="tpu_custom_call" | custom-call | tf_op jit(solution)/shard_map/pack_legendre/pallas_call | solution.py:311
  5.3 6.7 %collective-permute-start.1 = (f32[1256,128]{1,0:T(8,128)}, f32[1256,128]{1,0:T(8,128)S(1)}, u32[]{:S(2)}, u32[]{:S(2)}) collective-permute-start(f32[1256,128]{1,0:T(8,128)} %get-tuple-element.15), channel_id=1, source_target_pairs={{0,6},{1,7},{2,0},{3,1},{4,2},{5,3},{6,4},{7,5},{8,14},{9,15},{10,... | collective-permute-start | bytes 1929224 | tf_op jit(solution)/shard_map/ppermute | solution.py:326
  12.1 1.9 %collective-permute-start = (f32[1264,128]{1,0:T(8,128)S(1)}, f32[1264,128]{1,0:T(8,128)S(1)}, u32[]{:S(2)}, u32[]{:S(2)}) collective-permute-start(f32[1264,128]{1,0:T(8,128)S(1)} %get-tuple-element.14), channel_id=1, source_target_pairs={{0,2},{1,3},{2,4},{3,5},{4,6},{5,7},{6,0},{7,1},{8,10},{9,11},{10,... | collective-permute-start | bytes 1941512 | tf_op jit(solution)/shard_map/ppermute | solution.py:326
  14.0 0.0 copy-done.3
  14.0 0.1 convert_element_type.21
  14.1 0.1 copy.12
  14.2 0.1 convert_element_type.23.waves_ref
  14.3 0.0 copy-done.5
  14.3 0.0 copy-start.6
  14.3 1.2 copy-done.6
  15.5 7.3 %forward_fourier.1 = f32[512,256]{1,0:T(8,128)S(1)} custom-call(s32[10]{0:T(128)S(1)} %copy-done.5, f32[1,640]{1,0:T(1,128)S(1)} %convert_element_type.23.waves_ref, f32[2,10,4,2688]{3,2,1,0:T(4,128)S(1)} %copy-done.6), custom_call_target="tpu_custom_call" | custom-call | flops 3000000000 | bytes 2000000 | tf_op jit(solution)/shard_map/forward_fourier/pallas_call | solution.py:142
  22.8 1.3 %copy.13 = f32[512,1,256]{2,1,0:T(1,128)} copy(f32[512,1,256]{2,0,1:T(8,128)S(1)} %bitcast.16) | data formatting | bytes 1048576 | tf_op jit(solution)/shard_map/all_to_all | solution.py:530
  24.2 22.4 %all-to-all-start = ((f32[512,1,256]{2,1,0:T(1,128)}), f32[512,1,256]{2,1,0:T(1,128)}, u32[]{:S(2)}, u32[]{:S(2)}) async-start(f32[512,1,256]{2,1,0:T(1,128)} %copy.13), calls=%async_computation | async-start | bytes 1048576 | tf_op jit(solution)/shard_map/all_to_all | solution.py:530
  46.5 0.0 copy-start.7
  46.5 0.0 collective-permute-done.1.refs_1_.refs_6_
  46.6 4.8 %collective-permute-start.3 = (f32[1008,128]{1,0:T(8,128)S(1)}, f32[1008,128]{1,0:T(8,128)S(1)}, u32[]{:S(2)}, u32[]{:S(2)}) collective-permute-start(f32[1008,128]{1,0:T(8,128)S(1)} %pad_maximum_fusion.1), channel_id=1, source_target_pairs={{0,7},{1,0},{2,1},{3,2},{4,3},{5,4},{6,5},{7,6},{8,15},{9,8},{10,9... | collective-permute-start | bytes 1548296 | tf_op jit(solution)/shard_map/ppermute | solution.py:326
  51.4 0.0 collective-permute-done.refs_0_.refs_2_
  51.5 0.8 pad_maximum_fusion
  52.3 1.9 %collective-permute-start.2 = (f32[1008,128]{1,0:T(8,128)}, f32[1008,128]{1,0:T(8,128)S(1)}, u32[]{:S(2)}, u32[]{:S(2)}) collective-permute-start(f32[1008,128]{1,0:T(8,128)} %pad_maximum_fusion), channel_id=1, source_target_pairs={{0,1},{1,2},{2,3},{3,4},{4,5},{5,6},{6,7},{7,0},{8,9},{9,10},{10,1... | collective-permute-start | bytes 1548296 | tf_op jit(solution)/shard_map/ppermute | solution.py:326
  54.2 0.7 slice.18
  54.9 2.7 %collective-permute-start.4 = (f32[256,128]{1,0:T(8,128)}, f32[256,128]{1,0:T(8,128)S(1)}, u32[]{:S(2)}, u32[]{:S(2)}) collective-permute-start(f32[256,128]{1,0:T(8,128)} %slice.18), channel_id=1, source_target_pairs={{0,2},{1,3},{2,4},{3,5},{4,6},{5,7},{6,0},{7,1},{8,10},{9,11},{10,... | collective-permute-start | bytes 393224 | tf_op jit(solution)/shard_map/ppermute | solution.py:326
  57.6 0.7 slice.19
  58.3 4.6 %collective-permute-start.5 = (f32[248,128]{1,0:T(8,128)}, f32[248,128]{1,0:T(8,128)S(1)}, u32[]{:S(2)}, u32[]{:S(2)}) collective-permute-start(f32[248,128]{1,0:T(8,128)} %slice.19), channel_id=1, source_target_pairs={{0,6},{1,7},{2,0},{3,1},{4,2},{5,3},{6,4},{7,5},{8,14},{9,15},{10,... | collective-permute-start | bytes 380936 | tf_op jit(solution)/shard_map/ppermute | solution.py:326
  62.9 0.0 copy-done.7
  63.0 0.1 copy.14.depth_ref
  63.0 6.3 %all-to-all-done = f32[512,1,256]{2,1,0:T(1,128)} async-done(((f32[512,1,256]{2,1,0:T(1,128)}), f32[512,1,256]{2,1,0:T(1,128)}, u32[]{:S(2)}, u32[]{:S(2)}) %all-to-all-start) | async-done | bytes 524320 | tf_op jit(solution)/shard_map/all_to_all | solution.py:530
  69.4 1.1 copy.21
  70.5 0.0 copy-start.1
  70.5 0.0 copy-start.2
  70.5 1.6 %collective-permute-done.5.refs_5_.refs_8_ = f32[248,128]{1,0:T(8,128)S(1)} collective-permute-done((f32[248,128]{1,0:T(8,128)}, f32[248,128]{1,0:T(8,128)S(1)}, u32[]{:S(2)}, u32[]{:S(2)}) %collective-permute-start.5) | collective-permute-done | bytes 127008 | tf_op jit(solution)/shard_map/ppermute | solution.py:326
  72.1 0.2 collective-permute-done.4.refs_4_
  72.3 0.0 collective-permute-done.3.refs_3_.refs_5_.refs_7_
  72.3 0.0 collective-permute-done.2.refs_2_.refs_1_.refs_3_
  72.3 0.0 copy-done.1
  72.3 0.0 copy-done.2
  72.3 4.0 %legendre_round.1 = f32[512,256]{1,0:T(8,128)S(1)} custom-call(s32[2]{0:T(128)S(1)} %pad_add_fusion.me_ref, s32[640]{0:T(1024)S(1)} %copy-done.3, f32[512,256]{1,0:T(8,128)S(1)} %bitcast.13, f32[32,32]{1,0:T(8,128)S(1)} %copy-done.1, f32[32,32]{1,0:T(8,128)S(1)} %copy-done.2, f32[32,1]{1,0:T(8,128)S(1)} %copy.14.depth_ref, f32[8,128]{1,0:T(8,128)S(1)} %arrival.1.zero_ref, ...), custom_call_target="tpu_custom_call" | custom-call | tf_op jit(solution)/shard_map/legendre_round/pallas_call | solution.py:503
  76.3 0.5 copy.15
  76.8 41.9 %all_to_all.22 = f32[512,1,256]{2,1,0:T(1,128)S(1)} all-to-all(f32[512,1,256]{2,1,0:T(1,128)S(1)} %copy.15), channel_id=1, replica_groups=mesh['lat'=64,'fld'=8] {'fld','lat'}, dimensions={0} | all-to-all | bytes 1048576 | tf_op jit(solution)/shard_map/all_to_all | solution.py:535
  118.8 9.5 %inverse_fourier.1 = f32[2,10,4,2688]{3,2,1,0:T(4,128)} custom-call(s32[10]{0:T(128)S(1)} %copy-done.5, f32[1,640]{1,0:T(1,128)S(1)} %convert_element_type.23.waves_ref, f32[512,256]{1,0:T(8,128)S(1)} %bitcast.15), custom_call_target="tpu_custom_call" | custom-call | tf_op jit(solution)/shard_map/inverse_fourier/pallas_call | solution.py:221
  (6 shorter events, 0.1 us)
Async XLA Ops:
  0.0 14.0 %copy-start.3 = (s32[640]{0:T(1024)S(1)}, s32[640]{0:T(1024)}, u32[]{:S(2)}) copy-start(s32[640]{0:T(1024)} %assignment_ref.1) | copy-start | bytes 7684
  0.0 14.3 %copy-start.5 = (s32[10]{0:T(128)S(1)}, s32[10]{0:T(128)}, u32[]{:S(2)}) copy-start(s32[10]{0:T(128)} %points_ref.3) | copy-start | bytes 124
  0.1 1.6 %copy-start = (f32[10,80,640]{2,1,0:T(8,128)S(1)}, f32[10,80,640]{2,1,0:T(8,128)}, u32[]{:S(2)}) copy-start(f32[10,80,640]{2,1,0:T(8,128)} %legendre_ref.1) | copy-start | bytes 6144004
  1.7 0.7 copy-start.4
  5.3 41.2 %collective-permute-start.1 = (f32[1256,128]{1,0:T(8,128)}, f32[1256,128]{1,0:T(8,128)S(1)}, u32[]{:S(2)}, u32[]{:S(2)}) collective-permute-start(f32[1256,128]{1,0:T(8,128)} %get-tuple-element.15), channel_id=1, source_target_pairs={{0,6},{1,7},{2,0},{3,1},{4,2},{5,3},{6,4},{7,5},{8,14},{9,15},{10,... | collective-permute-start | bytes 1929224 | tf_op jit(solution)/shard_map/ppermute | solution.py:326
  12.1 39.4 %collective-permute-start = (f32[1264,128]{1,0:T(8,128)S(1)}, f32[1264,128]{1,0:T(8,128)S(1)}, u32[]{:S(2)}, u32[]{:S(2)}) collective-permute-start(f32[1264,128]{1,0:T(8,128)S(1)} %get-tuple-element.14), channel_id=1, source_target_pairs={{0,2},{1,3},{2,4},{3,5},{4,6},{5,7},{6,0},{7,1},{8,10},{9,11},{10,... | collective-permute-start | bytes 1941512 | tf_op jit(solution)/shard_map/ppermute | solution.py:326
  14.3 1.2 copy-start.6
  24.2 45.2 %all-to-all-start = ((f32[512,1,256]{2,1,0:T(1,128)}), f32[512,1,256]{2,1,0:T(1,128)}, u32[]{:S(2)}, u32[]{:S(2)}) async-start(f32[512,1,256]{2,1,0:T(1,128)} %copy.13), calls=%async_computation | async-start | bytes 1048576 | tf_op jit(solution)/shard_map/all_to_all | solution.py:530
  46.5 16.4 %copy-start.7 = (f32[32]{0:T(128)S(1)}, f32[32]{0:T(128)}, u32[]{:S(2)}) copy-start(f32[32]{0:T(128)} %param.15) | copy-start | bytes 388
  46.6 25.7 %collective-permute-start.3 = (f32[1008,128]{1,0:T(8,128)S(1)}, f32[1008,128]{1,0:T(8,128)S(1)}, u32[]{:S(2)}, u32[]{:S(2)}) collective-permute-start(f32[1008,128]{1,0:T(8,128)S(1)} %pad_maximum_fusion.1), channel_id=1, source_target_pairs={{0,7},{1,0},{2,1},{3,2},{4,3},{5,4},{6,5},{7,6},{8,15},{9,8},{10,9... | collective-permute-start | bytes 1548296 | tf_op jit(solution)/shard_map/ppermute | solution.py:326
  52.3 20.0 %collective-permute-start.2 = (f32[1008,128]{1,0:T(8,128)}, f32[1008,128]{1,0:T(8,128)S(1)}, u32[]{:S(2)}, u32[]{:S(2)}) collective-permute-start(f32[1008,128]{1,0:T(8,128)} %pad_maximum_fusion), channel_id=1, source_target_pairs={{0,1},{1,2},{2,3},{3,4},{4,5},{5,6},{6,7},{7,0},{8,9},{9,10},{10,1... | collective-permute-start | bytes 1548296 | tf_op jit(solution)/shard_map/ppermute | solution.py:326
  54.9 17.4 %collective-permute-start.4 = (f32[256,128]{1,0:T(8,128)}, f32[256,128]{1,0:T(8,128)S(1)}, u32[]{:S(2)}, u32[]{:S(2)}) collective-permute-start(f32[256,128]{1,0:T(8,128)} %slice.18), channel_id=1, source_target_pairs={{0,2},{1,3},{2,4},{3,5},{4,6},{5,7},{6,0},{7,1},{8,10},{9,11},{10,... | collective-permute-start | bytes 393224 | tf_op jit(solution)/shard_map/ppermute | solution.py:326
  58.3 13.8 %collective-permute-start.5 = (f32[248,128]{1,0:T(8,128)}, f32[248,128]{1,0:T(8,128)S(1)}, u32[]{:S(2)}, u32[]{:S(2)}) collective-permute-start(f32[248,128]{1,0:T(8,128)} %slice.19), channel_id=1, source_target_pairs={{0,6},{1,7},{2,0},{3,1},{4,2},{5,3},{6,4},{7,5},{8,14},{9,15},{10,... | collective-permute-start | bytes 380936 | tf_op jit(solution)/shard_map/ppermute | solution.py:326
  70.5 1.8 %copy-start.1 = (f32[32,32]{1,0:T(8,128)S(1)}, f32[32,32]{1,0:T(8,128)}, u32[]{:S(2)}) copy-start(f32[32,32]{1,0:T(8,128)} %to_ref.1) | copy-start | bytes 12292
  70.5 1.8 %copy-start.2 = (f32[32,32]{1,0:T(8,128)S(1)}, f32[32,32]{1,0:T(8,128)}, u32[]{:S(2)}) copy-start(f32[32,32]{1,0:T(8,128)} %from_ref.1) | copy-start | bytes 12292

commit v6 on v5

--- a/solution.py
+++ b/solution.py
@@ -33,6 +33,7 @@
 WLANE = 64
 FIRST = 256
 VMEM = 20 << 20
+FORWARD_VMEM = 56 << 20
 ROUND_VMEM = 48 << 20
 TRAVEL_COST = 5_000_000_000
 
@@ -153,7 +154,7 @@
             pltpu.VMEM((128, 2 * WAVES), F32),
             pltpu.VMEM((MSG, WAVES), F32),
         ],
-        compiler_params=pltpu.CompilerParams(vmem_limit_bytes=VMEM),
+        compiler_params=pltpu.CompilerParams(vmem_limit_bytes=FORWARD_VMEM),
         cost_estimate=pl.CostEstimate(
             flops=3_000_000_000, bytes_accessed=2_000_000, transcendentals=0
         ),

time: 129 us -> 131 us (1.016)
  Pallas kernels: 23.8 us -> 25.9 us
    pallas_call x1, Pallas kernels: 7.34 us -> 9.43 us  [forward(): pl.pallas_call(forward_kernel, grid=(ROWS,), in_specs=[pl.BlockSpec(memor...]
    ppermute x6, waiting for transfers between devices: 1.8 us -> 3.84 us  [shift(): return lax.ppermute(x, 'fld', [(i, (i + step) % FLD) for i in range(FLD)])]
    all_to_all x1, waiting for transfers between devices: 6.34 us -> 4.38 us  [body(): coeffs = lax.all_to_all(fourier, ('fld', 'lat'), 0, 0, tiled=True)]
  transfers between devices with their start and end apart: 7 -> 7, of which waited for: 3 -> 3; matrix products, arithmetic and copies ran while one was open for 4% -> 5% of each run, Pallas kernels for 6% -> 7%
where the time goes in v6:
time: 131 us
  starting transfers between devices  45.1 us (34%)
  blocking collectives  41.5 us (32%)
  Pallas kernels  25.9 us (20%)
  local copies, waits for them, and re-layouts  8.63 us (7%)
  waiting for transfers between devices  8.23 us (6%)
    all_to_all x1, blocking collectives, body(): back = lax.all_to_all(synthesis, ('fld', 'lat'), 0, 0, tiled=True)  41.5 us
    ppermute x6, starting transfers between devices, shift(): return lax.ppermute(x, 'fld', [(i, (i + step) % FLD) for i in range(FLD)])  22.7 us
    all_to_all x1, starting transfers between devices, body(): coeffs = lax.all_to_all(fourier, ('fld', 'lat'), 0, 0, tiled=True)  22.3 us
    pallas_call x1, Pallas kernels, inverse(): pl.pallas_call(inverse_kernel, grid=(ROWS,), in_specs=[pl.BlockSpec(memor...  9.49 us
    pallas_call x1, Pallas kernels, forward(): pl.pallas_call(forward_kernel, grid=(ROWS,), in_specs=[pl.BlockSpec(memor...  9.43 us
    all_to_all x1, waiting for transfers between devices, body(): coeffs = lax.all_to_all(fourier, ('fld', 'lat'), 0, 0, tiled=True)  4.38 us
    pallas_call x1, Pallas kernels, legendre_round(): pl.pallas_call(legendre_kernel, grid=(1,), in_specs=[smem, smem] + [vmem]...  3.96 us
    ppermute x6, waiting for transfers between devices, shift(): return lax.ppermute(x, 'fld', [(i, (i + step) % FLD) for i in range(FLD)])  3.84 us
  transfers between devices with their start and end apart: 7, of which 3 were waited for; matrix products, arithmetic and copies ran while one was open for 5% of the time, Pallas kernels for 7%

profile of v6, /device:TPU:1, one launch (start us, length us, event | category | flops | bytes accessed | tf_op | source)
XLA Modules:
  0.0 130.5 jit_solution(3300794021805583349)
XLA Ops:
  0.0 0.0 copy-start.3
  0.0 0.1 pad_add_fusion.me_ref
  0.1 0.0 copy-start
  0.1 1.6 %copy-done = f32[10,80,640]{2,1,0:T(8,128)S(1)} copy-done((f32[10,80,640]{2,1,0:T(8,128)S(1)}, f32[10,80,640]{2,1,0:T(8,128)}, u32[]{:S(2)}) %copy-start) | copy-done | bytes 2048024
  1.7 0.0 copy-start.5
  1.7 0.7 copy-done.5
  2.3 3.0 %pack_legendre.1 = (f32[504,128]{1,0:T(8,128)S(1)}, f32[504,128]{1,0:T(8,128)S(1)}, f32[504,128]{1,0:T(8,128)S(1)}, f32[1264,128]{1,0:T(8,128)S(1)}, f32[1256,128]{1,0:T(8,128)}) custom-call(s32[2]{0:T(128)S(1)} %pad_add_fusion.me_ref, f32[10,80,640]{2,1,0:T(8,128)S(1)} %copy-done, f32[1,80]{1,0:T(1,128)S(1)} %bitcast.16), custom_call_target="tpu_custom_call" | custom-call | tf_op jit(solution)/shard_map/pack_legendre/pallas_call | solution.py:312
  5.3 6.7 %collective-permute-start.1 = (f32[1256,128]{1,0:T(8,128)}, f32[1256,128]{1,0:T(8,128)S(1)}, u32[]{:S(2)}, u32[]{:S(2)}) collective-permute-start(f32[1256,128]{1,0:T(8,128)} %get-tuple-element.15), channel_id=1, source_target_pairs={{0,6},{1,7},{2,0},{3,1},{4,2},{5,3},{6,4},{7,5},{8,14},{9,15},{10,... | collective-permute-start | bytes 1929224 | tf_op jit(solution)/shard_map/ppermute | solution.py:327
  12.0 1.9 %collective-permute-start = (f32[1264,128]{1,0:T(8,128)S(1)}, f32[1264,128]{1,0:T(8,128)S(1)}, u32[]{:S(2)}, u32[]{:S(2)}) collective-permute-start(f32[1264,128]{1,0:T(8,128)S(1)} %get-tuple-element.14), channel_id=1, source_target_pairs={{0,2},{1,3},{2,4},{3,5},{4,6},{5,7},{6,0},{7,1},{8,10},{9,11},{10,... | collective-permute-start | bytes 1941512 | tf_op jit(solution)/shard_map/ppermute | solution.py:327
  14.0 0.0 copy-done.3
  14.0 0.1 convert_element_type.21
  14.1 0.1 copy.12
  14.2 0.7 convert_element_type.23.waves_ref
  14.9 9.4 %forward_fourier.1 = f32[512,256]{1,0:T(8,128)} custom-call(s32[10]{0:T(128)} %points_ref.3, f32[1,640]{1,0:T(1,128)} %convert_element_type.23.waves_ref, f32[2,10,4,2688]{3,2,1,0:T(4,128)} %grid_ref.1), custom_call_target="tpu_custom_call" | custom-call | flops 3000000000 | bytes 2000000 | tf_op jit(solution)/shard_map/forward_fourier/pallas_call | solution.py:143
  24.3 2.4 %copy.13 = f32[512,1,256]{2,1,0:T(1,128)} copy(f32[512,1,256]{2,0,1:T(8,128)} %bitcast.17) | data formatting | bytes 1048576 | tf_op jit(solution)/shard_map/all_to_all | solution.py:531
  26.7 22.3 %all-to-all-start = ((f32[512,1,256]{2,1,0:T(1,128)}), f32[512,1,256]{2,1,0:T(1,128)}, u32[]{:S(2)}, u32[]{:S(2)}) async-start(f32[512,1,256]{2,1,0:T(1,128)} %copy.13), calls=%async_computation | async-start | bytes 1048576 | tf_op jit(solution)/shard_map/all_to_all | solution.py:531
  49.0 0.0 copy-start.7
  49.0 0.0 collective-permute-done.1.refs_1_.refs_6_
  49.1 4.8 %collective-permute-start.3 = (f32[1008,128]{1,0:T(8,128)S(1)}, f32[1008,128]{1,0:T(8,128)S(1)}, u32[]{:S(2)}, u32[]{:S(2)}) collective-permute-start(f32[1008,128]{1,0:T(8,128)S(1)} %pad_maximum_fusion.1), channel_id=1, source_target_pairs={{0,7},{1,0},{2,1},{3,2},{4,3},{5,4},{6,5},{7,6},{8,15},{9,8},{10,9... | collective-permute-start | bytes 1548296 | tf_op jit(solution)/shard_map/ppermute | solution.py:327
  54.0 0.0 collective-permute-done.refs_0_.refs_2_
  54.0 0.8 pad_maximum_fusion
  54.8 1.9 %collective-permute-start.2 = (f32[1008,128]{1,0:T(8,128)}, f32[1008,128]{1,0:T(8,128)S(1)}, u32[]{:S(2)}, u32[]{:S(2)}) collective-permute-start(f32[1008,128]{1,0:T(8,128)} %pad_maximum_fusion), channel_id=1, source_target_pairs={{0,1},{1,2},{2,3},{3,4},{4,5},{5,6},{6,7},{7,0},{8,9},{9,10},{10,1... | collective-permute-start | bytes 1548296 | tf_op jit(solution)/shard_map/ppermute | solution.py:327
  56.7 0.7 slice.18
  57.4 2.7 %collective-permute-start.4 = (f32[256,128]{1,0:T(8,128)}, f32[256,128]{1,0:T(8,128)S(1)}, u32[]{:S(2)}, u32[]{:S(2)}) collective-permute-start(f32[256,128]{1,0:T(8,128)} %slice.18), channel_id=1, source_target_pairs={{0,2},{1,3},{2,4},{3,5},{4,6},{5,7},{6,0},{7,1},{8,10},{9,11},{10,... | collective-permute-start | bytes 393224 | tf_op jit(solution)/shard_map/ppermute | solution.py:327
  60.1 0.7 slice.19
  60.8 4.6 %collective-permute-start.5 = (f32[248,128]{1,0:T(8,128)}, f32[248,128]{1,0:T(8,128)S(1)}, u32[]{:S(2)}, u32[]{:S(2)}) collective-permute-start(f32[248,128]{1,0:T(8,128)} %slice.19), channel_id=1, source_target_pairs={{0,6},{1,7},{2,0},{3,1},{4,2},{5,3},{6,4},{7,5},{8,14},{9,15},{10,... | collective-permute-start | bytes 380936 | tf_op jit(solution)/shard_map/ppermute | solution.py:327
  65.5 0.0 copy-done.7
  65.5 0.1 copy.14.depth_ref
  65.6 4.4 %all-to-all-done = f32[512,1,256]{2,1,0:T(1,128)} async-done(((f32[512,1,256]{2,1,0:T(1,128)}), f32[512,1,256]{2,1,0:T(1,128)}, u32[]{:S(2)}, u32[]{:S(2)}) %all-to-all-start) | async-done | bytes 524320 | tf_op jit(solution)/shard_map/all_to_all | solution.py:531
  69.9 1.1 copy.21
  71.0 0.0 copy-start.1
  71.0 0.0 copy-start.2
  71.0 3.6 %collective-permute-done.5.refs_5_.refs_8_ = f32[248,128]{1,0:T(8,128)S(1)} collective-permute-done((f32[248,128]{1,0:T(8,128)}, f32[248,128]{1,0:T(8,128)S(1)}, u32[]{:S(2)}, u32[]{:S(2)}) %collective-permute-start.5) | collective-permute-done | bytes 127008 | tf_op jit(solution)/shard_map/ppermute | solution.py:327
  74.6 0.3 collective-permute-done.4.refs_4_
  74.9 0.0 collective-permute-done.3.refs_3_.refs_5_.refs_7_
  74.9 0.0 collective-permute-done.2.refs_2_.refs_1_.refs_3_
  74.9 0.0 copy-done.1
  74.9 0.0 copy-done.2
  74.9 4.0 %legendre_round.1 = f32[512,256]{1,0:T(8,128)S(1)} custom-call(s32[2]{0:T(128)S(1)} %pad_add_fusion.me_ref, s32[640]{0:T(1024)S(1)} %copy-done.3, f32[512,256]{1,0:T(8,128)S(1)} %bitcast.13, f32[32,32]{1,0:T(8,128)S(1)} %copy-done.1, f32[32,32]{1,0:T(8,128)S(1)} %copy-done.2, f32[32,1]{1,0:T(8,128)S(1)} %copy.14.depth_ref, f32[8,128]{1,0:T(8,128)S(1)} %arrival.1.zero_ref, ...), custom_call_target="tpu_custom_call" | custom-call | tf_op jit(solution)/shard_map/legendre_round/pallas_call | solution.py:504
  78.9 0.0 copy-start.4
  78.9 0.0 copy-start.6
  78.9 0.5 copy.15
  79.5 41.5 %all_to_all.22 = f32[512,1,256]{2,1,0:T(1,128)S(1)} all-to-all(f32[512,1,256]{2,1,0:T(1,128)S(1)} %copy.15), channel_id=1, replica_groups=mesh['lat'=64,'fld'=8] {'fld','lat'}, dimensions={0} | all-to-all | bytes 1048576 | tf_op jit(solution)/shard_map/all_to_all | solution.py:536
  121.0 0.0 copy-done.4
  121.0 0.0 copy-done.6
  121.0 9.5 %inverse_fourier.1 = f32[2,10,4,2688]{3,2,1,0:T(4,128)} custom-call(s32[10]{0:T(128)S(1)} %copy-done.6, f32[1,640]{1,0:T(1,128)S(1)} %copy-done.4, f32[512,256]{1,0:T(8,128)S(1)} %bitcast.15), custom_call_target="tpu_custom_call" | custom-call | tf_op jit(solution)/shard_map/inverse_fourier/pallas_call | solution.py:222
  (6 shorter events, 0.1 us)
Async XLA Ops:
  0.0 14.0 %copy-start.3 = (s32[640]{0:T(1024)S(1)}, s32[640]{0:T(1024)}, u32[]{:S(2)}) copy-start(s32[640]{0:T(1024)} %assignment_ref.1) | copy-start | bytes 7684
  0.1 1.6 %copy-start = (f32[10,80,640]{2,1,0:T(8,128)S(1)}, f32[10,80,640]{2,1,0:T(8,128)}, u32[]{:S(2)}) copy-start(f32[10,80,640]{2,1,0:T(8,128)} %legendre_ref.1) | copy-start | bytes 6144004
  1.7 0.7 copy-start.5
  5.3 43.7 %collective-permute-start.1 = (f32[1256,128]{1,0:T(8,128)}, f32[1256,128]{1,0:T(8,128)S(1)}, u32[]{:S(2)}, u32[]{:S(2)}) collective-permute-start(f32[1256,128]{1,0:T(8,128)} %get-tuple-element.15), channel_id=1, source_target_pairs={{0,6},{1,7},{2,0},{3,1},{4,2},{5,3},{6,4},{7,5},{8,14},{9,15},{10,... | collective-permute-start | bytes 1929224 | tf_op jit(solution)/shard_map/ppermute | solution.py:327
  12.0 41.9 %collective-permute-start = (f32[1264,128]{1,0:T(8,128)S(1)}, f32[1264,128]{1,0:T(8,128)S(1)}, u32[]{:S(2)}, u32[]{:S(2)}) collective-permute-start(f32[1264,128]{1,0:T(8,128)S(1)} %get-tuple-element.14), channel_id=1, source_target_pairs={{0,2},{1,3},{2,4},{3,5},{4,6},{5,7},{6,0},{7,1},{8,10},{9,11},{10,... | collective-permute-start | bytes 1941512 | tf_op jit(solution)/shard_map/ppermute | solution.py:327
  26.7 43.3 %all-to-all-start = ((f32[512,1,256]{2,1,0:T(1,128)}), f32[512,1,256]{2,1,0:T(1,128)}, u32[]{:S(2)}, u32[]{:S(2)}) async-start(f32[512,1,256]{2,1,0:T(1,128)} %copy.13), calls=%async_computation | async-start | bytes 1048576 | tf_op jit(solution)/shard_map/all_to_all | solution.py:531
  49.0 16.4 %copy-start.7 = (f32[32]{0:T(128)S(1)}, f32[32]{0:T(128)}, u32[]{:S(2)}) copy-start(f32[32]{0:T(128)} %param.15) | copy-start | bytes 388
  49.1 25.8 %collective-permute-start.3 = (f32[1008,128]{1,0:T(8,128)S(1)}, f32[1008,128]{1,0:T(8,128)S(1)}, u32[]{:S(2)}, u32[]{:S(2)}) collective-permute-start(f32[1008,128]{1,0:T(8,128)S(1)} %pad_maximum_fusion.1), channel_id=1, source_target_pairs={{0,7},{1,0},{2,1},{3,2},{4,3},{5,4},{6,5},{7,6},{8,15},{9,8},{10,9... | collective-permute-start | bytes 1548296 | tf_op jit(solution)/shard_map/ppermute | solution.py:327
  54.8 20.1 %collective-permute-start.2 = (f32[1008,128]{1,0:T(8,128)}, f32[1008,128]{1,0:T(8,128)S(1)}, u32[]{:S(2)}, u32[]{:S(2)}) collective-permute-start(f32[1008,128]{1,0:T(8,128)} %pad_maximum_fusion), channel_id=1, source_target_pairs={{0,1},{1,2},{2,3},{3,4},{4,5},{5,6},{6,7},{7,0},{8,9},{9,10},{10,1... | collective-permute-start | bytes 1548296 | tf_op jit(solution)/shard_map/ppermute | solution.py:327
  57.4 17.5 %collective-permute-start.4 = (f32[256,128]{1,0:T(8,128)}, f32[256,128]{1,0:T(8,128)S(1)}, u32[]{:S(2)}, u32[]{:S(2)}) collective-permute-start(f32[256,128]{1,0:T(8,128)} %slice.18), channel_id=1, source_target_pairs={{0,2},{1,3},{2,4},{3,5},{4,6},{5,7},{6,0},{7,1},{8,10},{9,11},{10,... | collective-permute-start | bytes 393224 | tf_op jit(solution)/shard_map/ppermute | solution.py:327
  60.8 13.8 %collective-permute-start.5 = (f32[248,128]{1,0:T(8,128)}, f32[248,128]{1,0:T(8,128)S(1)}, u32[]{:S(2)}, u32[]{:S(2)}) collective-permute-start(f32[248,128]{1,0:T(8,128)} %slice.19), channel_id=1, source_target_pairs={{0,6},{1,7},{2,0},{3,1},{4,2},{5,3},{6,4},{7,5},{8,14},{9,15},{10,... | collective-permute-start | bytes 380936 | tf_op jit(solution)/shard_map/ppermute | solution.py:327
  71.0 3.9 %copy-start.1 = (f32[32,32]{1,0:T(8,128)S(1)}, f32[32,32]{1,0:T(8,128)}, u32[]{:S(2)}) copy-start(f32[32,32]{1,0:T(8,128)} %to_ref.1) | copy-start | bytes 12292
  71.0 3.9 %copy-start.2 = (f32[32,32]{1,0:T(8,128)S(1)}, f32[32,32]{1,0:T(8,128)}, u32[]{:S(2)}) copy-start(f32[32,32]{1,0:T(8,128)} %from_ref.1) | copy-start | bytes 12292
  78.9 42.1 %copy-start.4 = (f32[1,640]{1,0:T(1,128)S(1)}, f32[1,640]{1,0:T(1,128)}, u32[]{:S(2)}) copy-start(f32[1,640]{1,0:T(1,128)} %convert_element_type.23.waves_ref) | copy-start | bytes 7684
  78.9 42.1 %copy-start.6 = (s32[10]{0:T(128)S(1)}, s32[10]{0:T(128)}, u32[]{:S(2)}) copy-start(s32[10]{0:T(128)} %points_ref.3) | copy-start | bytes 124
